TPU v7x, 256 devices: a whole 4x4x8 slice. The times are simulated.
256 devices in a mesh: row: 32 (over y, x, core), col: 8 (over z).
Axes of the slice: x: 4, y: 4, z: 8, core: 2. Of those that a mesh axis runs over, the one named last changes fastest.
Arguments:
- tokens: bfloat16 [8192, 4096], P('row', 'col'), may hold values from -6 to 6
- contig_lengths: int32 [64], replicated, may hold values from 1 to 768, 8192 in all
- w_in: bfloat16 [4096, 4096], P('row', 'col'), may hold values from -0.09375 to 0.09375
- conv_filter: float32 [128, 4096], P(None, 'col'), may hold values from -0.5 to 0.5
- d_gated: bfloat16 [8192, 4096], P('row', 'col'), may hold values from -6 to 6
Outputs:
- gated: bfloat16 [8192, 4096], P('row', 'col')
- d_tokens: bfloat16 [8192, 4096], P('row', 'col')
- grad_in: float32 [4096, 4096], P('row', 'col')
Inputs may be any that keep to these rules, and one draw needn't show every extreme that they name: `contig_lengths`: the 64 lengths sum to 8192; the longest is exactly 768.
All inputs are finite; a program needn't handle non-finite values.
Results may differ from a plain program's by a relative error of at most 0.022.
Values may be sent and summed in bfloat16 or wider, within the bound.
No kernel may reach another device: no remote copies, remote signals or barrier semaphores. Data moves between devices by JAX's collectives and lax.ppermute only.
A program may use at most 64 MiB of HBM per device.

v0:
```python
import math

import jax
import jax.numpy as jnp
from jax import lax
from jax.sharding import PartitionSpec as P


def shifted_2(value, axis, steps):
    count = lax.axis_size(axis)
    first, last = (max(0, -steps), min(count, count - steps))
    return lax.ppermute(value, axis, [(source, source + steps) for source in range(first, last)])


def contig_offsets(contig_lengths, positions):
    ends = jnp.cumsum(contig_lengths)
    starts = ends - contig_lengths
    before = jnp.where(starts[None, :] <= positions[:, None], starts[None, :], 0)
    return positions - jnp.max(before, axis=1)


def causal_mix(extended, offsets, taps_filter, count):
    tap_count = taps_filter.shape[0]
    group_size = math.gcd(32, tap_count)

    def causal_one_group(group_index, running):
        for inner in range(group_size):
            tap = group_index * group_size + inner
            shifted = lax.dynamic_slice_in_dim(extended, tap_count - 1 - tap, count, 0)
            weight = lax.dynamic_slice_in_dim(taps_filter, tap, 1, 0)
            running = running + jnp.where((tap <= offsets)[:, None], shifted * weight, 0.0)
        return running

    initial = jnp.zeros((count, extended.shape[1]), jnp.float32)
    return lax.fori_loop(
        jnp.int32(0), jnp.int32(tap_count // group_size), causal_one_group, initial
    )


def reverse_mix(extended, ext_offsets, taps_filter, count):
    tap_count = taps_filter.shape[0]
    group_size = math.gcd(32, tap_count)

    def reverse_one_group(group_index, running):
        for inner in range(group_size):
            tap = group_index * group_size + inner
            shifted = lax.dynamic_slice_in_dim(extended, tap, count, 0)
            live = lax.dynamic_slice_in_dim(ext_offsets, tap, count, 0) >= tap
            weight = lax.dynamic_slice_in_dim(taps_filter, tap, 1, 0)
            running = running + jnp.where(live[:, None], shifted * weight, 0.0)
        return running

    initial = jnp.zeros((count, extended.shape[1]), jnp.float32)
    return lax.fori_loop(
        jnp.int32(0), jnp.int32(tap_count // group_size), reverse_one_group, initial
    )


def fold_with(left, piece):
    return jnp.dot(left, piece, preferred_element_type=jnp.float32)


def back_with(right, piece):
    return lax.dot_general(
        right, piece, (((1,), (1,)), ((), ())), preferred_element_type=jnp.float32
    )


def weight_term(left, right):
    return lax.dot_general(
        left, right, (((0,), (0,)), ((), ())), preferred_element_type=jnp.float32
    )


def body(tokens, contig_lengths, w_in, conv_filter, d_gated):
    tok_rows = tokens.shape[0]
    tap_count = conv_filter.shape[0]
    seq_total = tok_rows * lax.axis_size("row")
    full_tokens = lax.all_gather(tokens, "col", axis=1, tiled=True)
    projected = fold_with(full_tokens, lax.all_gather(w_in, "row", axis=0, tiled=True))
    projected = projected.astype(jnp.bfloat16)
    proj_f = projected.astype(jnp.float32)
    prior_tail = shifted_2(projected[tok_rows - tap_count + 1 :], "row", 1)
    first_row = lax.axis_index("row") * tok_rows
    positions = first_row + jnp.arange(tok_rows, dtype=jnp.int32)
    offsets = contig_offsets(contig_lengths, positions)
    extended = jnp.concatenate([prior_tail, projected], 0).astype(jnp.float32)
    conv_out = causal_mix(extended, offsets, conv_filter, tok_rows)
    sigma = jax.nn.sigmoid(proj_f)
    gate_val = proj_f * sigma
    gated = (conv_out * gate_val).astype(jnp.bfloat16)
    upstream = d_gated.astype(jnp.float32)
    d_conv = upstream * gate_val
    d_gate = upstream * conv_out * (sigma * (1.0 + proj_f * (1.0 - sigma)))
    next_head = shifted_2(d_conv[: tap_count - 1].astype(jnp.bfloat16), "row", -1).astype(
        jnp.float32
    )
    ext_grad = jnp.concatenate([d_conv, next_head], 0)
    ext_positions = first_row + jnp.arange(tok_rows + tap_count - 1, dtype=jnp.int32)
    ext_offsets = contig_offsets(contig_lengths, ext_positions)
    d_proj = (reverse_mix(ext_grad, ext_offsets, conv_filter, tok_rows) + d_gate).astype(
        jnp.bfloat16
    )
    grad_in = lax.psum_scatter(
        weight_term(full_tokens, d_proj).astype(jnp.bfloat16),
        "row",
        scatter_dimension=0,
        tiled=True,
    ).astype(jnp.float32) / math.sqrt(seq_total)
    token_terms = back_with(d_proj, lax.all_gather(w_in, "row", axis=0, tiled=True))
    d_tokens = lax.psum_scatter(
        token_terms.astype(jnp.bfloat16), "col", scatter_dimension=1, tiled=True
    )
    return (gated, d_tokens, grad_in)


def solution(mesh):
    placed = (P("row", "col"), P(), P("row", "col"), P(None, "col"), P("row", "col"))
    return jax.shard_map(
        body,
        mesh=mesh,
        in_specs=placed,
        out_specs=(P("row", "col"), P("row", "col"), P("row", "col")),
        check_vma=False,
    )
```

profile of v0, /device:TPU:96, one launch (start us, length us, event | category | flops | bytes accessed | tf_op | source)
XLA Modules:
  0.0 317.6 jit_solution(2429166563605330082)
XLA Ops:
  7.2 0.7 all-gather.3.cloned.1.call-update
  7.9 0.7 all-gather.5.cloned.1.call-update
  8.7 0.7 copy.14
  9.6 0.1 reduce
  9.7 0.7 sub.237
  10.6 41.5 %all-gather.3.cloned.1.call-done = bf16[256,4096]{1,0:T(8,128)(2,1)} async-done(((bf16[256,512]{1,0:T(8,128)(2,1)}), bf16[256,4096]{1,0:T(8,128)(2,1)}) %all-gather.3.cloned.1.call-update) | async-done | bytes 2097168 | tf_op jit(solution)/shard_map/all_gather | solution.py:79
  52.0 53.0 %all-gather.5.cloned.1.call-done = bf16[4096,512]{1,0:T(8,128)(2,1)} async-done(((bf16[128,512]{1,0:T(8,128)(2,1)}), bf16[4096,512]{1,0:T(8,128)(2,1)}) %all-gather.5.cloned.1.call-update) | async-done | bytes 4194320 | tf_op jit(solution)/shard_map/all_gather | solution.py:80
  105.1 4.2 %convert_multiply_fusion.3 = (f32[256,512]{1,0:T(8,128)S(1)}, bf16[256,512]{1,0:T(8,128)(2,1)S(1)}) fusion(bf16[256,512]{1,0:T(8,128)(2,1)} %param.13, bf16[256,4096]{1,0:T(8,128)(2,1)} %all-gather.3.cloned.1.call-done, bf16[4096,512]{1,0:T(8,128)(2,1)} %all-gather.5.cloned.1.call-done), kind=kOutput, calls=%fused_computation.189 | convolution fusion | flops 1074790400 | bytes 7340032 | tf_op jit(solution)/shard_map/dot_general | solution.py:60
  109.3 1.3 collective-permute-start.1
  110.6 3.0 collective-permute-start
  113.8 24.4 %while.28 = (s32[]{:T(128)}, f32[256,512]{1,0:T(8,128)S(1)}, s32[383]{0:T(512)S(1)}, f32[383,512]{1,0:T(8,128)S(1)}, f32[128,512]{1,0:T(8,128)S(1)}, /*index=5*/...) while((s32[]{:T(128)}, f32[256,512]{1,0:T(8,128)S(1)}, ...), condition=%wide.region_6.7_spmd.clone, body=%wide.region_5.6_spmd.clone.sunk | while | flops 12722371 | bytes 18075188 | solution.py:54
  114.1 0.1 constant_dynamic-slice_fusion.70
  114.8 5.1 %select_add_fusion.7 = f32[256,512]{1,0:T(8,128)S(1)} fusion(f32[383,512]{1,0:T(8,128)S(1)} %get-tuple-element.1060, s32[]{:T(128)S(6)} %select_n.1873, s32[]{:T(128)S(6)} %select_n.1874, s32[]{:T(128)S(6)} %select_n.1875, s32[]{:T(128)S(6)} %select_n.1876, s32[]{:T(128)S(6)} %select_n.1877, s32[]{:T(128)S(6)} %select_n.1878, s32[]{:T(128)S(6)} %select_n.1879, ...), kind=kLoop, calls=%fused_computation.115.clone.1 | loop fusion | flops 12713984 | bytes 17899648 | tf_op jit(solution)/shard_map/while/body/add | solution.py:50
  120.2 0.1 constant_dynamic-slice_fusion.70
  120.9 5.1 %select_add_fusion.7 = f32[256,512]{1,0:T(8,128)S(1)} fusion(f32[383,512]{1,0:T(8,128)S(1)} %get-tuple-element.1060, s32[]{:T(128)S(6)} %select_n.1873, s32[]{:T(128)S(6)} %select_n.1874, s32[]{:T(128)S(6)} %select_n.1875, s32[]{:T(128)S(6)} %select_n.1876, s32[]{:T(128)S(6)} %select_n.1877, s32[]{:T(128)S(6)} %select_n.1878, s32[]{:T(128)S(6)} %select_n.1879, ...), kind=kLoop, calls=%fused_computation.115.clone.1 | loop fusion | flops 12713984 | bytes 17899648 | tf_op jit(solution)/shard_map/while/body/add | solution.py:50
  126.3 0.1 constant_dynamic-slice_fusion.70
  127.0 5.1 %select_add_fusion.7 = f32[256,512]{1,0:T(8,128)S(1)} fusion(f32[383,512]{1,0:T(8,128)S(1)} %get-tuple-element.1060, s32[]{:T(128)S(6)} %select_n.1873, s32[]{:T(128)S(6)} %select_n.1874, s32[]{:T(128)S(6)} %select_n.1875, s32[]{:T(128)S(6)} %select_n.1876, s32[]{:T(128)S(6)} %select_n.1877, s32[]{:T(128)S(6)} %select_n.1878, s32[]{:T(128)S(6)} %select_n.1879, ...), kind=kLoop, calls=%fused_computation.115.clone.1 | loop fusion | flops 12713984 | bytes 17899648 | tf_op jit(solution)/shard_map/while/body/add | solution.py:50
  132.4 0.1 constant_dynamic-slice_fusion.70
  133.1 5.1 %select_add_fusion.7 = f32[256,512]{1,0:T(8,128)S(1)} fusion(f32[383,512]{1,0:T(8,128)S(1)} %get-tuple-element.1060, s32[]{:T(128)S(6)} %select_n.1873, s32[]{:T(128)S(6)} %select_n.1874, s32[]{:T(128)S(6)} %select_n.1875, s32[]{:T(128)S(6)} %select_n.1876, s32[]{:T(128)S(6)} %select_n.1877, s32[]{:T(128)S(6)} %select_n.1878, s32[]{:T(128)S(6)} %select_n.1879, ...), kind=kLoop, calls=%fused_computation.115.clone.1 | loop fusion | flops 12713984 | bytes 17899648 | tf_op jit(solution)/shard_map/while/body/add | solution.py:50
  138.3 23.2 %while.27 = (s32[]{:T(128)}, f32[256,512]{1,0:T(8,128)S(1)}, s32[256]{0:T(256)S(1)}, f32[383,512]{1,0:T(8,128)S(1)}, f32[128,512]{1,0:T(8,128)S(1)}, /*index=5*/...) while((s32[]{:T(128)}, f32[256,512]{1,0:T(8,128)S(1)}, ...), condition=%wide.region_3.4_spmd.clone, body=%wide.region_2.3_spmd.clone.sunk | while | flops 12722435 | bytes 18044772 | solution.py:35
  139.1 5.0 %select_add_fusion.6 = f32[256,512]{1,0:T(8,128)S(1)} fusion(f32[383,512]{1,0:T(8,128)S(1)} %get-tuple-element.1306, s32[]{:T(128)S(6)} %select_n.1777, s32[]{:T(128)S(6)} %select_n.1778, s32[]{:T(128)S(6)} %select_n.1779, s32[]{:T(128)S(6)} %select_n.1780, s32[]{:T(128)S(6)} %select_n.1781, s32[]{:T(128)S(6)} %select_n.1782, s32[]{:T(128)S(6)} %select_n.1783, ...), kind=kLoop, calls=%fused_computation.25.clone.1 | loop fusion | flops 12713984 | bytes 17899648 | tf_op jit(solution)/shard_map/while/body/add | solution.py:31
  144.9 5.0 %select_add_fusion.6 = f32[256,512]{1,0:T(8,128)S(1)} fusion(f32[383,512]{1,0:T(8,128)S(1)} %get-tuple-element.1306, s32[]{:T(128)S(6)} %select_n.1777, s32[]{:T(128)S(6)} %select_n.1778, s32[]{:T(128)S(6)} %select_n.1779, s32[]{:T(128)S(6)} %select_n.1780, s32[]{:T(128)S(6)} %select_n.1781, s32[]{:T(128)S(6)} %select_n.1782, s32[]{:T(128)S(6)} %select_n.1783, ...), kind=kLoop, calls=%fused_computation.25.clone.1 | loop fusion | flops 12713984 | bytes 17899648 | tf_op jit(solution)/shard_map/while/body/add | solution.py:31
  150.7 5.0 %select_add_fusion.6 = f32[256,512]{1,0:T(8,128)S(1)} fusion(f32[383,512]{1,0:T(8,128)S(1)} %get-tuple-element.1306, s32[]{:T(128)S(6)} %select_n.1777, s32[]{:T(128)S(6)} %select_n.1778, s32[]{:T(128)S(6)} %select_n.1779, s32[]{:T(128)S(6)} %select_n.1780, s32[]{:T(128)S(6)} %select_n.1781, s32[]{:T(128)S(6)} %select_n.1782, s32[]{:T(128)S(6)} %select_n.1783, ...), kind=kLoop, calls=%fused_computation.25.clone.1 | loop fusion | flops 12713984 | bytes 17899648 | tf_op jit(solution)/shard_map/while/body/add | solution.py:31
  156.5 5.0 %select_add_fusion.6 = f32[256,512]{1,0:T(8,128)S(1)} fusion(f32[383,512]{1,0:T(8,128)S(1)} %get-tuple-element.1306, s32[]{:T(128)S(6)} %select_n.1777, s32[]{:T(128)S(6)} %select_n.1778, s32[]{:T(128)S(6)} %select_n.1779, s32[]{:T(128)S(6)} %select_n.1780, s32[]{:T(128)S(6)} %select_n.1781, s32[]{:T(128)S(6)} %select_n.1782, s32[]{:T(128)S(6)} %select_n.1783, ...), kind=kLoop, calls=%fused_computation.25.clone.1 | loop fusion | flops 12713984 | bytes 17899648 | tf_op jit(solution)/shard_map/while/body/add | solution.py:31
  161.5 1.0 fusion.51
  162.5 4.8 %fusion.48 = bf16[4096,512]{0,1:T(8,128)(2,1)} fusion(bf16[256,512]{1,0:T(8,128)(2,1)S(1)} %get-tuple-element.531, bf16[256,4096]{1,0:T(8,128)(2,1)} %all-gather.3.cloned.1.call-done), kind=kOutput, calls=%fused_computation.181 | convolution fusion | flops 1075838976 | bytes 6553600 | tf_op jit(solution)/shard_map/dot_general | solution.py:70
  167.3 6.5 %copy.16 = bf16[4096,512]{1,0:T(8,128)(2,1)} copy(bf16[4096,512]{0,1:T(8,128)(2,1)} %fusion.48) | data formatting | bytes 8388608
  173.9 4.8 %convolution_convert_fusion.1 = bf16[256,4096]{1,0:T(8,128)(2,1)} fusion(bf16[256,512]{1,0:T(8,128)(2,1)S(1)} %get-tuple-element.531, bf16[4096,512]{1,0:T(8,128)(2,1)} %all-gather.5.cloned.1.call-done), kind=kOutput, calls=%fused_computation.182 | convolution fusion | flops 1074790400 | bytes 6553600 | tf_op jit(solution)/shard_map/dot_general | solution.py:64
  178.8 87.8 %reduce-scatter.7.cloned.1.call-done = bf16[128,512]{1,0:T(8,128)(2,1)} async-done(((bf16[4096,512]{1,0:T(8,128)(2,1)}), bf16[128,512]{1,0:T(8,128)(2,1)}) %reduce-scatter.7.cloned.1.call-update) | async-done | bytes 131088
  266.6 1.0 copy.17
  267.7 0.8 copy.15
  268.5 42.6 %reduce-scatter.5.cloned.1.call-done = bf16[256,512]{1,0:T(8,128)(2,1)} async-done(((bf16[256,4096]{1,0:T(8,128)(2,1)}), bf16[256,512]{1,0:T(8,128)(2,1)}) %reduce-scatter.5.cloned.1.call-update) | async-done | bytes 262160 | tf_op jit(solution)/shard_map/reduce_scatter | solution.py:111
  (63 shorter events, 3.6 us)
Async XLA Ops:
  7.2 44.9 %all-gather.3.cloned.1.call-start = ((), (), s32[]{:S(2)}) async-start(), calls=%async_computation.2 | async-start | bytes 2359296 | tf_op jit(solution)/shard_map/all_gather | solution.py:79
  7.9 97.2 %all-gather.5.cloned.1.call-start = ((), (), s32[]{:S(2)}) async-start(), calls=%async_computation.3 | async-start | bytes 4325376 | tf_op jit(solution)/shard_map/all_gather | solution.py:80
  8.6 258.0 %reduce-scatter.7.cloned.1.call-start = ((), (), s32[]{:S(2)}) async-start(), calls=%async_computation.5 | async-start | bytes 4325376
  10.6 103.2 %copy-start = (f32[128,512]{1,0:T(8,128)S(1)}, f32[128,512]{1,0:T(8,128)}, u32[]{:S(2)}) copy-start(f32[128,512]{1,0:T(8,128)} %param.12) | copy-start | bytes 786436
  109.3 4.4 %collective-permute-start.1 = (bf16[127,512]{1,0:T(8,128)(2,1)S(1)}, bf16[127,512]{1,0:T(8,128)(2,1)S(1)}, u32[]{:S(2)}, u32[]{:S(2)}) collective-permute-start(bf16[127,512]{1,0:T(8,128)(2,1)S(1)} %slice.12), channel_id=1, source_target_pairs={{8,0},{16,8},{24,16},{32,24},{40,32},{48,40},{56,48},{64,56},{72,6... | collective-permute-start | bytes 390152 | tf_op jit(solution)/shard_map/ppermute | solution.py:12
  110.6 27.6 %collective-permute-start = (bf16[127,512]{1,0:T(8,128)(2,1)S(1)}, bf16[127,512]{1,0:T(8,128)(2,1)S(1)}, u32[]{:S(2)}, u32[]{:S(2)}) collective-permute-start(bf16[127,512]{1,0:T(8,128)(2,1)S(1)} %slice.9), channel_id=1, source_target_pairs={{0,8},{8,16},{16,24},{24,32},{32,40},{40,48},{48,56},{56,64},{64,7... | collective-permute-start | bytes 390152 | tf_op jit(solution)/shard_map/ppermute | solution.py:12
  138.3 23.2 %copy-start.1 = (bf16[256,512]{1,0:T(8,128)(2,1)S(1)}, bf16[256,512]{1,0:T(8,128)(2,1)}, u32[]{:S(2)}) copy-start(bf16[256,512]{1,0:T(8,128)(2,1)} %param.13) | copy-start | bytes 786436
  173.9 137.2 %reduce-scatter.5.cloned.1.call-start = ((), (), s32[]{:S(2)}) async-start(), calls=%async_computation.4 | async-start | bytes 2359296 | tf_op jit(solution)/shard_map/reduce_scatter | solution.py:111
Sparse Core Ops, SparseCore 0:
  9.8 42.1 all-gather.2
  54.6 50.4 all-gather.4
  174.0 92.5 reduce-scatter.6
  269.7 41.2 reduce-scatter.4
where the time goes:
time: 319 us; the launch traced here: 318 us
  waiting for transfers between devices  226 us (71%)
  other arithmetic  44.5 us (14%)
  matrix products  13.9 us (4%)
  between operations  13.9 us (4%)
  local copies, waits for them, and re-layouts  10.5 us (3%)
  starting transfers between devices  4.49 us (1%)
  loops' own time  4.01 us (1%)
    unnamed x5, waiting for transfers between devices  89.2 us
    all_gather x1, waiting for transfers between devices, body(): lax.all_gather(w_in, 'row', axis=0, tiled=True)  53 us
    reduce_scatter x1, waiting for transfers between devices, body(): lax.psum_scatter(token_terms.astype(jnp.bfloat16), 'col', scatter_dimensi...  42.6 us
    all_gather x1, waiting for transfers between devices, body(): full_tokens = lax.all_gather(tokens, 'col', axis=1, tiled=True)  41.5 us
    add x4, other arithmetic, reverse_one_group(): running = running + jnp.where(live[:, None], shifted * weight, 0.0)  20.3 us
    add x4, other arithmetic, causal_one_group(): running + jnp.where((tap <= offsets)[:, None], shifted * weight, 0.0)  20.1 us
    unnamed x7, local copies, waits for them, and re-layouts  8.36 us
  transfers between devices with their start and end apart: 6, of which 4 were waited for; matrix products, arithmetic and copies ran while one was open for 10% of the time, Pallas kernels for 0%

commit v1 on v0

v1 whole, which is shorter than its diff:
```python
import functools
import math

import jax
import jax.numpy as jnp
from jax import lax
from jax.experimental import pallas as pl
from jax.experimental.pallas import tpu as pltpu
from jax.sharding import PartitionSpec as P

BF = jnp.bfloat16
F32 = jnp.float32
NY, NX, NC, NZ = 4, 4, 2, 8
TILE = 16
LANES = 128


def row_of(y, x, c):
    return ((y % NY) * NX + x % NX) * NC + c % NC


CHIPS = [(y, x) for y in range(NY) for x in range(NX)]
def around_z(value, steps):
    pairs = []
    for y, x in CHIPS:
        for c in range(NC):
            for z in range(NZ):
                to = (z + steps * (1 - 2 * c)) % NZ
                pairs.append((row_of(y, x, c) * NZ + z, row_of(y, x, c) * NZ + to))
    return lax.ppermute(value, ("row", "col"), pairs)


def narrow(value, steps):
    pairs = []
    for y, x in CHIPS:
        pairs.append((row_of(y, x, 0), row_of(y, x + steps, 0)))
        pairs.append((row_of(y, x, 1), row_of(y + steps, x, 1)))
    return lax.ppermute(value, "row", pairs)


def wide(value, steps):
    pairs = []
    for y, x in CHIPS:
        pairs.append((row_of(y, x, 0), row_of(y + steps, x, 0)))
        pairs.append((row_of(y, x, 1), row_of(y, x + steps, 1)))
    return lax.ppermute(value, "row", pairs)


def to_other_core(value):
    return lax.ppermute(value, "row", [(row_of(y, x, c), row_of(y, x, c + 1)) for y, x in CHIPS for c in range(NC)])


def next_row(value, steps):
    count = NY * NX * NC
    return lax.ppermute(value, "row", [(r, (r + steps) % count) for r in range(count)])


def live_taps(contig_lengths, first_row, rows):
    ends = jnp.cumsum(contig_lengths)
    starts = ends - contig_lengths
    at = first_row + jnp.arange(rows, dtype=jnp.int32)
    start = jnp.max(jnp.where(starts[None, :] <= at[:, None], starts[None, :], 0), axis=1)
    end = jnp.min(jnp.where(ends[None, :] > at[:, None], ends[None, :], 1 << 30), axis=1)
    back = jnp.minimum(at - start, 127)
    ahead = jnp.minimum(end - 1 - at, 127)
    wide = lambda v: jnp.broadcast_to(v.astype(BF)[:, None], (rows, LANES))
    return wide(back), wide(ahead)


def after(value, *others):
    return lax.optimization_barrier((value, others))[0]


VMEM = pl.BlockSpec(memory_space=pltpu.VMEM)
SMEM = pl.BlockSpec(memory_space=pltpu.SMEM)
HBM = pl.BlockSpec(memory_space=pltpu.HBM)


def loop(count, step):
    def run(i, carry):
        step(i)
        return carry

    lax.fori_loop(jnp.int32(0), jnp.int32(count), run, jnp.int32(0))


def add_kernel(a, b, out):
    out[...] = (a[...].astype(F32) + b[...].astype(F32)).astype(BF)


def add(a, b):
    return pl.pallas_call(
        add_kernel,
        in_specs=[VMEM] * 2,
        out_specs=VMEM,
        out_shape=jax.ShapeDtypeStruct(a.shape, BF),
        compiler_params=pltpu.CompilerParams(vmem_limit_bytes=2 << 20),
        cost_estimate=pl.CostEstimate(flops=1 << 20, bytes_accessed=1 << 20, transcendentals=0),
        name="add",
    )(a, b)


def stack_kernel(first, *refs):
    for k in range(4):
        refs[4][lax.rem(first[0] + k, 4)] = refs[k][...]


def stack(first, pieces):
    return pl.pallas_call(
        stack_kernel,
        in_specs=[SMEM] + [VMEM] * 4,
        out_specs=VMEM,
        out_shape=jax.ShapeDtypeStruct((4, 128, 512), BF),
        compiler_params=pltpu.CompilerParams(vmem_limit_bytes=2 << 20),
        cost_estimate=pl.CostEstimate(flops=1 << 20, bytes_accessed=1 << 20, transcendentals=0),
        name="stack",
    )(first, *pieces)


def sum_kernel(*refs):
    for j in range(4):
        total = refs[0][j].astype(F32)
        for k in range(1, 4):
            total += refs[k][j].astype(F32)
        refs[4 + j][...] = total.astype(BF)


def sum_four(blocks):
    return pl.pallas_call(
        sum_kernel,
        in_specs=[VMEM] * 4,
        out_specs=[VMEM] * 4,
        out_shape=[jax.ShapeDtypeStruct((128, 512), BF)] * 4,
        compiler_params=pltpu.CompilerParams(vmem_limit_bytes=4 << 20),
        cost_estimate=pl.CostEstimate(flops=1 << 20, bytes_accessed=1 << 20, transcendentals=0),
        name="sum_four",
    )(*blocks)


def place_of(ids, steps):
    return lax.rem(ids[3] + jnp.where(ids[2] == 0, steps, NZ - steps), NZ)


def load_weight(ids, own, other, w, sems, act):
    def one_core(core, blocks, base):
        for i, block in enumerate(blocks):
            if core == 0:
                y = lax.rem(ids[0] + i, 4)
                for half in range(2):
                    at = w.at[2 * y + half, :, 0]
                    act(pltpu.make_async_copy(block.at[2 * half : 2 * half + 2], at, sems.at[base + 2 * i + half]))
            else:
                x = lax.rem(ids[1] + i, 4)
                for y in range(4):
                    at = w.at[2 * y + x // 2, lax.rem(x, 2), 1]
                    act(pltpu.make_async_copy(block.at[y], at, sems.at[base + 4 * i + y]))

    @pl.when(ids[2] == 0)
    def _():
        one_core(0, own, 0)
        one_core(1, other, 8)

    @pl.when(ids[2] == 1)
    def _():
        one_core(0, other, 0)
        one_core(1, own, 8)


def start(copy):
    copy.start()


def wait(copy):
    copy.wait()


def start(copy):
    copy.start()


def wait(copy):
    copy.wait()


def project_piece(ids, k, piece, w, mine_ref, cross_ref):
    for core, out in ((ids[2], mine_ref), (1 - ids[2], cross_ref)):
        for xp in range(2):
            lanes = pl.ds(pl.multiple_of(xp * 256 + core * 128, 128), 128)
            out[k, :, xp * 128 : xp * 128 + 128] = piece[:, lanes]
    return jnp.dot(piece[...], w[place_of(ids, k)].reshape(512, 512), preferred_element_type=F32)


EARLY, LATE = (0, 1, 7, 2, 6), (3, 5, 4)


def early_kernel(ids, *refs):
    pieces, own, other, (acc, w, mine_ref, cross_ref, tok, sems, tok_sems) = refs[0:5], refs[5:9], refs[9:13], refs[13:]
    load_weight(ids, own, other, w, sems, start)
    arrive = [pltpu.make_async_copy(piece, tok.at[n], tok_sems.at[n]) for n, piece in enumerate(pieces)]
    for copy in arrive:
        copy.start()
    load_weight(ids, own, other, w, sems, wait)
    total = None
    for n, k in enumerate(EARLY):
        arrive[n].wait()
        term = project_piece(ids, k, tok.at[n], w, mine_ref, cross_ref)
        total = term if total is None else total + term
    acc[...] = total


def late_kernel(ids, *refs):
    pieces, (acc, w, _, _, dg_ref, p_ref, tail_ref, head_ref, mine_ref, cross_ref) = refs[0:3], refs[3:]
    total = acc[...]
    for k, piece in zip(LATE, pieces):
        total += project_piece(ids, k, piece, w, mine_ref, cross_ref)
    p = total.astype(BF)
    p_ref[...] = p
    tail_ref[...] = p[128:256]
    top = p[0:128].astype(F32)
    head_ref[...] = (dg_ref[0:128].astype(F32) * (top * jax.nn.sigmoid(top))).astype(BF)


def project_early(ids, pieces, blocks):
    part_of = jax.ShapeDtypeStruct((NZ, 256, 256), BF)
    return pl.pallas_call(
        early_kernel,
        in_specs=[SMEM] + [HBM] * 13,
        out_specs=[VMEM] * 4,
        out_shape=[
            jax.ShapeDtypeStruct((256, 512), F32), jax.ShapeDtypeStruct((NZ, 2, 2, 128, 512), BF), part_of, part_of,
        ],
        scratch_shapes=[
            pltpu.VMEM((5, 256, 512), BF),
            pltpu.SemaphoreType.DMA((24,)),
            pltpu.SemaphoreType.DMA((5,)),
        ],
        compiler_params=pltpu.CompilerParams(vmem_limit_bytes=8 << 20),
        cost_estimate=pl.CostEstimate(flops=1 << 32, bytes_accessed=8 << 20, transcendentals=0),
        name="project_early",
    )(ids, *pieces, *blocks)


def project_late(ids, pieces, early, d_gated):
    half, part_of = jax.ShapeDtypeStruct((128, 512), BF), jax.ShapeDtypeStruct((NZ, 256, 256), BF)
    return pl.pallas_call(
        late_kernel,
        in_specs=[SMEM] + [VMEM] * 8,
        out_specs=[VMEM] * 5,
        out_shape=[jax.ShapeDtypeStruct((256, 512), BF), half, half, part_of, part_of],
        input_output_aliases={6: 3, 7: 4},
        compiler_params=pltpu.CompilerParams(vmem_limit_bytes=6 << 20),
        cost_estimate=pl.CostEstimate(flops=2 * 256 * 1536 * 512, bytes_accessed=4 << 20, transcendentals=0),
        name="project_late",
    )(ids, *pieces, *early, d_gated)


def mix(ext, live_ref, taps_ref, even, odd, mask, acc, reverse):
    acc[...] = jnp.zeros_like(acc)
    rows = ext.shape[0]

    def shift(b):
        for k in range(16):
            limit = (b + (8 * k - 1)).astype(F32).astype(BF)
            for u in range(8):
                at = slice(TILE * u, TILE * u + TILE)
                mask[k, at] = jnp.clip(live_ref[at] - limit, jnp.zeros((), BF), jnp.ones((), BF))

        def strip(s):
            lanes = pl.ds(pl.multiple_of(s * 256, 256), 256)
            if reverse:
                r = pltpu.roll(ext[:, lanes], lax.rem(rows - b, rows), 0)
                even[...] = r.astype(BF)
                odd[...] = jnp.concatenate([r[8:], r[:8]], 0).astype(BF)
            else:
                r = pltpu.roll(ext[:, lanes], b, 0)
                even[...] = r.astype(BF)
                odd[...] = jnp.concatenate([r[-8:], r[:-8]], 0).astype(BF)
            for h, moved in ((0, even), (1, odd)):
                weights = [taps_ref[b, 2 * a + h, :, lanes] for a in range(8)]
                sums = [None] * 8
                count = [0] * 8
                for v in range(16):
                    source = moved[TILE * v : TILE * v + TILE]
                    for a in range(8):
                        u = v - a if reverse else v - 8 + a
                        if not 0 <= u < 8:
                            continue
                        at = slice(TILE * u, TILE * u + TILE)
                        m = mask[2 * a + h, at]
                        term = source * weights[a] * jnp.concatenate([m, m], 1)
                        sums[u] = term if sums[u] is None else sums[u] + term
                        count[u] += 1
                        if count[u] == 8:
                            acc[at, lanes] += sums[u].astype(F32)

        loop(2, strip)

    loop(8, shift)


def gates(p, up, out):
    sigma = jax.nn.sigmoid(p)
    gate = p * sigma
    return (out * gate).astype(BF), up * out * (sigma * (1.0 + p * (1.0 - sigma))), up * gate


LOW, HIGH = slice(0, 128), slice(128, 256)


def ahead_inside_kernel(p_ref, dg_ref, taps_ref, live_ref, gated_ref, dgate_ref, ext, even, odd, mask, acc):
    ext[...] = p_ref[...].astype(F32)
    mix(ext, live_ref.at[HIGH], taps_ref, even, odd, mask, acc, False)
    p, up = p_ref[HIGH].astype(F32), dg_ref[HIGH].astype(F32)
    gated_ref[...], dgate_ref[...], _ = gates(p, up, acc[...])


def back_inside_kernel(p_ref, dg_ref, taps_ref, live_ref, part_ref, dconv_ref, ext, even, odd, mask, acc):
    p = p_ref[...].astype(F32)
    ext[...] = dg_ref[...].astype(F32) * (p * jax.nn.sigmoid(p))
    dconv_ref[...] = ext[HIGH]
    mix(ext, live_ref.at[LOW], taps_ref, even, odd, mask, acc, True)
    part_ref[...] = acc[...]


def ahead_edge_kernel(p_ref, dg_ref, taps_ref, live_ref, tail_ref, gated_hi, part_ref, gated_ref, low_ref, ext, even, odd, mask, acc):
    p, up = p_ref[LOW].astype(F32), dg_ref[LOW].astype(F32)
    ext[LOW] = tail_ref[...].astype(F32)
    ext[HIGH] = p
    mix(ext, live_ref.at[LOW], taps_ref, even, odd, mask, acc, False)
    gated_ref[LOW], d_gate, _ = gates(p, up, acc[...])
    gated_ref[HIGH] = gated_hi[...]
    low_ref[...] = (part_ref[...] + d_gate).astype(BF)


def back_edge_kernel(
    dconv_ref, head_ref, taps_ref, live_ref, low_ref, dgate_ref, ids, w_ref, dproj_ref, far_ref, w,
    ext, even, odd, mask, acc, sem,
):
    load = pltpu.make_async_copy(w_ref, w, sem)
    load.start()
    ext[LOW] = dconv_ref[...]
    ext[HIGH] = head_ref[...].astype(F32)
    mix(ext, live_ref.at[HIGH], taps_ref, even, odd, mask, acc, True)
    dproj_ref[LOW] = low_ref[...]
    dproj_ref[HIGH] = (acc[...] + dgate_ref[...]).astype(BF)
    load.wait()
    far_ref[...] = back_term(dproj_ref[...], w[place_of(ids, 4)].reshape(512, 512))


def back_term(d, block):
    return lax.dot_general(d, block, (((1,), (1,)), ((), ())), preferred_element_type=F32).astype(BF)


def mix_call(kernel, name, shapes, *operands, specs=None, scratch=()):
    return pl.pallas_call(
        kernel,
        in_specs=specs or [VMEM] * len(operands),
        out_specs=[VMEM] * len(shapes),
        out_shape=[jax.ShapeDtypeStruct(shape, kind) for shape, kind in shapes],
        scratch_shapes=[
            pltpu.VMEM((256, 512), F32),
            pltpu.VMEM((256, 256), BF),
            pltpu.VMEM((256, 256), BF),
            pltpu.VMEM((16, 128, LANES), BF),
            pltpu.VMEM((128, 512), F32),
            *scratch,
        ],
        compiler_params=pltpu.CompilerParams(vmem_limit_bytes=8 << 20),
        cost_estimate=pl.CostEstimate(flops=1 << 32, bytes_accessed=4 << 20, transcendentals=0),
        name=name,
    )(*operands)


def conv(ids, p, tail, head, d_gated, taps, back, ahead, w, cross):
    half, whole = (128, 512), (256, 512)
    tail = next_row(tail, 1)
    gated_hi, dgate_hi = mix_call(
        ahead_inside_kernel, "ahead_inside", [(half, BF), (half, F32)], p, d_gated, taps, back
    )
    head = next_row(after(head, gated_hi), -1)
    part, dconv_hi = mix_call(
        back_inside_kernel, "back_inside", [(half, F32), (half, F32)], p, d_gated, taps, ahead
    )
    theirs = to_other_core(after(cross, part))
    gated, low = mix_call(
        ahead_edge_kernel, "ahead_edge", [(whole, BF), (half, BF)], p, d_gated, taps, back, tail, gated_hi, part
    )
    d_proj, far, w = mix_call(
        back_edge_kernel, "back_edge", [(whole, BF), (whole, BF), (w.shape, BF)],
        dconv_hi, head, taps, ahead, low, dgate_hi, ids, w,
        specs=[VMEM] * 6 + [SMEM, HBM], scratch=[pltpu.SemaphoreType.DMA],
    )
    return gated, d_proj, far, w, theirs


NEAR = (3, 5, 2, 6, 1, 7, 0)


def near_kernel(ids, d_ref, w, *outs):
    d = d_ref[...]
    for steps, out in zip(NEAR, outs):
        out[...] = back_term(d, w[place_of(ids, steps)].reshape(512, 512))


def near_terms(ids, d_proj, weight):
    return pl.pallas_call(
        near_kernel,
        in_specs=[SMEM, VMEM, VMEM],
        out_specs=[VMEM] * 7,
        out_shape=[jax.ShapeDtypeStruct((256, 512), BF)] * 7,
        compiler_params=pltpu.CompilerParams(vmem_limit_bytes=4 << 20),
        cost_estimate=pl.CostEstimate(flops=2 * 256 * 512 * 512 * 7, bytes_accessed=6 << 20, transcendentals=0),
        name="near_terms",
    )(ids, d_proj, weight)


def add_three_kernel(a, b, c, out):
    out[...] = (a[...].astype(F32) + b[...].astype(F32) + c[...].astype(F32)).astype(BF)


def add_three(a, b, c):
    return pl.pallas_call(
        add_three_kernel,
        in_specs=[VMEM] * 3,
        out_specs=VMEM,
        out_shape=jax.ShapeDtypeStruct(a.shape, BF),
        compiler_params=pltpu.CompilerParams(vmem_limit_bytes=2 << 20),
        cost_estimate=pl.CostEstimate(flops=1 << 32, bytes_accessed=1 << 20, transcendentals=0),
        name="add_three",
    )(a, b, c)


def grad_kernel(ids, mine, theirs, d_mine, d_theirs, *refs):
    outs, out = refs[:4], refs[4]
    me = ids[2]
    dims = (((0,), (0,)), ((), ()))
    for k in range(NZ):
        zb = place_of(ids, k)
        total = lax.dot_general(mine[k], d_mine[...], dims, preferred_element_type=F32)
        total += lax.dot_general(theirs[(NZ - k) % NZ], d_theirs[...], dims, preferred_element_type=F32)
        total = total.astype(BF)
        for xp in range(2):
            dy = lax.rem(zb // 2 + 4 - ids[0], 4)
            dx = lax.rem(lax.rem(zb, 2) * 2 + xp + 4 - ids[1], 4)
            out[jnp.where(me == 0, dy, dx), jnp.where(me == 0, dx, dy)] = total[xp * 128 : xp * 128 + 128]
    for k in range(4):
        outs[k][...] = out[k]


def weight_terms(ids, mine, theirs, d_mine, d_theirs):
    return pl.pallas_call(
        grad_kernel,
        in_specs=[SMEM] + [VMEM] * 4,
        out_specs=[VMEM] * 4,
        out_shape=[jax.ShapeDtypeStruct((4, 128, 512), BF)] * 4,
        scratch_shapes=[pltpu.VMEM((4, 4, 128, 512), BF)],
        compiler_params=pltpu.CompilerParams(vmem_limit_bytes=6 << 20),
        cost_estimate=pl.CostEstimate(flops=2 * 512 * 2048 * 512, bytes_accessed=5 << 20, transcendentals=0),
        name="weight_terms",
    )(ids, mine, theirs, d_mine, d_theirs)


def sum_up(ids, d_proj, far, weight, mine, theirs):
    p = around_z(far, 1)
    d_theirs = to_other_core(d_proj)
    p3, q3, p2, q2, p1, q1, own = near_terms(ids, d_proj, weight)
    q = around_z(q3, -1)
    g = weight_terms(ids, mine, theirs, d_proj, after(d_theirs, own))
    p = around_z(add(after(p3, g[0]), p), 1)
    s = [g[0]] + [wide(g[k], k) for k in (1, 2, 3)]
    q = around_z(add(q2, q), -1)
    p = around_z(add(p2, p), 1)
    q_last = add(q1, q)
    q = around_z(q_last, -1)
    p_last = add(p1, p)
    p = around_z(p_last, 1)
    n = sum_four([after(s[0], p_last, q_last)] + s[1:])
    n = [n[0]] + [narrow(n[k], k) for k in (1, 2, 3)]
    d_tokens = add_three(own, p, q)
    return d_tokens, sum(v.astype(F32) for v in n)


def body(tokens, contig_lengths, w_in, conv_filter, d_gated):
    rows = tokens.shape[0]
    seq_total = rows * NY * NX * NC
    row, z = lax.axis_index("row"), lax.axis_index("col")
    core, chip = row % NC, row // NC
    y, x = chip // NX, chip % NX
    ids = jnp.stack([y, x, core, z]).astype(jnp.int32)

    w = [narrow(w_in, 4 - k) for k in (1, 2, 3)]
    p1, q1 = around_z(tokens, 1), around_z(tokens, -1)
    first = jnp.where(core == 0, x, y).astype(jnp.int32).reshape(1)
    row_block = stack(first, [w_in] + w)
    own = [row_block] + [wide(row_block, 4 - k) for k in (1, 2, 3)]
    other = [to_other_core(block) for block in own]
    p2, q2 = around_z(after(p1, row_block), 1), around_z(after(q1, row_block), -1)
    conv_filter, contig_lengths = after((conv_filter, contig_lengths), q1)
    back, ahead = live_taps(contig_lengths, row * rows, rows)
    taps = conv_filter.astype(BF).reshape(16, 8, 1, 512).transpose(1, 0, 2, 3)
    taps = jnp.broadcast_to(taps, (8, 16, TILE, 512))
    p3, q3 = around_z(p2, 1), around_z(q2, -1)
    p4 = around_z(after(p3, back, ahead, taps), 1)
    early = project_early(ids, [tokens, q1, p1, q2, p2], own + other)
    weight = early[1]
    projected, tail, head, mine, cross = project_late(ids, [q3, p3, p4], early, d_gated)
    gated, d_proj, far, weight, theirs = conv(
        ids, projected, tail, head, d_gated, taps, back, ahead, weight, cross
    )
    d_tokens, grad = sum_up(ids, d_proj, far, weight, mine, theirs)
    return gated, d_tokens, grad * (1.0 / math.sqrt(seq_total))


def solution(mesh):
    placed = (P("row", "col"), P(), P("row", "col"), P(None, "col"), P("row", "col"))
    return jax.shard_map(
        body,
        mesh=mesh,
        in_specs=placed,
        out_specs=(P("row", "col"), P("row", "col"), P("row", "col")),
        check_vma=False,
    )
```

time: 319 us -> 123 us (0.39)
  the two profiles are of different devices: /device:TPU:96 before, /device:TPU:4 now
where the time goes in v1:
time: 123 us; the launch traced here: 122 us
  starting transfers between devices  48.5 us (39%)
  waiting for transfers between devices  37.5 us (30%)
  Pallas kernels  30.7 us (25%)
  other arithmetic  2.8 us (2%)
  local copies, waits for them, and re-layouts  2.08 us (2%)
    ppermute x14, waiting for transfers between devices, around_z(): return lax.ppermute(value, ('row', 'col'), pairs)  36.6 us
    ppermute x14, starting transfers between devices, around_z(): return lax.ppermute(value, ('row', 'col'), pairs)  21.2 us
    pallas_call x4, Pallas kernels, mix_call(): pl.pallas_call(kernel, in_specs=specs or [VMEM] * len(operands), out_spec...  19.1 us
    ppermute x6, starting transfers between devices, narrow(): return lax.ppermute(value, 'row', pairs)  14.3 us
    ppermute x6, starting transfers between devices, wide(): return lax.ppermute(value, 'row', pairs)  9.43 us
    pallas_call x1, Pallas kernels, project_early(): pl.pallas_call(early_kernel, in_specs=[SMEM] + [HBM] * 13, out_specs=[VME...  5.2 us
  transfers between devices with their start and end apart: 34, of which 12 were waited for; matrix products, arithmetic and copies ran while one was open for 3% of the time, Pallas kernels for 23%

profile of v1, /device:TPU:4, one launch (start us, length us, event | category | flops | bytes accessed | tf_op | source)
XLA Modules:
  0.0 122.4 jit_solution(5429952814737023691)
XLA Ops:
  0.6 2.3 %collective-permute-start.2 = (bf16[128,512]{1,0:T(8,128)(2,1)}, bf16[128,512]{1,0:T(8,128)(2,1)S(1)}, u32[]{:S(2)}, u32[]{:S(2)}) collective-permute-start(bf16[128,512]{1,0:T(8,128)(2,1)} %refs_0_.2), channel_id=1, source_target_pairs={{0,32},{8,136},{16,48},{24,152},{32,0},{40,168},{48,16},{56,184},{... | collective-permute-start | bytes 393224 | tf_op jit(solution)/shard_map/ppermute | solution.py:38
  3.4 1.6 %collective-permute-start.3 = (bf16[128,512]{1,0:T(8,128)(2,1)}, bf16[128,512]{1,0:T(8,128)(2,1)S(1)}, u32[]{:S(2)}, u32[]{:S(2)}) collective-permute-start(bf16[128,512]{1,0:T(8,128)(2,1)} %refs_0_.2), channel_id=1, source_target_pairs={{0,16},{8,72},{16,32},{24,88},{32,48},{40,104},{48,0},{56,120},{64... | collective-permute-start | bytes 393224 | tf_op jit(solution)/shard_map/ppermute | solution.py:38
  5.0 4.2 %collective-permute-start = (bf16[256,512]{1,0:T(8,128)(2,1)}, bf16[256,512]{1,0:T(8,128)(2,1)S(1)}, u32[]{:S(2)}, u32[]{:S(2)}) collective-permute-start(bf16[256,512]{1,0:T(8,128)(2,1)} %refs_0_.3), channel_id=1, source_target_pairs={{0,7},{1,0},{2,1},{3,2},{4,3},{5,4},{6,5},{7,6},{8,9},{9,10},{10,1... | collective-permute-start | bytes 786440 | tf_op jit(solution)/shard_map/ppermute | solution.py:30
  10.2 1.7 %collective-permute-start.12 = (bf16[4,128,512]{2,1,0:T(8,128)(2,1)S(1)}, bf16[4,128,512]{2,1,0:T(8,128)(2,1)S(1)}, u32[]{:S(2)}, u32[]{:S(2)}) collective-permute-start(bf16[4,128,512]{2,1,0:T(8,128)(2,1)S(1)} %stack.21.refs_5_), channel_id=1, source_target_pairs={{0,64},{8,24},{16,80},{24,40},{32,96},{40,56},{48,112},{56,8},{64,... | collective-permute-start | bytes 1572872 | tf_op jit(solution)/shard_map/ppermute | solution.py:46
  11.9 2.9 %collective-permute-start.11 = (bf16[4,128,512]{2,1,0:T(8,128)(2,1)S(1)}, bf16[4,128,512]{2,1,0:T(8,128)(2,1)S(1)}, u32[]{:S(2)}, u32[]{:S(2)}) collective-permute-start(bf16[4,128,512]{2,1,0:T(8,128)(2,1)S(1)} %stack.21.refs_5_), channel_id=1, source_target_pairs={{0,128},{8,40},{16,144},{24,56},{32,160},{40,8},{48,176},{56,24},{... | collective-permute-start | bytes 1572872 | tf_op jit(solution)/shard_map/ppermute | solution.py:46
  16.1 1.5 %collective-permute-start.6 = (bf16[256,512]{1,0:T(8,128)(2,1)}, bf16[256,512]{1,0:T(8,128)(2,1)S(1)}, u32[]{:S(2)}, u32[]{:S(2)}) collective-permute-start(bf16[256,512]{1,0:T(8,128)(2,1)} %refs_0_.3), channel_id=1, source_target_pairs={{0,1},{1,2},{2,3},{3,4},{4,5},{5,6},{6,7},{7,0},{8,15},{9,8},{10,9... | collective-permute-start | bytes 786440 | tf_op jit(solution)/shard_map/ppermute | solution.py:30
  17.6 3.9 %collective-permute-start.4 = (bf16[256,512]{1,0:T(8,128)(2,1)S(1)}, bf16[256,512]{1,0:T(8,128)(2,1)S(1)}, u32[]{:S(2)}, u32[]{:S(2)}) collective-permute-start(bf16[256,512]{1,0:T(8,128)(2,1)S(1)} %collective-permute-done.refs_1_), channel_id=1, source_target_pairs={{0,7},{1,0},{2,1},{3,2},{4,3},{5,4},{6,5},{7,6},{8,9},{9,10},{10,1... | collective-permute-start | bytes 786440 | tf_op jit(solution)/shard_map/ppermute | solution.py:30
  21.5 6.3 %collective-permute-done.6.refs_2_ = bf16[256,512]{1,0:T(8,128)(2,1)S(1)} collective-permute-done((bf16[256,512]{1,0:T(8,128)(2,1)}, bf16[256,512]{1,0:T(8,128)(2,1)S(1)}, u32[]{:S(2)}, u32[]{:S(2)}) %collective-permute-start.6) | collective-permute-done | bytes 262176 | tf_op jit(solution)/shard_map/ppermute | solution.py:30
  31.5 3.9 %collective-permute-done.7.refs_4_ = bf16[256,512]{1,0:T(8,128)(2,1)S(1)} collective-permute-done((bf16[256,512]{1,0:T(8,128)(2,1)S(1)}, bf16[256,512]{1,0:T(8,128)(2,1)S(1)}, u32[]{:S(2)}, u32[]{:S(2)}) %collective-permute-start.7) | collective-permute-done | bytes 262176 | tf_op jit(solution)/shard_map/ppermute | solution.py:30
  35.6 8.1 %collective-permute-done.8.refs_1_ = bf16[256,512]{1,0:T(8,128)(2,1)S(1)} collective-permute-done((bf16[256,512]{1,0:T(8,128)(2,1)S(1)}, bf16[256,512]{1,0:T(8,128)(2,1)S(1)}, u32[]{:S(2)}, u32[]{:S(2)}) %collective-permute-start.8) | collective-permute-done | bytes 262176 | tf_op jit(solution)/shard_map/ppermute | solution.py:30
  44.1 2.3 %collective-permute-start.9 = (bf16[256,512]{1,0:T(8,128)(2,1)S(1)}, bf16[256,512]{1,0:T(8,128)(2,1)S(1)}, u32[]{:S(2)}, u32[]{:S(2)}) collective-permute-start(bf16[256,512]{1,0:T(8,128)(2,1)S(1)} %collective-permute-done.8.refs_1_), channel_id=1, source_target_pairs={{0,1},{1,2},{2,3},{3,4},{4,5},{5,6},{6,7},{7,0},{8,15},{9,8},{10,9... | collective-permute-start | bytes 786440 | tf_op jit(solution)/shard_map/ppermute | solution.py:30
  46.4 5.2 %project_early.1 = (f32[256,512]{1,0:T(8,128)S(1)}, bf16[8,2,2,128,512]{4,3,2,1,0:T(8,128)(2,1)S(1)}, bf16[8,256,256]{2,1,0:T(8,128)(2,1)S(1)}, bf16[8,256,256]{2,1,0:T(8,128)(2,1)S(1)}) custom-call(s32[4]{0:T(128)S(1)} %pad_add_fusion.ids, bf16[256,512]{1,0:T(8,128)(2,1)S(1)} %copy-done.2, bf16[256,512]{1,0:T(8,128)(2,1)S(1)} %collective-permute-done.refs_1_, ...), custom_call_target="tpu_custom_call" | custom-call | flops 4294967296 | bytes 8388608 | tf_op jit(solution)/shard_map/project_early/pallas_call | solution.py:225
  53.3 4.3 %ahead_inside.1 = (bf16[128,512]{1,0:T(8,128)(2,1)S(1)}, f32[128,512]{1,0:T(8,128)S(1)}) custom-call(bf16[256,512]{1,0:T(8,128)(2,1)S(1)} %get-tuple-element.55.p_ref, bf16[256,512]{1,0:T(8,128)(2,1)S(1)} %copy-done, bf16[8,16,16,512]{3,2,1,0:T(8,128)(2,1)S(1)} %broadcast_in_dim.46.taps_ref, bf16[256,128]{1,0:T(8,128)(2,1)S(1)} %broadcast_in_dim.42.live_ref), custom_call_target="tpu_custom_call" | custom-call | flops 4294967296 | bytes 4194304 | tf_op jit(solution)/shard_map/ahead_inside/pallas_call | solution.py:355
  57.6 4.3 %back_inside.1 = (f32[128,512]{1,0:T(8,128)S(1)}, f32[128,512]{1,0:T(8,128)S(1)}) custom-call(bf16[256,512]{1,0:T(8,128)(2,1)S(1)} %get-tuple-element.55.p_ref, bf16[256,512]{1,0:T(8,128)(2,1)S(1)} %copy-done, bf16[8,16,16,512]{3,2,1,0:T(8,128)(2,1)S(1)} %broadcast_in_dim.46.taps_ref, bf16[256,128]{1,0:T(8,128)(2,1)S(1)} %broadcast_in_dim.44.live_ref), custom_call_target="tpu_custom_call" | custom-call | flops 4294967296 | bytes 4194304 | tf_op jit(solution)/shard_map/back_inside/pallas_call | solution.py:355
  62.0 1.8 %collective-permute-start.18 = (bf16[128,512]{1,0:T(8,128)(2,1)S(1)}, bf16[128,512]{1,0:T(8,128)(2,1)S(1)}, u32[]{:S(2)}, u32[]{:S(2)}) collective-permute-start(bf16[128,512]{1,0:T(8,128)(2,1)S(1)} %get-tuple-element.62), channel_id=1, source_target_pairs={{0,248},{8,0},{16,8},{24,16},{32,24},{40,32},{48,40},{56,48},{64,5... | collective-permute-start | bytes 393224 | tf_op jit(solution)/shard_map/ppermute | solution.py:55
  63.8 5.0 %ahead_edge.1 = (bf16[256,512]{1,0:T(8,128)(2,1)}, bf16[128,512]{1,0:T(8,128)(2,1)S(1)}) custom-call(bf16[256,512]{1,0:T(8,128)(2,1)S(1)} %get-tuple-element.55.p_ref, bf16[256,512]{1,0:T(8,128)(2,1)S(1)} %copy-done, bf16[8,16,16,512]{3,2,1,0:T(8,128)(2,1)S(1)} %broadcast_in_dim.46.taps_ref, bf16[256,128]{1,0:T(8,128)(2,1)S(1)} %broadcast_in_dim.42.live_ref, ...), custom_call_target="tpu_custom_call" | custom-call | flops 4294967296 | bytes 4194304 | tf_op jit(solution)/shard_map/ahead_edge/pallas_call | solution.py:355
  68.8 5.4 %back_edge.1 = (bf16[256,512]{1,0:T(8,128)(2,1)S(1)}, bf16[256,512]{1,0:T(8,128)(2,1)S(1)}, bf16[8,2,2,128,512]{4,3,2,1,0:T(8,128)(2,1)S(1)}) custom-call(f32[128,512]{1,0:T(8,128)S(1)} %get-tuple-element.60.dconv_ref, bf16[128,512]{1,0:T(8,128)(2,1)S(1)} %collective-permute-done.18.head_ref, bf16[8,16,16,512]{3,2,1,0:T(8,128)(2,1)S(1)} %broadcast_in_dim.46.taps_ref, ...), custom_call_target="tpu_custom_call" | custom-call | flops 4294967296 | bytes 4194304 | tf_op jit(solution)/shard_map/back_edge/pallas_call | solution.py:355
  75.7 1.7 %near_terms.1 = (bf16[256,512]{1,0:T(8,128)(2,1)S(1)}, bf16[256,512]{1,0:T(8,128)(2,1)S(1)}, bf16[256,512]{1,0:T(8,128)(2,1)S(1)}, bf16[256,512]{1,0:T(8,128)(2,...) custom-call(s32[4]{0:T(128)S(1)} %pad_add_fusion.ids, ...), custom_call_target="tpu_custom_call" | custom-call | flops 939524096 | bytes 6291456 | tf_op jit(solution)/shard_map/near_terms/pallas_call | solution.py:406
  77.4 2.5 %collective-permute-start.25 = (bf16[256,512]{1,0:T(8,128)(2,1)S(1)}, bf16[256,512]{1,0:T(8,128)(2,1)S(1)}, u32[]{:S(2)}, u32[]{:S(2)}) collective-permute-start(bf16[256,512]{1,0:T(8,128)(2,1)S(1)} %get-tuple-element.80), channel_id=1, source_target_pairs={{0,7},{1,0},{2,1},{3,2},{4,3},{5,4},{6,5},{7,6},{8,9},{9,10},{10,1... | collective-permute-start | bytes 786440 | tf_op jit(solution)/shard_map/ppermute | solution.py:30
  79.9 2.0 %weight_terms.1 = (bf16[4,128,512]{2,1,0:T(8,128)(2,1)S(1)}, bf16[4,128,512]{2,1,0:T(8,128)(2,1)S(1)}, bf16[4,128,512]{2,1,0:T(8,128)(2,1)S(1)}, bf16[4,128,512]{2,1,0:T(8,128)(2,1)S(1)}) custom-call(s32[4]{0:T(128)S(1)} %pad_add_fusion.ids, bf16[8,256,256]{2,1,0:T(8,128)(2,1)S(1)} %get-tuple-element.71.mine, ...), custom_call_target="tpu_custom_call" | custom-call | flops 1073741824 | bytes 5242880 | tf_op jit(solution)/shard_map/weight_terms/pallas_call | solution.py:451
  81.9 1.8 %collective-permute-done.21.b = bf16[256,512]{1,0:T(8,128)(2,1)S(1)} collective-permute-done((bf16[256,512]{1,0:T(8,128)(2,1)S(1)}, bf16[256,512]{1,0:T(8,128)(2,1)S(1)}, u32[]{:S(2)}, u32[]{:S(2)}) %collective-permute-start.21) | collective-permute-done | bytes 262176 | tf_op jit(solution)/shard_map/ppermute | solution.py:30
  84.1 1.4 %collective-permute-start.29 = (bf16[4,128,512]{2,1,0:T(8,128)(2,1)S(1)}, bf16[4,128,512]{2,1,0:T(8,128)(2,1)S(1)}, u32[]{:S(2)}, u32[]{:S(2)}) collective-permute-start(bf16[4,128,512]{2,1,0:T(8,128)(2,1)S(1)} %get-tuple-element.83), channel_id=1, source_target_pairs={{0,128},{8,40},{16,144},{24,56},{32,160},{40,8},{48,176},{56,24},{... | collective-permute-start | bytes 1572872 | tf_op jit(solution)/shard_map/ppermute | solution.py:46
  85.6 1.8 %collective-permute-start.30 = (bf16[4,128,512]{2,1,0:T(8,128)(2,1)S(1)}, bf16[4,128,512]{2,1,0:T(8,128)(2,1)S(1)}, u32[]{:S(2)}, u32[]{:S(2)}) collective-permute-start(bf16[4,128,512]{2,1,0:T(8,128)(2,1)S(1)} %get-tuple-element.84), channel_id=1, source_target_pairs={{0,192},{8,56},{16,208},{24,8},{32,224},{40,24},{48,240},{56,40},{... | collective-permute-start | bytes 1572872 | tf_op jit(solution)/shard_map/ppermute | solution.py:46
  87.4 3.0 %collective-permute-start.26 = (bf16[256,512]{1,0:T(8,128)(2,1)S(1)}, bf16[256,512]{1,0:T(8,128)(2,1)S(1)}, u32[]{:S(2)}, u32[]{:S(2)}) collective-permute-start(bf16[256,512]{1,0:T(8,128)(2,1)S(1)} %add.72), channel_id=1, source_target_pairs={{0,7},{1,0},{2,1},{3,2},{4,3},{5,4},{6,5},{7,6},{8,9},{9,10},{10,1... | collective-permute-start | bytes 786440 | tf_op jit(solution)/shard_map/ppermute | solution.py:30
  91.5 3.0 %collective-permute-done.26.b = bf16[256,512]{1,0:T(8,128)(2,1)S(1)} collective-permute-done((bf16[256,512]{1,0:T(8,128)(2,1)S(1)}, bf16[256,512]{1,0:T(8,128)(2,1)S(1)}, u32[]{:S(2)}, u32[]{:S(2)}) %collective-permute-start.26) | collective-permute-done | bytes 262176 | tf_op jit(solution)/shard_map/ppermute | solution.py:30
  94.6 5.5 %collective-permute-done.23.b = bf16[256,512]{1,0:T(8,128)(2,1)S(1)} collective-permute-done((bf16[256,512]{1,0:T(8,128)(2,1)S(1)}, bf16[256,512]{1,0:T(8,128)(2,1)S(1)}, u32[]{:S(2)}, u32[]{:S(2)}) %collective-permute-start.23) | collective-permute-done | bytes 262176 | tf_op jit(solution)/shard_map/ppermute | solution.py:30
  101.3 5.1 %collective-permute-start.31 = (bf16[128,512]{1,0:T(8,128)(2,1)S(1)}, bf16[128,512]{1,0:T(8,128)(2,1)S(1)}, u32[]{:S(2)}, u32[]{:S(2)}) collective-permute-start(bf16[128,512]{1,0:T(8,128)(2,1)S(1)} %get-tuple-element.86), channel_id=1, source_target_pairs={{0,16},{8,72},{16,32},{24,88},{32,48},{40,104},{48,0},{56,120},{64... | collective-permute-start | bytes 393224 | tf_op jit(solution)/shard_map/ppermute | solution.py:38
  106.4 2.3 %collective-permute-start.32 = (bf16[128,512]{1,0:T(8,128)(2,1)S(1)}, bf16[128,512]{1,0:T(8,128)(2,1)S(1)}, u32[]{:S(2)}, u32[]{:S(2)}) collective-permute-start(bf16[128,512]{1,0:T(8,128)(2,1)S(1)} %get-tuple-element.87), channel_id=1, source_target_pairs={{0,32},{8,136},{16,48},{24,152},{32,0},{40,168},{48,16},{56,184},{... | collective-permute-start | bytes 393224 | tf_op jit(solution)/shard_map/ppermute | solution.py:38
  108.7 2.5 %collective-permute-start.33 = (bf16[128,512]{1,0:T(8,128)(2,1)S(1)}, bf16[128,512]{1,0:T(8,128)(2,1)S(1)}, u32[]{:S(2)}, u32[]{:S(2)}) collective-permute-start(bf16[128,512]{1,0:T(8,128)(2,1)S(1)} %get-tuple-element.88), channel_id=1, source_target_pairs={{0,48},{8,200},{16,0},{24,216},{32,16},{40,232},{48,32},{56,248},{... | collective-permute-start | bytes 393224 | tf_op jit(solution)/shard_map/ppermute | solution.py:38
  111.2 2.8 %collective-permute-start.27 = (bf16[256,512]{1,0:T(8,128)(2,1)S(1)}, bf16[256,512]{1,0:T(8,128)(2,1)S(1)}, u32[]{:S(2)}, u32[]{:S(2)}) collective-permute-start(bf16[256,512]{1,0:T(8,128)(2,1)S(1)} %add.73), channel_id=1, source_target_pairs={{0,7},{1,0},{2,1},{3,2},{4,3},{5,4},{6,5},{7,6},{8,9},{9,10},{10,1... | collective-permute-start | bytes 786440 | tf_op jit(solution)/shard_map/ppermute | solution.py:30
  114.9 3.0 %collective-permute-done.27.c = bf16[256,512]{1,0:T(8,128)(2,1)S(1)} collective-permute-done((bf16[256,512]{1,0:T(8,128)(2,1)S(1)}, bf16[256,512]{1,0:T(8,128)(2,1)S(1)}, u32[]{:S(2)}, u32[]{:S(2)}) %collective-permute-start.27) | collective-permute-done | bytes 262176 | tf_op jit(solution)/shard_map/ppermute | solution.py:30
  117.9 3.7 %collective-permute-done.24.b = bf16[256,512]{1,0:T(8,128)(2,1)S(1)} collective-permute-done((bf16[256,512]{1,0:T(8,128)(2,1)S(1)}, bf16[256,512]{1,0:T(8,128)(2,1)S(1)}, u32[]{:S(2)}, u32[]{:S(2)}) %collective-permute-start.24) | collective-permute-done | bytes 262176 | tf_op jit(solution)/shard_map/ppermute | solution.py:30
  (72 shorter events, 14.5 us)
Async XLA Ops:
  0.6 8.6 %collective-permute-start.2 = (bf16[128,512]{1,0:T(8,128)(2,1)}, bf16[128,512]{1,0:T(8,128)(2,1)S(1)}, u32[]{:S(2)}, u32[]{:S(2)}) collective-permute-start(bf16[128,512]{1,0:T(8,128)(2,1)} %refs_0_.2), channel_id=1, source_target_pairs={{0,32},{8,136},{16,48},{24,152},{32,0},{40,168},{48,16},{56,184},{... | collective-permute-start | bytes 393224 | tf_op jit(solution)/shard_map/ppermute | solution.py:38
  3.0 6.3 %collective-permute-start.1 = (bf16[128,512]{1,0:T(8,128)(2,1)}, bf16[128,512]{1,0:T(8,128)(2,1)S(1)}, u32[]{:S(2)}, u32[]{:S(2)}) collective-permute-start(bf16[128,512]{1,0:T(8,128)(2,1)} %refs_0_.2), channel_id=1, source_target_pairs={{0,48},{8,200},{16,0},{24,216},{32,16},{40,232},{48,32},{56,248},{... | collective-permute-start | bytes 393224 | tf_op jit(solution)/shard_map/ppermute | solution.py:38
  3.4 5.9 %collective-permute-start.3 = (bf16[128,512]{1,0:T(8,128)(2,1)}, bf16[128,512]{1,0:T(8,128)(2,1)S(1)}, u32[]{:S(2)}, u32[]{:S(2)}) collective-permute-start(bf16[128,512]{1,0:T(8,128)(2,1)} %refs_0_.2), channel_id=1, source_target_pairs={{0,16},{8,72},{16,32},{24,88},{32,48},{40,104},{48,0},{56,120},{64... | collective-permute-start | bytes 393224 | tf_op jit(solution)/shard_map/ppermute | solution.py:38
  5.0 12.6 %collective-permute-start = (bf16[256,512]{1,0:T(8,128)(2,1)}, bf16[256,512]{1,0:T(8,128)(2,1)S(1)}, u32[]{:S(2)}, u32[]{:S(2)}) collective-permute-start(bf16[256,512]{1,0:T(8,128)(2,1)} %refs_0_.3), channel_id=1, source_target_pairs={{0,7},{1,0},{2,1},{3,2},{4,3},{5,4},{6,5},{7,6},{8,9},{9,10},{10,1... | collective-permute-start | bytes 786440 | tf_op jit(solution)/shard_map/ppermute | solution.py:30
  10.2 19.3 %collective-permute-start.12 = (bf16[4,128,512]{2,1,0:T(8,128)(2,1)S(1)}, bf16[4,128,512]{2,1,0:T(8,128)(2,1)S(1)}, u32[]{:S(2)}, u32[]{:S(2)}) collective-permute-start(bf16[4,128,512]{2,1,0:T(8,128)(2,1)S(1)} %stack.21.refs_5_), channel_id=1, source_target_pairs={{0,64},{8,24},{16,80},{24,40},{32,96},{40,56},{48,112},{56,8},{64,... | collective-permute-start | bytes 1572872 | tf_op jit(solution)/shard_map/ppermute | solution.py:46
  11.9 18.2 %collective-permute-start.11 = (bf16[4,128,512]{2,1,0:T(8,128)(2,1)S(1)}, bf16[4,128,512]{2,1,0:T(8,128)(2,1)S(1)}, u32[]{:S(2)}, u32[]{:S(2)}) collective-permute-start(bf16[4,128,512]{2,1,0:T(8,128)(2,1)S(1)} %stack.21.refs_5_), channel_id=1, source_target_pairs={{0,128},{8,40},{16,144},{24,56},{32,160},{40,8},{48,176},{56,24},{... | collective-permute-start | bytes 1572872 | tf_op jit(solution)/shard_map/ppermute | solution.py:46
  14.8 15.4 %collective-permute-start.10 = (bf16[4,128,512]{2,1,0:T(8,128)(2,1)S(1)}, bf16[4,128,512]{2,1,0:T(8,128)(2,1)S(1)}, u32[]{:S(2)}, u32[]{:S(2)}) collective-permute-start(bf16[4,128,512]{2,1,0:T(8,128)(2,1)S(1)} %stack.21.refs_5_), channel_id=1, source_target_pairs={{0,192},{8,56},{16,208},{24,8},{32,224},{40,24},{48,240},{56,40},{... | collective-permute-start | bytes 1572872 | tf_op jit(solution)/shard_map/ppermute | solution.py:46
  16.1 11.7 %collective-permute-start.6 = (bf16[256,512]{1,0:T(8,128)(2,1)}, bf16[256,512]{1,0:T(8,128)(2,1)S(1)}, u32[]{:S(2)}, u32[]{:S(2)}) collective-permute-start(bf16[256,512]{1,0:T(8,128)(2,1)} %refs_0_.3), channel_id=1, source_target_pairs={{0,1},{1,2},{2,3},{3,4},{4,5},{5,6},{6,7},{7,0},{8,15},{9,8},{10,9... | collective-permute-start | bytes 786440 | tf_op jit(solution)/shard_map/ppermute | solution.py:30
  17.6 11.9 %collective-permute-start.4 = (bf16[256,512]{1,0:T(8,128)(2,1)S(1)}, bf16[256,512]{1,0:T(8,128)(2,1)S(1)}, u32[]{:S(2)}, u32[]{:S(2)}) collective-permute-start(bf16[256,512]{1,0:T(8,128)(2,1)S(1)} %collective-permute-done.refs_1_), channel_id=1, source_target_pairs={{0,7},{1,0},{2,1},{3,2},{4,3},{5,4},{6,5},{7,6},{8,9},{9,10},{10,1... | collective-permute-start | bytes 786440 | tf_op jit(solution)/shard_map/ppermute | solution.py:30
  27.8 7.6 %collective-permute-start.7 = (bf16[256,512]{1,0:T(8,128)(2,1)S(1)}, bf16[256,512]{1,0:T(8,128)(2,1)S(1)}, u32[]{:S(2)}, u32[]{:S(2)}) collective-permute-start(bf16[256,512]{1,0:T(8,128)(2,1)S(1)} %collective-permute-done.6.refs_2_), channel_id=1, source_target_pairs={{0,1},{1,2},{2,3},{3,4},{4,5},{5,6},{6,7},{7,0},{8,15},{9,8},{10,9... | collective-permute-start | bytes 786440 | tf_op jit(solution)/shard_map/ppermute | solution.py:30
  29.5 14.6 %collective-permute-start.13 = (bf16[4,128,512]{2,1,0:T(8,128)(2,1)S(1)}, bf16[4,128,512]{2,1,0:T(8,128)(2,1)S(1)}, u32[]{:S(2)}, u32[]{:S(2)}) collective-permute-start(bf16[4,128,512]{2,1,0:T(8,128)(2,1)S(1)} %stack.21.refs_5_), channel_id=1, source_target_pairs={{0,8},{8,0},{16,24},{24,16},{32,40},{40,32},{48,56},{56,48},{64,72... | collective-permute-start | bytes 1572872 | tf_op jit(solution)/shard_map/ppermute | solution.py:50
  29.5 16.9 %collective-permute-start.16 = (bf16[4,128,512]{2,1,0:T(8,128)(2,1)S(1)}, bf16[4,128,512]{2,1,0:T(8,128)(2,1)S(1)}, u32[]{:S(2)}, u32[]{:S(2)}) collective-permute-start(bf16[4,128,512]{2,1,0:T(8,128)(2,1)S(1)} %collective-permute-done.12.refs_8_), channel_id=1, source_target_pairs={{0,8},{8,0},{16,24},{24,16},{32,40},{40,32},{48,56},{56,48},{64,72... | collective-permute-start | bytes 1572872 | tf_op jit(solution)/shard_map/ppermute | solution.py:50
  30.0 16.4 %collective-permute-start.15 = (bf16[4,128,512]{2,1,0:T(8,128)(2,1)S(1)}, bf16[4,128,512]{2,1,0:T(8,128)(2,1)S(1)}, u32[]{:S(2)}, u32[]{:S(2)}) collective-permute-start(bf16[4,128,512]{2,1,0:T(8,128)(2,1)S(1)} %collective-permute-done.11.refs_7_), channel_id=1, source_target_pairs={{0,8},{8,0},{16,24},{24,16},{32,40},{40,32},{48,56},{56,48},{64,72... | collective-permute-start | bytes 1572872 | tf_op jit(solution)/shard_map/ppermute | solution.py:50
  30.1 16.3 %collective-permute-start.14 = (bf16[4,128,512]{2,1,0:T(8,128)(2,1)S(1)}, bf16[4,128,512]{2,1,0:T(8,128)(2,1)S(1)}, u32[]{:S(2)}, u32[]{:S(2)}) collective-permute-start(bf16[4,128,512]{2,1,0:T(8,128)(2,1)S(1)} %collective-permute-done.10.refs_6_), channel_id=1, source_target_pairs={{0,8},{8,0},{16,24},{24,16},{32,40},{40,32},{48,56},{56,48},{64,72... | collective-permute-start | bytes 1572872 | tf_op jit(solution)/shard_map/ppermute | solution.py:50
  35.4 8.3 %collective-permute-start.8 = (bf16[256,512]{1,0:T(8,128)(2,1)S(1)}, bf16[256,512]{1,0:T(8,128)(2,1)S(1)}, u32[]{:S(2)}, u32[]{:S(2)}) collective-permute-start(bf16[256,512]{1,0:T(8,128)(2,1)S(1)} %collective-permute-done.7.refs_4_), channel_id=1, source_target_pairs={{0,1},{1,2},{2,3},{3,4},{4,5},{5,6},{6,7},{7,0},{8,15},{9,8},{10,9... | collective-permute-start | bytes 786440 | tf_op jit(solution)/shard_map/ppermute | solution.py:30
  43.7 7.9 %collective-permute-start.5 = (bf16[256,512]{1,0:T(8,128)(2,1)S(1)}, bf16[256,512]{1,0:T(8,128)(2,1)S(1)}, u32[]{:S(2)}, u32[]{:S(2)}) collective-permute-start(bf16[256,512]{1,0:T(8,128)(2,1)S(1)} %collective-permute-done.4.refs_3_), channel_id=1, source_target_pairs={{0,7},{1,0},{2,1},{3,2},{4,3},{5,4},{6,5},{7,6},{8,9},{9,10},{10,1... | collective-permute-start | bytes 786440 | tf_op jit(solution)/shard_map/ppermute | solution.py:30
  44.1 7.8 %collective-permute-start.9 = (bf16[256,512]{1,0:T(8,128)(2,1)S(1)}, bf16[256,512]{1,0:T(8,128)(2,1)S(1)}, u32[]{:S(2)}, u32[]{:S(2)}) collective-permute-start(bf16[256,512]{1,0:T(8,128)(2,1)S(1)} %collective-permute-done.8.refs_1_), channel_id=1, source_target_pairs={{0,1},{1,2},{2,3},{3,4},{4,5},{5,6},{6,7},{7,0},{8,15},{9,8},{10,9... | collective-permute-start | bytes 786440 | tf_op jit(solution)/shard_map/ppermute | solution.py:30
  53.2 10.6 %collective-permute-start.17 = (bf16[128,512]{1,0:T(8,128)(2,1)S(1)}, bf16[128,512]{1,0:T(8,128)(2,1)S(1)}, u32[]{:S(2)}, u32[]{:S(2)}) collective-permute-start(bf16[128,512]{1,0:T(8,128)(2,1)S(1)} %get-tuple-element.56), channel_id=1, source_target_pairs={{0,8},{8,16},{16,24},{24,32},{32,40},{40,48},{48,56},{56,64},{64,7... | collective-permute-start | bytes 393224 | tf_op jit(solution)/shard_map/ppermute | solution.py:55
  62.0 6.8 %collective-permute-start.18 = (bf16[128,512]{1,0:T(8,128)(2,1)S(1)}, bf16[128,512]{1,0:T(8,128)(2,1)S(1)}, u32[]{:S(2)}, u32[]{:S(2)}) collective-permute-start(bf16[128,512]{1,0:T(8,128)(2,1)S(1)} %get-tuple-element.62), channel_id=1, source_target_pairs={{0,248},{8,0},{16,8},{24,16},{32,24},{40,32},{48,40},{56,48},{64,5... | collective-permute-start | bytes 393224 | tf_op jit(solution)/shard_map/ppermute | solution.py:55
  63.8 16.1 %collective-permute-start.19 = (bf16[8,256,256]{2,1,0:T(8,128)(2,1)S(1)}, bf16[8,256,256]{2,1,0:T(8,128)(2,1)S(1)}, u32[]{:S(2)}, u32[]{:S(2)}) collective-permute-start(bf16[8,256,256]{2,1,0:T(8,128)(2,1)S(1)} %get-tuple-element.73), channel_id=1, source_target_pairs={{0,8},{8,0},{16,24},{24,16},{32,40},{40,32},{48,56},{56,48},{64,72... | collective-permute-start | bytes 3145736 | tf_op jit(solution)/shard_map/ppermute | solution.py:50
  74.9 8.8 %collective-permute-start.21 = (bf16[256,512]{1,0:T(8,128)(2,1)S(1)}, bf16[256,512]{1,0:T(8,128)(2,1)S(1)}, u32[]{:S(2)}, u32[]{:S(2)}) collective-permute-start(bf16[256,512]{1,0:T(8,128)(2,1)S(1)} %get-tuple-element.77), channel_id=1, source_target_pairs={{0,1},{1,2},{2,3},{3,4},{4,5},{5,6},{6,7},{7,0},{8,15},{9,8},{10,9... | collective-permute-start | bytes 786440 | tf_op jit(solution)/shard_map/ppermute | solution.py:30
  77.4 10.0 %collective-permute-start.25 = (bf16[256,512]{1,0:T(8,128)(2,1)S(1)}, bf16[256,512]{1,0:T(8,128)(2,1)S(1)}, u32[]{:S(2)}, u32[]{:S(2)}) collective-permute-start(bf16[256,512]{1,0:T(8,128)(2,1)S(1)} %get-tuple-element.80), channel_id=1, source_target_pairs={{0,7},{1,0},{2,1},{3,2},{4,3},{5,4},{6,5},{7,6},{8,9},{9,10},{10,1... | collective-permute-start | bytes 786440 | tf_op jit(solution)/shard_map/ppermute | solution.py:30
  83.7 7.7 %collective-permute-start.22 = (bf16[256,512]{1,0:T(8,128)(2,1)S(1)}, bf16[256,512]{1,0:T(8,128)(2,1)S(1)}, u32[]{:S(2)}, u32[]{:S(2)}) collective-permute-start(bf16[256,512]{1,0:T(8,128)(2,1)S(1)} %add.69), channel_id=1, source_target_pairs={{0,1},{1,2},{2,3},{3,4},{4,5},{5,6},{6,7},{7,0},{8,15},{9,8},{10,9... | collective-permute-start | bytes 786440 | tf_op jit(solution)/shard_map/ppermute | solution.py:30
  83.8 16.4 %collective-permute-start.28 = (bf16[4,128,512]{2,1,0:T(8,128)(2,1)S(1)}, bf16[4,128,512]{2,1,0:T(8,128)(2,1)S(1)}, u32[]{:S(2)}, u32[]{:S(2)}) collective-permute-start(bf16[4,128,512]{2,1,0:T(8,128)(2,1)S(1)} %get-tuple-element.82), channel_id=1, source_target_pairs={{0,64},{8,24},{16,80},{24,40},{32,96},{40,56},{48,112},{56,8},{64,... | collective-permute-start | bytes 1572872 | tf_op jit(solution)/shard_map/ppermute | solution.py:46
  84.1 16.1 %collective-permute-start.29 = (bf16[4,128,512]{2,1,0:T(8,128)(2,1)S(1)}, bf16[4,128,512]{2,1,0:T(8,128)(2,1)S(1)}, u32[]{:S(2)}, u32[]{:S(2)}) collective-permute-start(bf16[4,128,512]{2,1,0:T(8,128)(2,1)S(1)} %get-tuple-element.83), channel_id=1, source_target_pairs={{0,128},{8,40},{16,144},{24,56},{32,160},{40,8},{48,176},{56,24},{... | collective-permute-start | bytes 1572872 | tf_op jit(solution)/shard_map/ppermute | solution.py:46
  85.6 15.5 %collective-permute-start.30 = (bf16[4,128,512]{2,1,0:T(8,128)(2,1)S(1)}, bf16[4,128,512]{2,1,0:T(8,128)(2,1)S(1)}, u32[]{:S(2)}, u32[]{:S(2)}) collective-permute-start(bf16[4,128,512]{2,1,0:T(8,128)(2,1)S(1)} %get-tuple-element.84), channel_id=1, source_target_pairs={{0,192},{8,56},{16,208},{24,8},{32,224},{40,24},{48,240},{56,40},{... | collective-permute-start | bytes 1572872 | tf_op jit(solution)/shard_map/ppermute | solution.py:46
  87.4 7.2 %collective-permute-start.26 = (bf16[256,512]{1,0:T(8,128)(2,1)S(1)}, bf16[256,512]{1,0:T(8,128)(2,1)S(1)}, u32[]{:S(2)}, u32[]{:S(2)}) collective-permute-start(bf16[256,512]{1,0:T(8,128)(2,1)S(1)} %add.72), channel_id=1, source_target_pairs={{0,7},{1,0},{2,1},{3,2},{4,3},{5,4},{6,5},{7,6},{8,9},{9,10},{10,1... | collective-permute-start | bytes 786440 | tf_op jit(solution)/shard_map/ppermute | solution.py:30
  91.4 8.7 %collective-permute-start.23 = (bf16[256,512]{1,0:T(8,128)(2,1)S(1)}, bf16[256,512]{1,0:T(8,128)(2,1)S(1)}, u32[]{:S(2)}, u32[]{:S(2)}) collective-permute-start(bf16[256,512]{1,0:T(8,128)(2,1)S(1)} %add.70), channel_id=1, source_target_pairs={{0,1},{1,2},{2,3},{3,4},{4,5},{5,6},{6,7},{7,0},{8,15},{9,8},{10,9... | collective-permute-start | bytes 786440 | tf_op jit(solution)/shard_map/ppermute | solution.py:30
  101.3 12.7 %collective-permute-start.31 = (bf16[128,512]{1,0:T(8,128)(2,1)S(1)}, bf16[128,512]{1,0:T(8,128)(2,1)S(1)}, u32[]{:S(2)}, u32[]{:S(2)}) collective-permute-start(bf16[128,512]{1,0:T(8,128)(2,1)S(1)} %get-tuple-element.86), channel_id=1, source_target_pairs={{0,16},{8,72},{16,32},{24,88},{32,48},{40,104},{48,0},{56,120},{64... | collective-permute-start | bytes 393224 | tf_op jit(solution)/shard_map/ppermute | solution.py:38
  106.4 7.6 %collective-permute-start.32 = (bf16[128,512]{1,0:T(8,128)(2,1)S(1)}, bf16[128,512]{1,0:T(8,128)(2,1)S(1)}, u32[]{:S(2)}, u32[]{:S(2)}) collective-permute-start(bf16[128,512]{1,0:T(8,128)(2,1)S(1)} %get-tuple-element.87), channel_id=1, source_target_pairs={{0,32},{8,136},{16,48},{24,152},{32,0},{40,168},{48,16},{56,184},{... | collective-permute-start | bytes 393224 | tf_op jit(solution)/shard_map/ppermute | solution.py:38
  111.2 6.7 %collective-permute-start.27 = (bf16[256,512]{1,0:T(8,128)(2,1)S(1)}, bf16[256,512]{1,0:T(8,128)(2,1)S(1)}, u32[]{:S(2)}, u32[]{:S(2)}) collective-permute-start(bf16[256,512]{1,0:T(8,128)(2,1)S(1)} %add.73), channel_id=1, source_target_pairs={{0,7},{1,0},{2,1},{3,2},{4,3},{5,4},{6,5},{7,6},{8,9},{9,10},{10,1... | collective-permute-start | bytes 786440 | tf_op jit(solution)/shard_map/ppermute | solution.py:30
  114.0 7.6 %collective-permute-start.24 = (bf16[256,512]{1,0:T(8,128)(2,1)S(1)}, bf16[256,512]{1,0:T(8,128)(2,1)S(1)}, u32[]{:S(2)}, u32[]{:S(2)}) collective-permute-start(bf16[256,512]{1,0:T(8,128)(2,1)S(1)} %add.71), channel_id=1, source_target_pairs={{0,1},{1,2},{2,3},{3,4},{4,5},{5,6},{6,7},{7,0},{8,15},{9,8},{10,9... | collective-permute-start | bytes 786440 | tf_op jit(solution)/shard_map/ppermute | solution.py:30
  (5 other events, 56.0 us)

commit v2 on v1

--- a/solution.py
+++ b/solution.py
@@ -182,37 +182,61 @@
     copy.wait()
 
 
-def project_piece(ids, k, piece, w, mine_ref, cross_ref):
+def split_piece(ids, k, piece, mine_ref, cross_ref):
     for core, out in ((ids[2], mine_ref), (1 - ids[2], cross_ref)):
         for xp in range(2):
             lanes = pl.ds(pl.multiple_of(xp * 256 + core * 128, 128), 128)
             out[k, :, xp * 128 : xp * 128 + 128] = piece[:, lanes]
+
+
+def piece_term(ids, k, piece, w):
     return jnp.dot(piece[...], w[place_of(ids, k)].reshape(512, 512), preferred_element_type=F32)
 
 
-EARLY, LATE = (0, 1, 7, 2, 6), (3, 5, 4)
-
-
-def early_kernel(ids, *refs):
-    pieces, own, other, (acc, w, mine_ref, cross_ref, tok, sems, tok_sems) = refs[0:5], refs[5:9], refs[9:13], refs[13:]
+FIRST, NEXT, LATE = (0, 1, 7, 2, 6), (3, 5), 4
+
+
+def split_kernel(ids, *refs):
+    pieces, (tok, mine_ref, cross_ref) = refs[0:5], refs[5:]
+    for n, k in enumerate(FIRST):
+        tok[n] = pieces[n][...]
+        split_piece(ids, k, pieces[n], mine_ref, cross_ref)
+
+
+def split_tokens(ids, pieces):
+    return pl.pallas_call(
+        split_kernel,
+        in_specs=[SMEM] + [VMEM] * 5,
+        out_specs=[VMEM] * 3,
+        out_shape=[jax.ShapeDtypeStruct((n, 256, lanes), BF) for n, lanes in ((5, 512), (NZ, 256), (NZ + 2, 256))],
+        compiler_params=pltpu.CompilerParams(vmem_limit_bytes=4 << 20),
+        cost_estimate=pl.CostEstimate(flops=1 << 20, bytes_accessed=4 << 20, transcendentals=0),
+        name="split_tokens",
+    )(ids, *pieces)
+
+
+def early_kernel(ids, tok, q3, p3, *refs):
+    own, other, (_, _, acc, w, mine_ref, cross_ref, more, sems, tok_sems) = refs[0:4], refs[4:8], refs[8:]
     load_weight(ids, own, other, w, sems, start)
-    arrive = [pltpu.make_async_copy(piece, tok.at[n], tok_sems.at[n]) for n, piece in enumerate(pieces)]
+    arrive = [pltpu.make_async_copy(piece, more.at[n], tok_sems.at[n]) for n, piece in enumerate((q3, p3))]
     for copy in arrive:
         copy.start()
+    for copy in arrive:
+        copy.wait()
+    for n, k in enumerate(NEXT):
+        split_piece(ids, k, more.at[n], mine_ref, cross_ref)
     load_weight(ids, own, other, w, sems, wait)
     total = None
-    for n, k in enumerate(EARLY):
-        arrive[n].wait()
-        term = project_piece(ids, k, tok.at[n], w, mine_ref, cross_ref)
+    for k, piece in zip(FIRST + NEXT, [tok.at[n] for n in range(5)] + [more.at[0], more.at[1]]):
+        term = piece_term(ids, k, piece, w)
         total = term if total is None else total + term
     acc[...] = total
 
 
 def late_kernel(ids, *refs):
-    pieces, (acc, w, _, _, dg_ref, p_ref, tail_ref, head_ref, mine_ref, cross_ref) = refs[0:3], refs[3:]
-    total = acc[...]
-    for k, piece in zip(LATE, pieces):
-        total += project_piece(ids, k, piece, w, mine_ref, cross_ref)
+    piece, acc, w, _, _, dg_ref, p_ref, tail_ref, head_ref, mine_ref, cross_ref = refs
+    total = acc[...] + piece_term(ids, LATE, piece, w)
+    split_piece(ids, LATE, piece, mine_ref, cross_ref)
     p = total.astype(BF)
     p_ref[...] = p
     tail_ref[...] = p[128:256]
@@ -220,80 +244,65 @@
     head_ref[...] = (dg_ref[0:128].astype(F32) * (top * jax.nn.sigmoid(top))).astype(BF)
 
 
-def project_early(ids, pieces, blocks):
-    part_of = jax.ShapeDtypeStruct((NZ, 256, 256), BF)
+def project_early(ids, tok, pieces, blocks, mine, cross):
     return pl.pallas_call(
         early_kernel,
-        in_specs=[SMEM] + [HBM] * 13,
+        in_specs=[SMEM, VMEM] + [HBM] * 10 + [VMEM] * 2,
         out_specs=[VMEM] * 4,
         out_shape=[
-            jax.ShapeDtypeStruct((256, 512), F32), jax.ShapeDtypeStruct((NZ, 2, 2, 128, 512), BF), part_of, part_of,
+            jax.ShapeDtypeStruct((256, 512), F32),
+            jax.ShapeDtypeStruct((NZ, 2, 2, 128, 512), BF),
+            jax.ShapeDtypeStruct(mine.shape, BF),
+            jax.ShapeDtypeStruct(cross.shape, BF),
         ],
+        input_output_aliases={12: 2, 13: 3},
         scratch_shapes=[
-            pltpu.VMEM((5, 256, 512), BF),
+            pltpu.VMEM((2, 256, 512), BF),
             pltpu.SemaphoreType.DMA((24,)),
-            pltpu.SemaphoreType.DMA((5,)),
+            pltpu.SemaphoreType.DMA((2,)),
         ],
-        compiler_params=pltpu.CompilerParams(vmem_limit_bytes=8 << 20),
+        compiler_params=pltpu.CompilerParams(vmem_limit_bytes=6 << 20),
         cost_estimate=pl.CostEstimate(flops=1 << 32, bytes_accessed=8 << 20, transcendentals=0),
         name="project_early",
-    )(ids, *pieces, *blocks)
-
-
-def project_late(ids, pieces, early, d_gated):
-    half, part_of = jax.ShapeDtypeStruct((128, 512), BF), jax.ShapeDtypeStruct((NZ, 256, 256), BF)
+    )(ids, tok, *pieces, *blocks, mine, cross)
+
+
+def project_late(ids, piece, early, d_gated):
+    half = jax.ShapeDtypeStruct((128, 512), BF)
+    part_of, more = jax.ShapeDtypeStruct((NZ, 256, 256), BF), jax.ShapeDtypeStruct((NZ + 2, 256, 256), BF)
     return pl.pallas_call(
         late_kernel,
-        in_specs=[SMEM] + [VMEM] * 8,
+        in_specs=[SMEM] + [VMEM] * 6,
         out_specs=[VMEM] * 5,
-        out_shape=[jax.ShapeDtypeStruct((256, 512), BF), half, half, part_of, part_of],
-        input_output_aliases={6: 3, 7: 4},
+        out_shape=[jax.ShapeDtypeStruct((256, 512), BF), half, half, part_of, more],
+        input_output_aliases={4: 3, 5: 4},
         compiler_params=pltpu.CompilerParams(vmem_limit_bytes=6 << 20),
-        cost_estimate=pl.CostEstimate(flops=2 * 256 * 1536 * 512, bytes_accessed=4 << 20, transcendentals=0),
+        cost_estimate=pl.CostEstimate(flops=2 * 256 * 512 * 512, bytes_accessed=4 << 20, transcendentals=0),
         name="project_late",
-    )(ids, *pieces, *early, d_gated)
-
-
-def mix(ext, live_ref, taps_ref, even, odd, mask, acc, reverse):
+    )(ids, piece, *early, d_gated)
+
+
+def mix(ext, live_ref, taps_ref, even, odd, acc, reverse):
     acc[...] = jnp.zeros_like(acc)
     rows = ext.shape[0]
+    zero, one = jnp.zeros((), BF), jnp.ones((), BF)
 
     def shift(b):
-        for k in range(16):
-            limit = (b + (8 * k - 1)).astype(F32).astype(BF)
-            for u in range(8):
-                at = slice(TILE * u, TILE * u + TILE)
-                mask[k, at] = jnp.clip(live_ref[at] - limit, jnp.zeros((), BF), jnp.ones((), BF))
-
-        def strip(s):
-            lanes = pl.ds(pl.multiple_of(s * 256, 256), 256)
-            if reverse:
-                r = pltpu.roll(ext[:, lanes], lax.rem(rows - b, rows), 0)
-                even[...] = r.astype(BF)
-                odd[...] = jnp.concatenate([r[8:], r[:8]], 0).astype(BF)
-            else:
-                r = pltpu.roll(ext[:, lanes], b, 0)
-                even[...] = r.astype(BF)
-                odd[...] = jnp.concatenate([r[-8:], r[:-8]], 0).astype(BF)
-            for h, moved in ((0, even), (1, odd)):
-                weights = [taps_ref[b, 2 * a + h, :, lanes] for a in range(8)]
-                sums = [None] * 8
-                count = [0] * 8
-                for v in range(16):
-                    source = moved[TILE * v : TILE * v + TILE]
-                    for a in range(8):
-                        u = v - a if reverse else v - 8 + a
-                        if not 0 <= u < 8:
-                            continue
-                        at = slice(TILE * u, TILE * u + TILE)
-                        m = mask[2 * a + h, at]
-                        term = source * weights[a] * jnp.concatenate([m, m], 1)
-                        sums[u] = term if sums[u] is None else sums[u] + term
-                        count[u] += 1
-                        if count[u] == 8:
-                            acc[at, lanes] += sums[u].astype(F32)
-
-        loop(2, strip)
+        r = ext[...]
+        even[...] = r.astype(BF)
+        odd[...] = jnp.concatenate([r[8:], r[:8]] if reverse else [r[-8:], r[:-8]], 0).astype(BF)
+        ext[...] = pltpu.roll(r, rows - 1 if reverse else 1, 0)
+        for u in range(8):
+            at = slice(TILE * u, TILE * u + TILE)
+            live = live_ref[at] - b.astype(F32).astype(BF)
+            total = None
+            for k in range(16):
+                v = u + k // 2 if reverse else u + 8 - k // 2
+                source = (odd if k % 2 else even)[TILE * v : TILE * v + TILE]
+                m = jnp.minimum(jnp.maximum(live - jnp.array(8 * k - 1, BF), zero), one)
+                term = source * taps_ref[b, k] * jnp.concatenate([m] * 4, 1)
+                total = term if total is None else total + term
+            acc[at] += total.astype(F32)
 
     loop(8, shift)
 
@@ -307,42 +316,44 @@
 LOW, HIGH = slice(0, 128), slice(128, 256)
 
 
-def ahead_inside_kernel(p_ref, dg_ref, taps_ref, live_ref, gated_ref, dgate_ref, ext, even, odd, mask, acc):
+def ahead_inside_kernel(p_ref, dg_ref, taps_ref, live_ref, gated_ref, dgate_ref, ext, even, odd, acc):
     ext[...] = p_ref[...].astype(F32)
-    mix(ext, live_ref.at[HIGH], taps_ref, even, odd, mask, acc, False)
+    mix(ext, live_ref.at[HIGH], taps_ref, even, odd, acc, False)
     p, up = p_ref[HIGH].astype(F32), dg_ref[HIGH].astype(F32)
     gated_ref[...], dgate_ref[...], _ = gates(p, up, acc[...])
 
 
-def back_inside_kernel(p_ref, dg_ref, taps_ref, live_ref, part_ref, dconv_ref, ext, even, odd, mask, acc):
+def back_inside_kernel(p_ref, dg_ref, taps_ref, live_ref, part_ref, dconv_ref, ext, even, odd, acc):
     p = p_ref[...].astype(F32)
     ext[...] = dg_ref[...].astype(F32) * (p * jax.nn.sigmoid(p))
     dconv_ref[...] = ext[HIGH]
-    mix(ext, live_ref.at[LOW], taps_ref, even, odd, mask, acc, True)
+    mix(ext, live_ref.at[LOW], taps_ref, even, odd, acc, True)
     part_ref[...] = acc[...]
 
 
-def ahead_edge_kernel(p_ref, dg_ref, taps_ref, live_ref, tail_ref, gated_hi, part_ref, gated_ref, low_ref, ext, even, odd, mask, acc):
+def ahead_edge_kernel(p_ref, dg_ref, taps_ref, live_ref, tail_ref, gated_hi, part_ref, gated_ref, low_ref, ext, even, odd, acc):
     p, up = p_ref[LOW].astype(F32), dg_ref[LOW].astype(F32)
     ext[LOW] = tail_ref[...].astype(F32)
     ext[HIGH] = p
-    mix(ext, live_ref.at[LOW], taps_ref, even, odd, mask, acc, False)
+    mix(ext, live_ref.at[LOW], taps_ref, even, odd, acc, False)
     gated_ref[LOW], d_gate, _ = gates(p, up, acc[...])
     gated_ref[HIGH] = gated_hi[...]
     low_ref[...] = (part_ref[...] + d_gate).astype(BF)
 
 
 def back_edge_kernel(
-    dconv_ref, head_ref, taps_ref, live_ref, low_ref, dgate_ref, ids, w_ref, dproj_ref, far_ref, w,
-    ext, even, odd, mask, acc, sem,
+    dconv_ref, head_ref, taps_ref, live_ref, low_ref, dgate_ref, ids, w_ref, _, dproj_ref, far_ref, w, cross_ref,
+    ext, even, odd, acc, sem,
 ):
     load = pltpu.make_async_copy(w_ref, w, sem)
     load.start()
     ext[LOW] = dconv_ref[...]
     ext[HIGH] = head_ref[...].astype(F32)
-    mix(ext, live_ref.at[HIGH], taps_ref, even, odd, mask, acc, True)
+    mix(ext, live_ref.at[HIGH], taps_ref, even, odd, acc, True)
     dproj_ref[LOW] = low_ref[...]
     dproj_ref[HIGH] = (acc[...] + dgate_ref[...]).astype(BF)
+    cross_ref[NZ] = dproj_ref[:, 0:256]
+    cross_ref[NZ + 1] = dproj_ref[:, 256:512]
     load.wait()
     far_ref[...] = back_term(dproj_ref[...], w[place_of(ids, 4)].reshape(512, 512))
 
@@ -351,7 +362,7 @@
     return lax.dot_general(d, block, (((1,), (1,)), ((), ())), preferred_element_type=F32).astype(BF)
 
 
-def mix_call(kernel, name, shapes, *operands, specs=None, scratch=()):
+def mix_call(kernel, name, shapes, *operands, specs=None, scratch=(), aliases={}):
     return pl.pallas_call(
         kernel,
         in_specs=specs or [VMEM] * len(operands),
@@ -359,12 +370,12 @@
         out_shape=[jax.ShapeDtypeStruct(shape, kind) for shape, kind in shapes],
         scratch_shapes=[
             pltpu.VMEM((256, 512), F32),
-            pltpu.VMEM((256, 256), BF),
-            pltpu.VMEM((256, 256), BF),
-            pltpu.VMEM((16, 128, LANES), BF),
+            pltpu.VMEM((256, 512), BF),
+            pltpu.VMEM((256, 512), BF),
             pltpu.VMEM((128, 512), F32),
             *scratch,
         ],
+        input_output_aliases=aliases,
         compiler_params=pltpu.CompilerParams(vmem_limit_bytes=8 << 20),
         cost_estimate=pl.CostEstimate(flops=1 << 32, bytes_accessed=4 << 20, transcendentals=0),
         name=name,
@@ -381,16 +392,15 @@
     part, dconv_hi = mix_call(
         back_inside_kernel, "back_inside", [(half, F32), (half, F32)], p, d_gated, taps, ahead
     )
-    theirs = to_other_core(after(cross, part))
     gated, low = mix_call(
         ahead_edge_kernel, "ahead_edge", [(whole, BF), (half, BF)], p, d_gated, taps, back, tail, gated_hi, part
     )
-    d_proj, far, w = mix_call(
-        back_edge_kernel, "back_edge", [(whole, BF), (whole, BF), (w.shape, BF)],
-        dconv_hi, head, taps, ahead, low, dgate_hi, ids, w,
-        specs=[VMEM] * 6 + [SMEM, HBM], scratch=[pltpu.SemaphoreType.DMA],
+    d_proj, far, w, cross = mix_call(
+        back_edge_kernel, "back_edge", [(whole, BF), (whole, BF), (w.shape, BF), (cross.shape, BF)],
+        dconv_hi, head, taps, ahead, low, dgate_hi, ids, w, cross,
+        specs=[VMEM] * 6 + [SMEM, HBM, VMEM], scratch=[pltpu.SemaphoreType.DMA], aliases={8: 3},
     )
-    return gated, d_proj, far, w, theirs
+    return gated, d_proj, far, w, cross
 
 
 NEAR = (3, 5, 2, 6, 1, 7, 0)
@@ -425,13 +435,15 @@
         out_specs=VMEM,
         out_shape=jax.ShapeDtypeStruct(a.shape, BF),
         compiler_params=pltpu.CompilerParams(vmem_limit_bytes=2 << 20),
-        cost_estimate=pl.CostEstimate(flops=1 << 32, bytes_accessed=1 << 20, transcendentals=0),
+        cost_estimate=pl.CostEstimate(flops=1 << 34, bytes_accessed=1 << 20, transcendentals=0),
         name="add_three",
     )(a, b, c)
 
 
-def grad_kernel(ids, mine, theirs, d_mine, d_theirs, *refs):
-    outs, out = refs[:4], refs[4]
+def grad_kernel(ids, mine, theirs, d_mine, *refs):
+    outs, out, d_theirs = refs[:4], refs[4], refs[5]
+    d_theirs[:, 0:256] = theirs[NZ]
+    d_theirs[:, 256:512] = theirs[NZ + 1]
     me = ids[2]
     dims = (((0,), (0,)), ((), ()))
     for k in range(NZ):
@@ -447,25 +459,25 @@
         outs[k][...] = out[k]
 
 
-def weight_terms(ids, mine, theirs, d_mine, d_theirs):
+def weight_terms(ids, mine, theirs, d_mine):
     return pl.pallas_call(
         grad_kernel,
-        in_specs=[SMEM] + [VMEM] * 4,
+        in_specs=[SMEM] + [VMEM] * 3,
         out_specs=[VMEM] * 4,
         out_shape=[jax.ShapeDtypeStruct((4, 128, 512), BF)] * 4,
-        scratch_shapes=[pltpu.VMEM((4, 4, 128, 512), BF)],
+        scratch_shapes=[pltpu.VMEM((4, 4, 128, 512), BF), pltpu.VMEM((256, 512), BF)],
         compiler_params=pltpu.CompilerParams(vmem_limit_bytes=6 << 20),
         cost_estimate=pl.CostEstimate(flops=2 * 512 * 2048 * 512, bytes_accessed=5 << 20, transcendentals=0),
         name="weight_terms",
-    )(ids, mine, theirs, d_mine, d_theirs)
-
-
-def sum_up(ids, d_proj, far, weight, mine, theirs):
+    )(ids, mine, theirs, d_mine)
+
+
+def sum_up(ids, d_proj, far, weight, mine, cross):
     p = around_z(far, 1)
-    d_theirs = to_other_core(d_proj)
+    theirs = to_other_core(cross)
     p3, q3, p2, q2, p1, q1, own = near_terms(ids, d_proj, weight)
     q = around_z(q3, -1)
-    g = weight_terms(ids, mine, theirs, d_proj, after(d_theirs, own))
+    g = weight_terms(ids, mine, after(theirs, own), d_proj)
     p = around_z(add(after(p3, g[0]), p), 1)
     s = [g[0]] + [wide(g[k], k) for k in (1, 2, 3)]
     q = around_z(add(q2, q), -1)
@@ -477,7 +489,7 @@
     n = sum_four([after(s[0], p_last, q_last)] + s[1:])
     n = [n[0]] + [narrow(n[k], k) for k in (1, 2, 3)]
     d_tokens = add_three(own, p, q)
-    return d_tokens, sum(v.astype(F32) for v in n)
+    return d_tokens, sum(v.astype(F32) for v in after(n, d_tokens))
 
 
 def body(tokens, contig_lengths, w_in, conv_filter, d_gated):
@@ -493,21 +505,22 @@
     first = jnp.where(core == 0, x, y).astype(jnp.int32).reshape(1)
     row_block = stack(first, [w_in] + w)
     own = [row_block] + [wide(row_block, 4 - k) for k in (1, 2, 3)]
-    other = [to_other_core(block) for block in own]
-    p2, q2 = around_z(after(p1, row_block), 1), around_z(after(q1, row_block), -1)
+    p2, q2 = around_z(p1, 1), around_z(q1, -1)
     conv_filter, contig_lengths = after((conv_filter, contig_lengths), q1)
     back, ahead = live_taps(contig_lengths, row * rows, rows)
     taps = conv_filter.astype(BF).reshape(16, 8, 1, 512).transpose(1, 0, 2, 3)
     taps = jnp.broadcast_to(taps, (8, 16, TILE, 512))
     p3, q3 = around_z(p2, 1), around_z(q2, -1)
-    p4 = around_z(after(p3, back, ahead, taps), 1)
-    early = project_early(ids, [tokens, q1, p1, q2, p2], own + other)
+    tok, mine, cross = split_tokens(ids, [tokens, q1, p1, q2, p2])
+    other = [to_other_core(block) for block in after(own, p3, q3, back, ahead, taps, tok)]
+    p4 = around_z(p3, 1)
+    early = project_early(ids, tok, [q3, p3], own + other, mine, cross)
     weight = early[1]
-    projected, tail, head, mine, cross = project_late(ids, [q3, p3, p4], early, d_gated)
-    gated, d_proj, far, weight, theirs = conv(
+    projected, tail, head, mine, cross = project_late(ids, p4, early, d_gated)
+    gated, d_proj, far, weight, cross = conv(
         ids, projected, tail, head, d_gated, taps, back, ahead, weight, cross
     )
-    d_tokens, grad = sum_up(ids, d_proj, far, weight, mine, theirs)
+    d_tokens, grad = sum_up(ids, d_proj, far, weight, mine, cross)
     return gated, d_tokens, grad * (1.0 / math.sqrt(seq_total))
 
 

time: 123 us -> 107 us (0.87)
  the two profiles are of different devices: /device:TPU:4 before, /device:TPU:96 now
where the time goes in v2:
time: 107 us; the launch traced here: 106 us
  starting transfers between devices  42.8 us (40%)
  waiting for transfers between devices  29.9 us (28%)
  Pallas kernels  27.9 us (26%)
  local copies, waits for them, and re-layouts  2.08 us (2%)
  other arithmetic  1.85 us (2%)
    ppermute x14, starting transfers between devices, around_z(): return lax.ppermute(value, ('row', 'col'), pairs)  20.7 us
    pallas_call x4, Pallas kernels, mix_call(): pl.pallas_call(kernel, in_specs=specs or [VMEM] * len(operands), out_spec...  16.1 us
    ppermute x14, waiting for transfers between devices, around_z(): return lax.ppermute(value, ('row', 'col'), pairs)  13.5 us
    ppermute x6, waiting for transfers between devices, wide(): return lax.ppermute(value, 'row', pairs)  10 us
    ppermute x6, starting transfers between devices, wide(): return lax.ppermute(value, 'row', pairs)  7.93 us
    ppermute x6, starting transfers between devices, narrow(): return lax.ppermute(value, 'row', pairs)  7.75 us
    ppermute x2, starting transfers between devices, next_row(): lax.ppermute(value, 'row', [(r, (r + steps) % count) for r in range(count)])  5.22 us
    ppermute x6, waiting for transfers between devices, narrow(): return lax.ppermute(value, 'row', pairs)  5.15 us
  transfers between devices with their start and end apart: 33, of which 15 were waited for; matrix products, arithmetic and copies ran while one was open for 2% of the time, Pallas kernels for 18%

profile of v2, /device:TPU:96, one launch (start us, length us, event | category | flops | bytes accessed | tf_op | source)
XLA Modules:
  0.0 105.5 jit_solution(11329166403549735796)
XLA Ops:
  0.8 3.1 %collective-permute-start = (bf16[256,512]{1,0:T(8,128)(2,1)}, bf16[256,512]{1,0:T(8,128)(2,1)S(1)}, u32[]{:S(2)}, u32[]{:S(2)}) collective-permute-start(bf16[256,512]{1,0:T(8,128)(2,1)} %refs_0_.2), channel_id=1, source_target_pairs={{0,1},{1,2},{2,3},{3,4},{4,5},{5,6},{6,7},{7,0},{8,15},{9,8},{10,9... | collective-permute-start | bytes 786440 | tf_op jit(solution)/shard_map/ppermute | solution.py:30
  4.0 2.8 %collective-permute-start.7 = (bf16[128,512]{1,0:T(8,128)(2,1)}, bf16[128,512]{1,0:T(8,128)(2,1)S(1)}, u32[]{:S(2)}, u32[]{:S(2)}) collective-permute-start(bf16[128,512]{1,0:T(8,128)(2,1)} %refs_0_.3), channel_id=1, source_target_pairs={{0,48},{8,200},{16,0},{24,216},{32,16},{40,232},{48,32},{56,248},{... | collective-permute-start | bytes 393224 | tf_op jit(solution)/shard_map/ppermute | solution.py:38
  8.4 1.1 %collective-permute-done.4.refs_1_ = bf16[256,512]{1,0:T(8,128)(2,1)S(1)} collective-permute-done((bf16[256,512]{1,0:T(8,128)(2,1)}, bf16[256,512]{1,0:T(8,128)(2,1)S(1)}, u32[]{:S(2)}, u32[]{:S(2)}) %collective-permute-start.4) | collective-permute-done | bytes 262176 | tf_op jit(solution)/shard_map/ppermute | solution.py:30
  9.7 3.6 %collective-permute-start.1 = (bf16[256,512]{1,0:T(8,128)(2,1)S(1)}, bf16[256,512]{1,0:T(8,128)(2,1)S(1)}, u32[]{:S(2)}, u32[]{:S(2)}) collective-permute-start(bf16[256,512]{1,0:T(8,128)(2,1)S(1)} %collective-permute-done.refs_2_), channel_id=1, source_target_pairs={{0,1},{1,2},{2,3},{3,4},{4,5},{5,6},{6,7},{7,0},{8,15},{9,8},{10,9... | collective-permute-start | bytes 786440 | tf_op jit(solution)/shard_map/ppermute | solution.py:30
  13.5 1.3 %collective-permute-done.9.refs_3_ = bf16[128,512]{1,0:T(8,128)(2,1)S(1)} collective-permute-done((bf16[128,512]{1,0:T(8,128)(2,1)}, bf16[128,512]{1,0:T(8,128)(2,1)S(1)}, u32[]{:S(2)}, u32[]{:S(2)}) %collective-permute-start.9) | collective-permute-done | bytes 131104 | tf_op jit(solution)/shard_map/ppermute | solution.py:38
  14.8 0.9 copy-done.2
  15.7 3.1 %collective-permute-start.10 = (bf16[4,128,512]{2,1,0:T(8,128)(2,1)S(1)}, bf16[4,128,512]{2,1,0:T(8,128)(2,1)S(1)}, u32[]{:S(2)}, u32[]{:S(2)}) collective-permute-start(bf16[4,128,512]{2,1,0:T(8,128)(2,1)S(1)} %stack.21.refs_0_), channel_id=1, source_target_pairs={{0,192},{8,56},{16,208},{24,8},{32,224},{40,24},{48,240},{56,40},{... | collective-permute-start | bytes 1572872 | tf_op jit(solution)/shard_map/ppermute | solution.py:46
  19.5 1.0 collective-permute-start.12
  22.1 2.0 %collective-permute-start.2 = (bf16[256,512]{1,0:T(8,128)(2,1)S(1)}, bf16[256,512]{1,0:T(8,128)(2,1)S(1)}, u32[]{:S(2)}, u32[]{:S(2)}) collective-permute-start(bf16[256,512]{1,0:T(8,128)(2,1)S(1)} %collective-permute-done.1.refs_4_), channel_id=1, source_target_pairs={{0,1},{1,2},{2,3},{3,4},{4,5},{5,6},{6,7},{7,0},{8,15},{9,8},{10,9... | collective-permute-start | bytes 786440 | tf_op jit(solution)/shard_map/ppermute | solution.py:30
  25.2 5.9 %collective-permute-done.10.refs_1_ = bf16[4,128,512]{2,1,0:T(8,128)(2,1)S(1)} collective-permute-done((bf16[4,128,512]{2,1,0:T(8,128)(2,1)S(1)}, bf16[4,128,512]{2,1,0:T(8,128)(2,1)S(1)}, u32[]{:S(2)}, u32[]{:S(2)}) %collective-permute-start.10) | collective-permute-done | bytes 524320 | tf_op jit(solution)/shard_map/ppermute | solution.py:46
  31.2 4.1 %collective-permute-done.12.refs_3_ = bf16[4,128,512]{2,1,0:T(8,128)(2,1)} collective-permute-done((bf16[4,128,512]{2,1,0:T(8,128)(2,1)S(1)}, bf16[4,128,512]{2,1,0:T(8,128)(2,1)}, u32[]{:S(2)}, u32[]{:S(2)}) %collective-permute-start.12) | collective-permute-done | bytes 524320 | tf_op jit(solution)/shard_map/ppermute | solution.py:46
  36.8 1.9 %collective-permute-start.3 = (bf16[256,512]{1,0:T(8,128)(2,1)S(1)}, bf16[256,512]{1,0:T(8,128)(2,1)S(1)}, u32[]{:S(2)}, u32[]{:S(2)}) collective-permute-start(bf16[256,512]{1,0:T(8,128)(2,1)S(1)} %collective-permute-done.2.p3), channel_id=1, source_target_pairs={{0,1},{1,2},{2,3},{3,4},{4,5},{5,6},{6,7},{7,0},{8,15},{9,8},{10,9... | collective-permute-start | bytes 786440 | tf_op jit(solution)/shard_map/ppermute | solution.py:30
  39.9 5.0 %project_early.1 = (f32[256,512]{1,0:T(8,128)S(1)}, bf16[8,2,2,128,512]{4,3,2,1,0:T(8,128)(2,1)S(1)}, bf16[8,256,256]{2,1,0:T(8,128)(2,1)S(1)}, bf16[10,256,256]{2,1,0:T(8,128)(2,1)S(1)}) custom-call(s32[4]{0:T(128)S(1)} %pad_add_fusion.ids, bf16[5,256,512]{2,1,0:T(8,128)(2,1)S(1)} %get-tuple-element.54.tok, ...), custom_call_target="tpu_custom_call", output_to_operand_aliasing={{2}: (12, {}), {3}: (13, {})} | custom-call | flops 4294967296 | bytes 8388608 | tf_op jit(solution)/shard_map/project_early/pallas_call | solution.py:248
  44.9 0.9 project_late.1
  45.8 3.6 %ahead_inside.1 = (bf16[128,512]{1,0:T(8,128)(2,1)S(1)}, f32[128,512]{1,0:T(8,128)S(1)}) custom-call(bf16[256,512]{1,0:T(8,128)(2,1)S(1)} %get-tuple-element.67.p_ref, bf16[256,512]{1,0:T(8,128)(2,1)S(1)} %copy-done.1, bf16[8,16,16,512]{3,2,1,0:T(8,128)(2,1)S(1)} %broadcast_in_dim.46.taps_ref, bf16[256,128]{1,0:T(8,128)(2,1)S(1)} %broadcast_in_dim.42.live_ref), custom_call_target="tpu_custom_call" | custom-call | flops 4294967296 | bytes 4194304 | tf_op jit(solution)/shard_map/ahead_inside/pallas_call | solution.py:366
  50.0 3.6 %back_inside.1 = (f32[128,512]{1,0:T(8,128)S(1)}, f32[128,512]{1,0:T(8,128)S(1)}) custom-call(bf16[256,512]{1,0:T(8,128)(2,1)S(1)} %get-tuple-element.67.p_ref, bf16[256,512]{1,0:T(8,128)(2,1)S(1)} %copy-done.1, bf16[8,16,16,512]{3,2,1,0:T(8,128)(2,1)S(1)} %broadcast_in_dim.46.taps_ref, bf16[256,128]{1,0:T(8,128)(2,1)S(1)} %broadcast_in_dim.44.live_ref), custom_call_target="tpu_custom_call" | custom-call | flops 4294967296 | bytes 4194304 | tf_op jit(solution)/shard_map/back_inside/pallas_call | solution.py:366
  53.6 4.7 %collective-permute-start.18 = (bf16[128,512]{1,0:T(8,128)(2,1)S(1)}, bf16[128,512]{1,0:T(8,128)(2,1)S(1)}, u32[]{:S(2)}, u32[]{:S(2)}) collective-permute-start(bf16[128,512]{1,0:T(8,128)(2,1)S(1)} %get-tuple-element.74), channel_id=1, source_target_pairs={{0,248},{8,0},{16,8},{24,16},{32,24},{40,32},{48,40},{56,48},{64,5... | collective-permute-start | bytes 393224 | tf_op jit(solution)/shard_map/ppermute | solution.py:55
  58.3 4.3 %ahead_edge.1 = (bf16[256,512]{1,0:T(8,128)(2,1)}, bf16[128,512]{1,0:T(8,128)(2,1)S(1)}) custom-call(bf16[256,512]{1,0:T(8,128)(2,1)S(1)} %get-tuple-element.67.p_ref, bf16[256,512]{1,0:T(8,128)(2,1)S(1)} %copy-done.1, bf16[8,16,16,512]{3,2,1,0:T(8,128)(2,1)S(1)} %broadcast_in_dim.46.taps_ref, bf16[256,128]{1,0:T(8,128)(2,1)S(1)} %broadcast_in_dim.42.live_ref, ...), custom_call_target="tpu_custom_call" | custom-call | flops 4294967296 | bytes 4194304 | tf_op jit(solution)/shard_map/ahead_edge/pallas_call | solution.py:366
  62.5 4.7 %back_edge.1 = (bf16[256,512]{1,0:T(8,128)(2,1)S(1)}, bf16[256,512]{1,0:T(8,128)(2,1)S(1)}, bf16[8,2,2,128,512]{4,3,2,1,0:T(8,128)(2,1)S(1)}, bf16[10,256,256]{2,1,0:T(8,128)(2,1)S(1)}) custom-call(f32[128,512]{1,0:T(8,128)S(1)} %get-tuple-element.72.dconv_ref, ...), custom_call_target="tpu_custom_call", output_to_operand_aliasing={{3}: (8, {})} | custom-call | flops 4294967296 | bytes 4194304 | tf_op jit(solution)/shard_map/back_edge/pallas_call | solution.py:366
  67.3 2.0 %collective-permute-start.20 = (bf16[256,512]{1,0:T(8,128)(2,1)S(1)}, bf16[256,512]{1,0:T(8,128)(2,1)S(1)}, u32[]{:S(2)}, u32[]{:S(2)}) collective-permute-start(bf16[256,512]{1,0:T(8,128)(2,1)S(1)} %get-tuple-element.89), channel_id=1, source_target_pairs={{0,1},{1,2},{2,3},{3,4},{4,5},{5,6},{6,7},{7,0},{8,15},{9,8},{10,9... | collective-permute-start | bytes 786440 | tf_op jit(solution)/shard_map/ppermute | solution.py:30
  69.3 1.7 %near_terms.1 = (bf16[256,512]{1,0:T(8,128)(2,1)S(1)}, bf16[256,512]{1,0:T(8,128)(2,1)S(1)}, bf16[256,512]{1,0:T(8,128)(2,1)S(1)}, bf16[256,512]{1,0:T(8,128)(2,...) custom-call(s32[4]{0:T(128)S(1)} %pad_add_fusion.ids, ...), custom_call_target="tpu_custom_call" | custom-call | flops 939524096 | bytes 6291456 | tf_op jit(solution)/shard_map/near_terms/pallas_call | solution.py:416
  71.2 2.0 %weight_terms.1 = (bf16[4,128,512]{2,1,0:T(8,128)(2,1)S(1)}, bf16[4,128,512]{2,1,0:T(8,128)(2,1)S(1)}, bf16[4,128,512]{2,1,0:T(8,128)(2,1)S(1)}, bf16[4,128,512]{2,1,0:T(8,128)(2,1)S(1)}) custom-call(s32[4]{0:T(128)S(1)} %pad_add_fusion.ids, bf16[8,256,256]{2,1,0:T(8,128)(2,1)S(1)} %get-tuple-element.84.mine, ...), custom_call_target="tpu_custom_call" | custom-call | flops 1073741824 | bytes 5242880 | tf_op jit(solution)/shard_map/weight_terms/pallas_call | solution.py:463
  73.2 2.1 %collective-permute-done.20.b = bf16[256,512]{1,0:T(8,128)(2,1)S(1)} collective-permute-done((bf16[256,512]{1,0:T(8,128)(2,1)S(1)}, bf16[256,512]{1,0:T(8,128)(2,1)S(1)}, u32[]{:S(2)}, u32[]{:S(2)}) %collective-permute-start.20) | collective-permute-done | bytes 262176 | tf_op jit(solution)/shard_map/ppermute | solution.py:30
  75.4 2.2 %collective-permute-start.21 = (bf16[256,512]{1,0:T(8,128)(2,1)S(1)}, bf16[256,512]{1,0:T(8,128)(2,1)S(1)}, u32[]{:S(2)}, u32[]{:S(2)}) collective-permute-start(bf16[256,512]{1,0:T(8,128)(2,1)S(1)} %add.69), channel_id=1, source_target_pairs={{0,1},{1,2},{2,3},{3,4},{4,5},{5,6},{6,7},{7,0},{8,15},{9,8},{10,9... | collective-permute-start | bytes 786440 | tf_op jit(solution)/shard_map/ppermute | solution.py:30
  78.4 2.4 %collective-permute-start.29 = (bf16[4,128,512]{2,1,0:T(8,128)(2,1)S(1)}, bf16[4,128,512]{2,1,0:T(8,128)(2,1)S(1)}, u32[]{:S(2)}, u32[]{:S(2)}) collective-permute-start(bf16[4,128,512]{2,1,0:T(8,128)(2,1)S(1)} %get-tuple-element.96), channel_id=1, source_target_pairs={{0,192},{8,56},{16,208},{24,8},{32,224},{40,24},{48,240},{56,40},{... | collective-permute-start | bytes 1572872 | tf_op jit(solution)/shard_map/ppermute | solution.py:46
  80.9 2.8 %collective-permute-done.21.b = bf16[256,512]{1,0:T(8,128)(2,1)S(1)} collective-permute-done((bf16[256,512]{1,0:T(8,128)(2,1)S(1)}, bf16[256,512]{1,0:T(8,128)(2,1)S(1)}, u32[]{:S(2)}, u32[]{:S(2)}) %collective-permute-start.21) | collective-permute-done | bytes 262176 | tf_op jit(solution)/shard_map/ppermute | solution.py:30
  83.8 2.5 %collective-permute-start.22 = (bf16[256,512]{1,0:T(8,128)(2,1)S(1)}, bf16[256,512]{1,0:T(8,128)(2,1)S(1)}, u32[]{:S(2)}, u32[]{:S(2)}) collective-permute-start(bf16[256,512]{1,0:T(8,128)(2,1)S(1)} %add.70), channel_id=1, source_target_pairs={{0,1},{1,2},{2,3},{3,4},{4,5},{5,6},{6,7},{7,0},{8,15},{9,8},{10,9... | collective-permute-start | bytes 786440 | tf_op jit(solution)/shard_map/ppermute | solution.py:30
  86.3 4.6 %collective-permute-done.25.b = bf16[256,512]{1,0:T(8,128)(2,1)S(1)} collective-permute-done((bf16[256,512]{1,0:T(8,128)(2,1)S(1)}, bf16[256,512]{1,0:T(8,128)(2,1)S(1)}, u32[]{:S(2)}, u32[]{:S(2)}) %collective-permute-start.25) | collective-permute-done | bytes 262176 | tf_op jit(solution)/shard_map/ppermute | solution.py:30
  91.0 2.0 %collective-permute-done.22.b = bf16[256,512]{1,0:T(8,128)(2,1)S(1)} collective-permute-done((bf16[256,512]{1,0:T(8,128)(2,1)S(1)}, bf16[256,512]{1,0:T(8,128)(2,1)S(1)}, u32[]{:S(2)}, u32[]{:S(2)}) %collective-permute-start.22) | collective-permute-done | bytes 262176 | tf_op jit(solution)/shard_map/ppermute | solution.py:30
  93.1 2.8 %collective-permute-start.23 = (bf16[256,512]{1,0:T(8,128)(2,1)S(1)}, bf16[256,512]{1,0:T(8,128)(2,1)S(1)}, u32[]{:S(2)}, u32[]{:S(2)}) collective-permute-start(bf16[256,512]{1,0:T(8,128)(2,1)S(1)} %add.71), channel_id=1, source_target_pairs={{0,1},{1,2},{2,3},{3,4},{4,5},{5,6},{6,7},{7,0},{8,15},{9,8},{10,9... | collective-permute-start | bytes 786440 | tf_op jit(solution)/shard_map/ppermute | solution.py:30
  96.3 3.0 %collective-permute-start.31 = (bf16[128,512]{1,0:T(8,128)(2,1)S(1)}, bf16[128,512]{1,0:T(8,128)(2,1)S(1)}, u32[]{:S(2)}, u32[]{:S(2)}) collective-permute-start(bf16[128,512]{1,0:T(8,128)(2,1)S(1)} %get-tuple-element.99), channel_id=1, source_target_pairs={{0,32},{8,136},{16,48},{24,152},{32,0},{40,168},{48,16},{56,184},{... | collective-permute-start | bytes 393224 | tf_op jit(solution)/shard_map/ppermute | solution.py:38
  101.0 2.8 %collective-permute-done.30 = bf16[128,512]{1,0:T(8,128)(2,1)S(1)} collective-permute-done((bf16[128,512]{1,0:T(8,128)(2,1)S(1)}, bf16[128,512]{1,0:T(8,128)(2,1)S(1)}, u32[]{:S(2)}, u32[]{:S(2)}) %collective-permute-start.30) | collective-permute-done | bytes 131104 | tf_op jit(solution)/shard_map/ppermute | solution.py:38
  (73 shorter events, 14.3 us)
Async XLA Ops:
  0.6 8.9 %collective-permute-start.4 = (bf16[256,512]{1,0:T(8,128)(2,1)}, bf16[256,512]{1,0:T(8,128)(2,1)S(1)}, u32[]{:S(2)}, u32[]{:S(2)}) collective-permute-start(bf16[256,512]{1,0:T(8,128)(2,1)} %refs_0_.2), channel_id=1, source_target_pairs={{0,7},{1,0},{2,1},{3,2},{4,3},{5,4},{6,5},{7,6},{8,9},{9,10},{10,1... | collective-permute-start | bytes 786440 | tf_op jit(solution)/shard_map/ppermute | solution.py:30
  0.8 8.9 %collective-permute-start = (bf16[256,512]{1,0:T(8,128)(2,1)}, bf16[256,512]{1,0:T(8,128)(2,1)S(1)}, u32[]{:S(2)}, u32[]{:S(2)}) collective-permute-start(bf16[256,512]{1,0:T(8,128)(2,1)} %refs_0_.2), channel_id=1, source_target_pairs={{0,1},{1,2},{2,3},{3,4},{4,5},{5,6},{6,7},{7,0},{8,15},{9,8},{10,9... | collective-permute-start | bytes 786440 | tf_op jit(solution)/shard_map/ppermute | solution.py:30
  4.0 9.4 %collective-permute-start.7 = (bf16[128,512]{1,0:T(8,128)(2,1)}, bf16[128,512]{1,0:T(8,128)(2,1)S(1)}, u32[]{:S(2)}, u32[]{:S(2)}) collective-permute-start(bf16[128,512]{1,0:T(8,128)(2,1)} %refs_0_.3), channel_id=1, source_target_pairs={{0,48},{8,200},{16,0},{24,216},{32,16},{40,232},{48,32},{56,248},{... | collective-permute-start | bytes 393224 | tf_op jit(solution)/shard_map/ppermute | solution.py:38
  6.7 6.8 %collective-permute-start.8 = (bf16[128,512]{1,0:T(8,128)(2,1)}, bf16[128,512]{1,0:T(8,128)(2,1)S(1)}, u32[]{:S(2)}, u32[]{:S(2)}) collective-permute-start(bf16[128,512]{1,0:T(8,128)(2,1)} %refs_0_.3), channel_id=1, source_target_pairs={{0,32},{8,136},{16,48},{24,152},{32,0},{40,168},{48,16},{56,184},{... | collective-permute-start | bytes 393224 | tf_op jit(solution)/shard_map/ppermute | solution.py:38
  7.5 7.3 %collective-permute-start.9 = (bf16[128,512]{1,0:T(8,128)(2,1)}, bf16[128,512]{1,0:T(8,128)(2,1)S(1)}, u32[]{:S(2)}, u32[]{:S(2)}) collective-permute-start(bf16[128,512]{1,0:T(8,128)(2,1)} %refs_0_.3), channel_id=1, source_target_pairs={{0,16},{8,72},{16,32},{24,88},{32,48},{40,104},{48,0},{56,120},{64... | collective-permute-start | bytes 393224 | tf_op jit(solution)/shard_map/ppermute | solution.py:38
  9.5 14.6 %collective-permute-start.5 = (bf16[256,512]{1,0:T(8,128)(2,1)S(1)}, bf16[256,512]{1,0:T(8,128)(2,1)S(1)}, u32[]{:S(2)}, u32[]{:S(2)}) collective-permute-start(bf16[256,512]{1,0:T(8,128)(2,1)S(1)} %collective-permute-done.4.refs_1_), channel_id=1, source_target_pairs={{0,7},{1,0},{2,1},{3,2},{4,3},{5,4},{6,5},{7,6},{8,9},{9,10},{10,1... | collective-permute-start | bytes 786440 | tf_op jit(solution)/shard_map/ppermute | solution.py:30
  9.7 12.4 %collective-permute-start.1 = (bf16[256,512]{1,0:T(8,128)(2,1)S(1)}, bf16[256,512]{1,0:T(8,128)(2,1)S(1)}, u32[]{:S(2)}, u32[]{:S(2)}) collective-permute-start(bf16[256,512]{1,0:T(8,128)(2,1)S(1)} %collective-permute-done.refs_2_), channel_id=1, source_target_pairs={{0,1},{1,2},{2,3},{3,4},{4,5},{5,6},{6,7},{7,0},{8,15},{9,8},{10,9... | collective-permute-start | bytes 786440 | tf_op jit(solution)/shard_map/ppermute | solution.py:30
  15.7 15.4 %collective-permute-start.10 = (bf16[4,128,512]{2,1,0:T(8,128)(2,1)S(1)}, bf16[4,128,512]{2,1,0:T(8,128)(2,1)S(1)}, u32[]{:S(2)}, u32[]{:S(2)}) collective-permute-start(bf16[4,128,512]{2,1,0:T(8,128)(2,1)S(1)} %stack.21.refs_0_), channel_id=1, source_target_pairs={{0,192},{8,56},{16,208},{24,8},{32,224},{40,24},{48,240},{56,40},{... | collective-permute-start | bytes 1572872 | tf_op jit(solution)/shard_map/ppermute | solution.py:46
  18.8 12.3 %collective-permute-start.11 = (bf16[4,128,512]{2,1,0:T(8,128)(2,1)S(1)}, bf16[4,128,512]{2,1,0:T(8,128)(2,1)S(1)}, u32[]{:S(2)}, u32[]{:S(2)}) collective-permute-start(bf16[4,128,512]{2,1,0:T(8,128)(2,1)S(1)} %stack.21.refs_0_), channel_id=1, source_target_pairs={{0,128},{8,40},{16,144},{24,56},{32,160},{40,8},{48,176},{56,24},{... | collective-permute-start | bytes 1572872 | tf_op jit(solution)/shard_map/ppermute | solution.py:46
  19.5 15.8 %collective-permute-start.12 = (bf16[4,128,512]{2,1,0:T(8,128)(2,1)S(1)}, bf16[4,128,512]{2,1,0:T(8,128)(2,1)}, u32[]{:S(2)}, u32[]{:S(2)}) collective-permute-start(bf16[4,128,512]{2,1,0:T(8,128)(2,1)S(1)} %stack.21.refs_0_), channel_id=1, source_target_pairs={{0,64},{8,24},{16,80},{24,40},{32,96},{40,56},{48,112},{56,8},{64,... | collective-permute-start | bytes 1572872 | tf_op jit(solution)/shard_map/ppermute | solution.py:46
  22.1 13.2 %collective-permute-start.2 = (bf16[256,512]{1,0:T(8,128)(2,1)S(1)}, bf16[256,512]{1,0:T(8,128)(2,1)S(1)}, u32[]{:S(2)}, u32[]{:S(2)}) collective-permute-start(bf16[256,512]{1,0:T(8,128)(2,1)S(1)} %collective-permute-done.1.refs_4_), channel_id=1, source_target_pairs={{0,1},{1,2},{2,3},{3,4},{4,5},{5,6},{6,7},{7,0},{8,15},{9,8},{10,9... | collective-permute-start | bytes 786440 | tf_op jit(solution)/shard_map/ppermute | solution.py:30
  24.1 11.2 %collective-permute-start.6 = (bf16[256,512]{1,0:T(8,128)(2,1)S(1)}, bf16[256,512]{1,0:T(8,128)(2,1)S(1)}, u32[]{:S(2)}, u32[]{:S(2)}) collective-permute-start(bf16[256,512]{1,0:T(8,128)(2,1)S(1)} %collective-permute-done.5.refs_3_), channel_id=1, source_target_pairs={{0,7},{1,0},{2,1},{3,2},{4,3},{5,4},{6,5},{7,6},{8,9},{9,10},{10,1... | collective-permute-start | bytes 786440 | tf_op jit(solution)/shard_map/ppermute | solution.py:30
  35.8 3.4 %collective-permute-start.14 = (bf16[4,128,512]{2,1,0:T(8,128)(2,1)S(1)}, bf16[4,128,512]{2,1,0:T(8,128)(2,1)S(1)}, u32[]{:S(2)}, u32[]{:S(2)}) collective-permute-start(bf16[4,128,512]{2,1,0:T(8,128)(2,1)S(1)} %collective-permute-done.10.refs_1_), channel_id=1, source_target_pairs={{0,8},{8,0},{16,24},{24,16},{32,40},{40,32},{48,56},{56,48},{64,72... | collective-permute-start | bytes 1572872 | tf_op jit(solution)/shard_map/ppermute | solution.py:50
  36.3 3.6 %collective-permute-start.15 = (bf16[4,128,512]{2,1,0:T(8,128)(2,1)S(1)}, bf16[4,128,512]{2,1,0:T(8,128)(2,1)S(1)}, u32[]{:S(2)}, u32[]{:S(2)}) collective-permute-start(bf16[4,128,512]{2,1,0:T(8,128)(2,1)S(1)} %collective-permute-done.11.refs_2_), channel_id=1, source_target_pairs={{0,8},{8,0},{16,24},{24,16},{32,40},{40,32},{48,56},{56,48},{64,72... | collective-permute-start | bytes 1572872 | tf_op jit(solution)/shard_map/ppermute | solution.py:50
  36.4 3.6 %collective-permute-start.16 = (bf16[4,128,512]{2,1,0:T(8,128)(2,1)}, bf16[4,128,512]{2,1,0:T(8,128)(2,1)S(1)}, u32[]{:S(2)}, u32[]{:S(2)}) collective-permute-start(bf16[4,128,512]{2,1,0:T(8,128)(2,1)} %collective-permute-done.12.refs_3_), channel_id=1, source_target_pairs={{0,8},{8,0},{16,24},{24,16},{32,40},{40,32},{48,56},{56,48},{64,72... | collective-permute-start | bytes 1572872 | tf_op jit(solution)/shard_map/ppermute | solution.py:50
  36.8 8.1 %collective-permute-start.3 = (bf16[256,512]{1,0:T(8,128)(2,1)S(1)}, bf16[256,512]{1,0:T(8,128)(2,1)S(1)}, u32[]{:S(2)}, u32[]{:S(2)}) collective-permute-start(bf16[256,512]{1,0:T(8,128)(2,1)S(1)} %collective-permute-done.2.p3), channel_id=1, source_target_pairs={{0,1},{1,2},{2,3},{3,4},{4,5},{5,6},{6,7},{7,0},{8,15},{9,8},{10,9... | collective-permute-start | bytes 786440 | tf_op jit(solution)/shard_map/ppermute | solution.py:30
  49.4 8.8 %collective-permute-start.17 = (bf16[128,512]{1,0:T(8,128)(2,1)S(1)}, bf16[128,512]{1,0:T(8,128)(2,1)S(1)}, u32[]{:S(2)}, u32[]{:S(2)}) collective-permute-start(bf16[128,512]{1,0:T(8,128)(2,1)S(1)} %get-tuple-element.68), channel_id=1, source_target_pairs={{0,8},{8,16},{16,24},{24,32},{32,40},{40,48},{48,56},{56,64},{64,7... | collective-permute-start | bytes 393224 | tf_op jit(solution)/shard_map/ppermute | solution.py:55
  53.6 8.9 %collective-permute-start.18 = (bf16[128,512]{1,0:T(8,128)(2,1)S(1)}, bf16[128,512]{1,0:T(8,128)(2,1)S(1)}, u32[]{:S(2)}, u32[]{:S(2)}) collective-permute-start(bf16[128,512]{1,0:T(8,128)(2,1)S(1)} %get-tuple-element.74), channel_id=1, source_target_pairs={{0,248},{8,0},{16,8},{24,16},{32,24},{40,32},{48,40},{56,48},{64,5... | collective-permute-start | bytes 393224 | tf_op jit(solution)/shard_map/ppermute | solution.py:55
  67.2 4.0 %collective-permute-start.19 = (bf16[10,256,256]{2,1,0:T(8,128)(2,1)S(1)}, bf16[10,256,256]{2,1,0:T(8,128)(2,1)S(1)}, u32[]{:S(2)}, u32[]{:S(2)}) collective-permute-start(bf16[10,256,256]{2,1,0:T(8,128)(2,1)S(1)} %get-tuple-element.85), channel_id=1, source_target_pairs={{0,8},{8,0},{16,24},{24,16},{32,40},{40,32},{48,56},{56,48},{64,72... | collective-permute-start | bytes 3932168 | tf_op jit(solution)/shard_map/ppermute | solution.py:50
  67.3 8.0 %collective-permute-start.20 = (bf16[256,512]{1,0:T(8,128)(2,1)S(1)}, bf16[256,512]{1,0:T(8,128)(2,1)S(1)}, u32[]{:S(2)}, u32[]{:S(2)}) collective-permute-start(bf16[256,512]{1,0:T(8,128)(2,1)S(1)} %get-tuple-element.89), channel_id=1, source_target_pairs={{0,1},{1,2},{2,3},{3,4},{4,5},{5,6},{6,7},{7,0},{8,15},{9,8},{10,9... | collective-permute-start | bytes 786440 | tf_op jit(solution)/shard_map/ppermute | solution.py:30
  71.0 9.7 %collective-permute-start.24 = (bf16[256,512]{1,0:T(8,128)(2,1)S(1)}, bf16[256,512]{1,0:T(8,128)(2,1)S(1)}, u32[]{:S(2)}, u32[]{:S(2)}) collective-permute-start(bf16[256,512]{1,0:T(8,128)(2,1)S(1)} %get-tuple-element.92), channel_id=1, source_target_pairs={{0,7},{1,0},{2,1},{3,2},{4,3},{5,4},{6,5},{7,6},{8,9},{9,10},{10,1... | collective-permute-start | bytes 786440 | tf_op jit(solution)/shard_map/ppermute | solution.py:30
  75.4 8.4 %collective-permute-start.21 = (bf16[256,512]{1,0:T(8,128)(2,1)S(1)}, bf16[256,512]{1,0:T(8,128)(2,1)S(1)}, u32[]{:S(2)}, u32[]{:S(2)}) collective-permute-start(bf16[256,512]{1,0:T(8,128)(2,1)S(1)} %add.69), channel_id=1, source_target_pairs={{0,1},{1,2},{2,3},{3,4},{4,5},{5,6},{6,7},{7,0},{8,15},{9,8},{10,9... | collective-permute-start | bytes 786440 | tf_op jit(solution)/shard_map/ppermute | solution.py:30
  77.5 18.4 %collective-permute-start.27 = (bf16[4,128,512]{2,1,0:T(8,128)(2,1)S(1)}, bf16[4,128,512]{2,1,0:T(8,128)(2,1)S(1)}, u32[]{:S(2)}, u32[]{:S(2)}) collective-permute-start(bf16[4,128,512]{2,1,0:T(8,128)(2,1)S(1)} %get-tuple-element.94), channel_id=1, source_target_pairs={{0,64},{8,24},{16,80},{24,40},{32,96},{40,56},{48,112},{56,8},{64,... | collective-permute-start | bytes 1572872 | tf_op jit(solution)/shard_map/ppermute | solution.py:46
  77.5 18.4 %collective-permute-start.28 = (bf16[4,128,512]{2,1,0:T(8,128)(2,1)S(1)}, bf16[4,128,512]{2,1,0:T(8,128)(2,1)S(1)}, u32[]{:S(2)}, u32[]{:S(2)}) collective-permute-start(bf16[4,128,512]{2,1,0:T(8,128)(2,1)S(1)} %get-tuple-element.95), channel_id=1, source_target_pairs={{0,128},{8,40},{16,144},{24,56},{32,160},{40,8},{48,176},{56,24},{... | collective-permute-start | bytes 1572872 | tf_op jit(solution)/shard_map/ppermute | solution.py:46
  78.4 17.5 %collective-permute-start.29 = (bf16[4,128,512]{2,1,0:T(8,128)(2,1)S(1)}, bf16[4,128,512]{2,1,0:T(8,128)(2,1)S(1)}, u32[]{:S(2)}, u32[]{:S(2)}) collective-permute-start(bf16[4,128,512]{2,1,0:T(8,128)(2,1)S(1)} %get-tuple-element.96), channel_id=1, source_target_pairs={{0,192},{8,56},{16,208},{24,8},{32,224},{40,24},{48,240},{56,40},{... | collective-permute-start | bytes 1572872 | tf_op jit(solution)/shard_map/ppermute | solution.py:46
  80.8 10.0 %collective-permute-start.25 = (bf16[256,512]{1,0:T(8,128)(2,1)S(1)}, bf16[256,512]{1,0:T(8,128)(2,1)S(1)}, u32[]{:S(2)}, u32[]{:S(2)}) collective-permute-start(bf16[256,512]{1,0:T(8,128)(2,1)S(1)} %add.72), channel_id=1, source_target_pairs={{0,7},{1,0},{2,1},{3,2},{4,3},{5,4},{6,5},{7,6},{8,9},{9,10},{10,1... | collective-permute-start | bytes 786440 | tf_op jit(solution)/shard_map/ppermute | solution.py:30
  83.8 9.2 %collective-permute-start.22 = (bf16[256,512]{1,0:T(8,128)(2,1)S(1)}, bf16[256,512]{1,0:T(8,128)(2,1)S(1)}, u32[]{:S(2)}, u32[]{:S(2)}) collective-permute-start(bf16[256,512]{1,0:T(8,128)(2,1)S(1)} %add.70), channel_id=1, source_target_pairs={{0,1},{1,2},{2,3},{3,4},{4,5},{5,6},{6,7},{7,0},{8,15},{9,8},{10,9... | collective-permute-start | bytes 786440 | tf_op jit(solution)/shard_map/ppermute | solution.py:30
  90.9 9.3 %collective-permute-start.26 = (bf16[256,512]{1,0:T(8,128)(2,1)S(1)}, bf16[256,512]{1,0:T(8,128)(2,1)S(1)}, u32[]{:S(2)}, u32[]{:S(2)}) collective-permute-start(bf16[256,512]{1,0:T(8,128)(2,1)S(1)} %add.73), channel_id=1, source_target_pairs={{0,7},{1,0},{2,1},{3,2},{4,3},{5,4},{6,5},{7,6},{8,9},{9,10},{10,1... | collective-permute-start | bytes 786440 | tf_op jit(solution)/shard_map/ppermute | solution.py:30
  93.1 7.1 %collective-permute-start.23 = (bf16[256,512]{1,0:T(8,128)(2,1)S(1)}, bf16[256,512]{1,0:T(8,128)(2,1)S(1)}, u32[]{:S(2)}, u32[]{:S(2)}) collective-permute-start(bf16[256,512]{1,0:T(8,128)(2,1)S(1)} %add.71), channel_id=1, source_target_pairs={{0,1},{1,2},{2,3},{3,4},{4,5},{5,6},{6,7},{7,0},{8,15},{9,8},{10,9... | collective-permute-start | bytes 786440 | tf_op jit(solution)/shard_map/ppermute | solution.py:30
  96.2 7.7 %collective-permute-start.30 = (bf16[128,512]{1,0:T(8,128)(2,1)S(1)}, bf16[128,512]{1,0:T(8,128)(2,1)S(1)}, u32[]{:S(2)}, u32[]{:S(2)}) collective-permute-start(bf16[128,512]{1,0:T(8,128)(2,1)S(1)} %get-tuple-element.98), channel_id=1, source_target_pairs={{0,16},{8,72},{16,32},{24,88},{32,48},{40,104},{48,0},{56,120},{64... | collective-permute-start | bytes 393224 | tf_op jit(solution)/shard_map/ppermute | solution.py:38
  96.3 7.6 %collective-permute-start.31 = (bf16[128,512]{1,0:T(8,128)(2,1)S(1)}, bf16[128,512]{1,0:T(8,128)(2,1)S(1)}, u32[]{:S(2)}, u32[]{:S(2)}) collective-permute-start(bf16[128,512]{1,0:T(8,128)(2,1)S(1)} %get-tuple-element.99), channel_id=1, source_target_pairs={{0,32},{8,136},{16,48},{24,152},{32,0},{40,168},{48,16},{56,184},{... | collective-permute-start | bytes 393224 | tf_op jit(solution)/shard_map/ppermute | solution.py:38
  99.3 5.4 %collective-permute-start.32 = (bf16[128,512]{1,0:T(8,128)(2,1)S(1)}, bf16[128,512]{1,0:T(8,128)(2,1)S(1)}, u32[]{:S(2)}, u32[]{:S(2)}) collective-permute-start(bf16[128,512]{1,0:T(8,128)(2,1)S(1)} %get-tuple-element.100), channel_id=1, source_target_pairs={{0,48},{8,200},{16,0},{24,216},{32,16},{40,232},{48,32},{56,248},{... | collective-permute-start | bytes 393224 | tf_op jit(solution)/shard_map/ppermute | solution.py:38
  (5 other events, 39.0 us)

commit v3 on v2

--- a/solution.py
+++ b/solution.py
@@ -141,29 +141,21 @@
     return lax.rem(ids[3] + jnp.where(ids[2] == 0, steps, NZ - steps), NZ)
 
 
-def load_weight(ids, own, other, w, sems, act):
-    def one_core(core, blocks, base):
+def load_weight(ids, core, blocks, w, sems, act):
+    @pl.when(core == 0)
+    def _():
         for i, block in enumerate(blocks):
-            if core == 0:
-                y = lax.rem(ids[0] + i, 4)
-                for half in range(2):
-                    at = w.at[2 * y + half, :, 0]
-                    act(pltpu.make_async_copy(block.at[2 * half : 2 * half + 2], at, sems.at[base + 2 * i + half]))
-            else:
-                x = lax.rem(ids[1] + i, 4)
-                for y in range(4):
-                    at = w.at[2 * y + x // 2, lax.rem(x, 2), 1]
-                    act(pltpu.make_async_copy(block.at[y], at, sems.at[base + 4 * i + y]))
-
-    @pl.when(ids[2] == 0)
+            act(pltpu.make_async_copy(block, w.at[lax.rem(ids[0] + i, 4), :, 0], sems.at[i]))
+
+    @pl.when(core == 1)
     def _():
-        one_core(0, own, 0)
-        one_core(1, other, 8)
-
-    @pl.when(ids[2] == 1)
-    def _():
-        one_core(0, other, 0)
-        one_core(1, own, 8)
+        for i, block in enumerate(blocks):
+            act(pltpu.make_async_copy(block, w.at[:, lax.rem(ids[1] + i, 4), 1], sems.at[i]))
+
+
+def weight_rows(ids, k, w):
+    zb = place_of(ids, k)
+    return w.at[zb // 2, pl.ds(lax.rem(zb, 2) * 2, 2)]
 
 
 def start(copy):
@@ -189,17 +181,12 @@
             out[k, :, xp * 128 : xp * 128 + 128] = piece[:, lanes]
 
 
-def piece_term(ids, k, piece, w):
-    return jnp.dot(piece[...], w[place_of(ids, k)].reshape(512, 512), preferred_element_type=F32)
-
-
-FIRST, NEXT, LATE = (0, 1, 7, 2, 6), (3, 5), 4
+FIRST, NEXT = (0, 1, 7, 2, 6), (3, 5, 4)
 
 
 def split_kernel(ids, *refs):
-    pieces, (tok, mine_ref, cross_ref) = refs[0:5], refs[5:]
+    pieces, (mine_ref, cross_ref) = refs[0:5], refs[5:]
     for n, k in enumerate(FIRST):
-        tok[n] = pieces[n][...]
         split_piece(ids, k, pieces[n], mine_ref, cross_ref)
 
 
@@ -207,79 +194,75 @@
     return pl.pallas_call(
         split_kernel,
         in_specs=[SMEM] + [VMEM] * 5,
-        out_specs=[VMEM] * 3,
-        out_shape=[jax.ShapeDtypeStruct((n, 256, lanes), BF) for n, lanes in ((5, 512), (NZ, 256), (NZ + 2, 256))],
+        out_specs=[VMEM] * 2,
+        out_shape=[jax.ShapeDtypeStruct((n, 256, 256), BF) for n in (NZ, NZ + 2)],
         compiler_params=pltpu.CompilerParams(vmem_limit_bytes=4 << 20),
         cost_estimate=pl.CostEstimate(flops=1 << 20, bytes_accessed=4 << 20, transcendentals=0),
         name="split_tokens",
     )(ids, *pieces)
 
 
-def early_kernel(ids, tok, q3, p3, *refs):
-    own, other, (_, _, acc, w, mine_ref, cross_ref, more, sems, tok_sems) = refs[0:4], refs[4:8], refs[8:]
-    load_weight(ids, own, other, w, sems, start)
-    arrive = [pltpu.make_async_copy(piece, more.at[n], tok_sems.at[n]) for n, piece in enumerate((q3, p3))]
-    for copy in arrive:
-        copy.start()
-    for copy in arrive:
-        copy.wait()
-    for n, k in enumerate(NEXT):
-        split_piece(ids, k, more.at[n], mine_ref, cross_ref)
-    load_weight(ids, own, other, w, sems, wait)
+def core_term(ids, core, columns, w):
     total = None
-    for k, piece in zip(FIRST + NEXT, [tok.at[n] for n in range(5)] + [more.at[0], more.at[1]]):
-        term = piece_term(ids, k, piece, w)
+    for k in range(NZ):
+        rows = weight_rows(ids, k, w)[:, core].reshape(256, 512)
+        term = jnp.dot(columns[k], rows, preferred_element_type=F32)
         total = term if total is None else total + term
-    acc[...] = total
-
-
-def late_kernel(ids, *refs):
-    piece, acc, w, _, _, dg_ref, p_ref, tail_ref, head_ref, mine_ref, cross_ref = refs
-    total = acc[...] + piece_term(ids, LATE, piece, w)
-    split_piece(ids, LATE, piece, mine_ref, cross_ref)
-    p = total.astype(BF)
+    return total
+
+
+def own_kernel(ids, *refs):
+    pieces, own, (_, _, acc, w, mine_ref, cross_ref, sems) = refs[0:3], refs[3:7], refs[7:]
+    load_weight(ids, ids[2], own, w, sems, start)
+    for piece, k in zip(pieces, NEXT):
+        split_piece(ids, k, piece, mine_ref, cross_ref)
+    load_weight(ids, ids[2], own, w, sems, wait)
+    acc[...] = core_term(ids, ids[2], mine_ref, w)
+
+
+def project_own(ids, pieces, own, mine, cross):
+    return pl.pallas_call(
+        own_kernel,
+        in_specs=[SMEM] + [VMEM] * 3 + [HBM] * 4 + [VMEM] * 2,
+        out_specs=[VMEM] * 4,
+        out_shape=[
+            jax.ShapeDtypeStruct((256, 512), F32),
+            jax.ShapeDtypeStruct((4, 4, 2, 128, 512), BF),
+            jax.ShapeDtypeStruct(mine.shape, BF),
+            jax.ShapeDtypeStruct(cross.shape, BF),
+        ],
+        input_output_aliases={8: 2, 9: 3},
+        scratch_shapes=[pltpu.SemaphoreType.DMA((4,))],
+        compiler_params=pltpu.CompilerParams(vmem_limit_bytes=6 << 20),
+        cost_estimate=pl.CostEstimate(flops=1 << 32, bytes_accessed=4 << 20, transcendentals=0),
+        name="project_own",
+    )(ids, *pieces, *own, mine, cross)
+
+
+def other_kernel(ids, *refs):
+    other, (cross, acc, _, dg_ref, p_ref, tail_ref, head_ref, w, sems) = refs[0:4], refs[4:]
+    load_weight(ids, 1 - ids[2], other, w, sems, start)
+    load_weight(ids, 1 - ids[2], other, w, sems, wait)
+    p = (acc[...] + core_term(ids, 1 - ids[2], cross, w)).astype(BF)
     p_ref[...] = p
     tail_ref[...] = p[128:256]
     top = p[0:128].astype(F32)
     head_ref[...] = (dg_ref[0:128].astype(F32) * (top * jax.nn.sigmoid(top))).astype(BF)
 
 
-def project_early(ids, tok, pieces, blocks, mine, cross):
-    return pl.pallas_call(
-        early_kernel,
-        in_specs=[SMEM, VMEM] + [HBM] * 10 + [VMEM] * 2,
+def project_other(ids, other, cross, acc, w, d_gated):
+    half = jax.ShapeDtypeStruct((128, 512), BF)
+    return pl.pallas_call(
+        other_kernel,
+        in_specs=[SMEM] + [HBM] * 4 + [VMEM] * 4,
         out_specs=[VMEM] * 4,
-        out_shape=[
-            jax.ShapeDtypeStruct((256, 512), F32),
-            jax.ShapeDtypeStruct((NZ, 2, 2, 128, 512), BF),
-            jax.ShapeDtypeStruct(mine.shape, BF),
-            jax.ShapeDtypeStruct(cross.shape, BF),
-        ],
-        input_output_aliases={12: 2, 13: 3},
-        scratch_shapes=[
-            pltpu.VMEM((2, 256, 512), BF),
-            pltpu.SemaphoreType.DMA((24,)),
-            pltpu.SemaphoreType.DMA((2,)),
-        ],
+        out_shape=[jax.ShapeDtypeStruct((256, 512), BF), half, half, jax.ShapeDtypeStruct(w.shape, BF)],
+        input_output_aliases={7: 3},
+        scratch_shapes=[pltpu.SemaphoreType.DMA((4,))],
         compiler_params=pltpu.CompilerParams(vmem_limit_bytes=6 << 20),
-        cost_estimate=pl.CostEstimate(flops=1 << 32, bytes_accessed=8 << 20, transcendentals=0),
-        name="project_early",
-    )(ids, tok, *pieces, *blocks, mine, cross)
-
-
-def project_late(ids, piece, early, d_gated):
-    half = jax.ShapeDtypeStruct((128, 512), BF)
-    part_of, more = jax.ShapeDtypeStruct((NZ, 256, 256), BF), jax.ShapeDtypeStruct((NZ + 2, 256, 256), BF)
-    return pl.pallas_call(
-        late_kernel,
-        in_specs=[SMEM] + [VMEM] * 6,
-        out_specs=[VMEM] * 5,
-        out_shape=[jax.ShapeDtypeStruct((256, 512), BF), half, half, part_of, more],
-        input_output_aliases={4: 3, 5: 4},
-        compiler_params=pltpu.CompilerParams(vmem_limit_bytes=6 << 20),
-        cost_estimate=pl.CostEstimate(flops=2 * 256 * 512 * 512, bytes_accessed=4 << 20, transcendentals=0),
-        name="project_late",
-    )(ids, piece, *early, d_gated)
+        cost_estimate=pl.CostEstimate(flops=1 << 30, bytes_accessed=4 << 20, transcendentals=0),
+        name="project_other",
+    )(ids, *other, cross, acc, w, d_gated)
 
 
 def mix(ext, live_ref, taps_ref, even, odd, acc, reverse):
@@ -316,46 +299,40 @@
 LOW, HIGH = slice(0, 128), slice(128, 256)
 
 
-def ahead_inside_kernel(p_ref, dg_ref, taps_ref, live_ref, gated_ref, dgate_ref, ext, even, odd, acc):
+def inside_kernel(
+    p_ref, dg_ref, taps_ref, back_ref, ahead_ref, gated_ref, dgate_ref, part_ref, dconv_ref, ext, even, odd, acc
+):
     ext[...] = p_ref[...].astype(F32)
-    mix(ext, live_ref.at[HIGH], taps_ref, even, odd, acc, False)
+    mix(ext, back_ref.at[HIGH], taps_ref, even, odd, acc, False)
     p, up = p_ref[HIGH].astype(F32), dg_ref[HIGH].astype(F32)
-    gated_ref[...], dgate_ref[...], _ = gates(p, up, acc[...])
-
-
-def back_inside_kernel(p_ref, dg_ref, taps_ref, live_ref, part_ref, dconv_ref, ext, even, odd, acc):
-    p = p_ref[...].astype(F32)
-    ext[...] = dg_ref[...].astype(F32) * (p * jax.nn.sigmoid(p))
+    gated_ref[...], dgate_ref[...], ext[HIGH] = gates(p, up, acc[...])
+    p, up = p_ref[LOW].astype(F32), dg_ref[LOW].astype(F32)
+    ext[LOW] = up * (p * jax.nn.sigmoid(p))
     dconv_ref[...] = ext[HIGH]
-    mix(ext, live_ref.at[LOW], taps_ref, even, odd, acc, True)
-    part_ref[...] = acc[...]
-
-
-def ahead_edge_kernel(p_ref, dg_ref, taps_ref, live_ref, tail_ref, gated_hi, part_ref, gated_ref, low_ref, ext, even, odd, acc):
+    mix(ext, ahead_ref.at[LOW], taps_ref, even, odd, part_ref, True)
+
+
+def edges_kernel(
+    p_ref, dg_ref, taps_ref, back_ref, ahead_ref, tail_ref, head_ref, gated_hi, dgate_ref, part_ref, dconv_ref,
+    ids, w_ref, _, gated_ref, dproj_ref, far_ref, w, cross_ref, ext, even, odd, acc, sem,
+):
+    load = pltpu.make_async_copy(w_ref, w, sem)
+    load.start()
     p, up = p_ref[LOW].astype(F32), dg_ref[LOW].astype(F32)
     ext[LOW] = tail_ref[...].astype(F32)
     ext[HIGH] = p
-    mix(ext, live_ref.at[LOW], taps_ref, even, odd, acc, False)
+    mix(ext, back_ref.at[LOW], taps_ref, even, odd, acc, False)
     gated_ref[LOW], d_gate, _ = gates(p, up, acc[...])
     gated_ref[HIGH] = gated_hi[...]
-    low_ref[...] = (part_ref[...] + d_gate).astype(BF)
-
-
-def back_edge_kernel(
-    dconv_ref, head_ref, taps_ref, live_ref, low_ref, dgate_ref, ids, w_ref, _, dproj_ref, far_ref, w, cross_ref,
-    ext, even, odd, acc, sem,
-):
-    load = pltpu.make_async_copy(w_ref, w, sem)
-    load.start()
+    dproj_ref[LOW] = (part_ref[...] + d_gate).astype(BF)
     ext[LOW] = dconv_ref[...]
     ext[HIGH] = head_ref[...].astype(F32)
-    mix(ext, live_ref.at[HIGH], taps_ref, even, odd, acc, True)
-    dproj_ref[LOW] = low_ref[...]
+    mix(ext, ahead_ref.at[HIGH], taps_ref, even, odd, acc, True)
     dproj_ref[HIGH] = (acc[...] + dgate_ref[...]).astype(BF)
     cross_ref[NZ] = dproj_ref[:, 0:256]
     cross_ref[NZ + 1] = dproj_ref[:, 256:512]
     load.wait()
-    far_ref[...] = back_term(dproj_ref[...], w[place_of(ids, 4)].reshape(512, 512))
+    far_ref[...] = back_term(dproj_ref[...], weight_rows(ids, 4, w)[...].reshape(512, 512))
 
 
 def back_term(d, block):
@@ -384,23 +361,15 @@
 
 def conv(ids, p, tail, head, d_gated, taps, back, ahead, w, cross):
     half, whole = (128, 512), (256, 512)
-    tail = next_row(tail, 1)
-    gated_hi, dgate_hi = mix_call(
-        ahead_inside_kernel, "ahead_inside", [(half, BF), (half, F32)], p, d_gated, taps, back
+    tail, head = next_row(tail, 1), next_row(head, -1)
+    inside = mix_call(
+        inside_kernel, "inside", [(half, BF), (half, F32), (half, F32), (half, F32)], p, d_gated, taps, back, ahead
     )
-    head = next_row(after(head, gated_hi), -1)
-    part, dconv_hi = mix_call(
-        back_inside_kernel, "back_inside", [(half, F32), (half, F32)], p, d_gated, taps, ahead
+    return mix_call(
+        edges_kernel, "edges", [(whole, BF), (whole, BF), (whole, BF), (w.shape, BF), (cross.shape, BF)],
+        p, d_gated, taps, back, ahead, tail, head, *inside, ids, w, cross,
+        specs=[VMEM] * 11 + [SMEM, HBM, VMEM], scratch=[pltpu.SemaphoreType.DMA], aliases={13: 4},
     )
-    gated, low = mix_call(
-        ahead_edge_kernel, "ahead_edge", [(whole, BF), (half, BF)], p, d_gated, taps, back, tail, gated_hi, part
-    )
-    d_proj, far, w, cross = mix_call(
-        back_edge_kernel, "back_edge", [(whole, BF), (whole, BF), (w.shape, BF), (cross.shape, BF)],
-        dconv_hi, head, taps, ahead, low, dgate_hi, ids, w, cross,
-        specs=[VMEM] * 6 + [SMEM, HBM, VMEM], scratch=[pltpu.SemaphoreType.DMA], aliases={8: 3},
-    )
-    return gated, d_proj, far, w, cross
 
 
 NEAR = (3, 5, 2, 6, 1, 7, 0)
@@ -409,7 +378,7 @@
 def near_kernel(ids, d_ref, w, *outs):
     d = d_ref[...]
     for steps, out in zip(NEAR, outs):
-        out[...] = back_term(d, w[place_of(ids, steps)].reshape(512, 512))
+        out[...] = back_term(d, weight_rows(ids, steps, w)[...].reshape(512, 512))
 
 
 def near_terms(ids, d_proj, weight):
@@ -505,18 +474,17 @@
     first = jnp.where(core == 0, x, y).astype(jnp.int32).reshape(1)
     row_block = stack(first, [w_in] + w)
     own = [row_block] + [wide(row_block, 4 - k) for k in (1, 2, 3)]
-    p2, q2 = around_z(p1, 1), around_z(q1, -1)
+    p2, q2 = around_z(after(p1, row_block), 1), around_z(after(q1, row_block), -1)
     conv_filter, contig_lengths = after((conv_filter, contig_lengths), q1)
     back, ahead = live_taps(contig_lengths, row * rows, rows)
     taps = conv_filter.astype(BF).reshape(16, 8, 1, 512).transpose(1, 0, 2, 3)
     taps = jnp.broadcast_to(taps, (8, 16, TILE, 512))
     p3, q3 = around_z(p2, 1), around_z(q2, -1)
-    tok, mine, cross = split_tokens(ids, [tokens, q1, p1, q2, p2])
-    other = [to_other_core(block) for block in after(own, p3, q3, back, ahead, taps, tok)]
-    p4 = around_z(p3, 1)
-    early = project_early(ids, tok, [q3, p3], own + other, mine, cross)
-    weight = early[1]
-    projected, tail, head, mine, cross = project_late(ids, p4, early, d_gated)
+    mine, cross = split_tokens(ids, [tokens, q1, p1, q2, p2])
+    p4 = around_z(after(p3, own), 1)
+    other = [to_other_core(block) for block in after(own, back, ahead, taps, mine)]
+    acc, weight, mine, cross = project_own(ids, [q3, p3, p4], own, mine, cross)
+    projected, tail, head, weight = project_other(ids, other, cross, acc, weight, d_gated)
     gated, d_proj, far, weight, cross = conv(
         ids, projected, tail, head, d_gated, taps, back, ahead, weight, cross
     )

time: 107 us -> 108 us (level)
  Pallas kernels: 27.9 us -> 25.5 us
  waiting for transfers between devices: 29.9 us -> 31.8 us
  starting transfers between devices: 42.8 us -> 44.4 us
    ppermute x6, waiting for transfers between devices: 5.15 us -> 10.5 us  [narrow(): return lax.ppermute(value, 'row', pairs)]
    ppermute x6, waiting for transfers between devices: 10 us -> 6.89 us  [wide(): return lax.ppermute(value, 'row', pairs)]
    pallas_call x2, Pallas kernels: 5.89 us -> 3.16 us  [the longest x1 1.63 us: project_own(): pl.pallas_call(own_kernel, in_specs=[SMEM] + [VMEM] * 3 + [HBM] * 4 + [VM...]
    ppermute x14, starting transfers between devices: 20.7 us -> 22.6 us  [around_z(): return lax.ppermute(value, ('row', 'col'), pairs)]
    ppermute x5, waiting for transfers between devices: 1.22 us -> 0.01 us  [to_other_core(): lax.ppermute(value, 'row', [(row_of(y, x, c), row_of(y, x, c + 1)) for y,...]
    pallas_call x4 -> x2, Pallas kernels: 16.1 us -> 16.5 us  [mix_call(): pl.pallas_call(kernel, in_specs=specs or [VMEM] * len(operands), out_spec...]
  transfers between devices with their start and end apart: 33 -> 33, of which waited for: 15 -> 15; matrix products, arithmetic and copies ran while one was open for 2% -> 3% of each run, Pallas kernels for 18% -> 14%
where the time goes in v3:
time: 108 us
  starting transfers between devices  44.4 us (41%)
  waiting for transfers between devices  31.8 us (29%)
  Pallas kernels  25.5 us (24%)
  other arithmetic  2.8 us (3%)
  local copies, waits for them, and re-layouts  2.08 us (2%)
    ppermute x14, starting transfers between devices, around_z(): return lax.ppermute(value, ('row', 'col'), pairs)  22.6 us
    pallas_call x2, Pallas kernels, mix_call(): pl.pallas_call(kernel, in_specs=specs or [VMEM] * len(operands), out_spec...  16.5 us
    ppermute x14, waiting for transfers between devices, around_z(): return lax.ppermute(value, ('row', 'col'), pairs)  14.3 us
    ppermute x6, waiting for transfers between devices, narrow(): return lax.ppermute(value, 'row', pairs)  10.5 us
    ppermute x6, starting transfers between devices, wide(): return lax.ppermute(value, 'row', pairs)  7.85 us
    ppermute x6, starting transfers between devices, narrow(): return lax.ppermute(value, 'row', pairs)  7.75 us
    ppermute x6, waiting for transfers between devices, wide(): return lax.ppermute(value, 'row', pairs)  6.89 us
    ppermute x2, starting transfers between devices, next_row(): lax.ppermute(value, 'row', [(r, (r + steps) % count) for r in range(count)])  5.14 us
  transfers between devices with their start and end apart: 33, of which 15 were waited for; matrix products, arithmetic and copies ran while one was open for 3% of the time, Pallas kernels for 14%

profile of v3, /device:TPU:96, one launch (start us, length us, event | category | flops | bytes accessed | tf_op | source)
XLA Modules:
  0.0 107.5 jit_solution(12059350198899035935)
XLA Ops:
  0.6 3.2 %collective-permute-start.7 = (bf16[256,512]{1,0:T(8,128)(2,1)}, bf16[256,512]{1,0:T(8,128)(2,1)S(1)}, u32[]{:S(2)}, u32[]{:S(2)}) collective-permute-start(bf16[256,512]{1,0:T(8,128)(2,1)} %refs_0_.3), channel_id=1, source_target_pairs={{0,1},{1,2},{2,3},{3,4},{4,5},{5,6},{6,7},{7,0},{8,15},{9,8},{10,9... | collective-permute-start | bytes 786440 | tf_op jit(solution)/shard_map/ppermute | solution.py:30
  3.8 2.8 %collective-permute-start = (bf16[128,512]{1,0:T(8,128)(2,1)}, bf16[128,512]{1,0:T(8,128)(2,1)S(1)}, u32[]{:S(2)}, u32[]{:S(2)}) collective-permute-start(bf16[128,512]{1,0:T(8,128)(2,1)} %refs_0_.2), channel_id=1, source_target_pairs={{0,48},{8,200},{16,0},{24,216},{32,16},{40,232},{48,32},{56,248},{... | collective-permute-start | bytes 393224 | tf_op jit(solution)/shard_map/ppermute | solution.py:38
  8.3 2.5 %collective-permute-done.refs_1_ = bf16[128,512]{1,0:T(8,128)(2,1)S(1)} collective-permute-done((bf16[128,512]{1,0:T(8,128)(2,1)}, bf16[128,512]{1,0:T(8,128)(2,1)S(1)}, u32[]{:S(2)}, u32[]{:S(2)}) %collective-permute-start) | collective-permute-done | bytes 131104 | tf_op jit(solution)/shard_map/ppermute | solution.py:38
  10.8 2.5 %collective-permute-done.1.refs_2_ = bf16[128,512]{1,0:T(8,128)(2,1)S(1)} collective-permute-done((bf16[128,512]{1,0:T(8,128)(2,1)}, bf16[128,512]{1,0:T(8,128)(2,1)S(1)}, u32[]{:S(2)}, u32[]{:S(2)}) %collective-permute-start.1) | collective-permute-done | bytes 131104 | tf_op jit(solution)/shard_map/ppermute | solution.py:38
  13.4 1.3 %collective-permute-done.2.refs_3_ = bf16[128,512]{1,0:T(8,128)(2,1)S(1)} collective-permute-done((bf16[128,512]{1,0:T(8,128)(2,1)}, bf16[128,512]{1,0:T(8,128)(2,1)S(1)}, u32[]{:S(2)}, u32[]{:S(2)}) %collective-permute-start.2) | collective-permute-done | bytes 131104 | tf_op jit(solution)/shard_map/ppermute | solution.py:38
  15.6 1.1 %collective-permute-start.9 = (bf16[256,512]{1,0:T(8,128)(2,1)S(1)}, bf16[256,512]{1,0:T(8,128)(2,1)S(1)}, u32[]{:S(2)}, u32[]{:S(2)}) collective-permute-start(bf16[256,512]{1,0:T(8,128)(2,1)S(1)} %collective-permute-done.7.refs_2_), channel_id=1, source_target_pairs={{0,1},{1,2},{2,3},{3,4},{4,5},{5,6},{6,7},{7,0},{8,15},{9,8},{10,9... | collective-permute-start | bytes 786440 | tf_op jit(solution)/shard_map/ppermute | solution.py:30
  16.7 3.0 %collective-permute-start.3 = (bf16[4,128,512]{2,1,0:T(8,128)(2,1)S(1)}, bf16[4,128,512]{2,1,0:T(8,128)(2,1)S(1)}, u32[]{:S(2)}, u32[]{:S(2)}) collective-permute-start(bf16[4,128,512]{2,1,0:T(8,128)(2,1)S(1)} %stack.21.refs_3_), channel_id=1, source_target_pairs={{0,192},{8,56},{16,208},{24,8},{32,224},{40,24},{48,240},{56,40},{... | collective-permute-start | bytes 1572872 | tf_op jit(solution)/shard_map/ppermute | solution.py:46
  21.4 1.0 collective-permute-start.8
  24.1 2.7 %collective-permute-start.15 = (bf16[256,512]{1,0:T(8,128)(2,1)S(1)}, bf16[256,512]{1,0:T(8,128)(2,1)S(1)}, u32[]{:S(2)}, u32[]{:S(2)}) collective-permute-start(bf16[256,512]{1,0:T(8,128)(2,1)S(1)} %collective-permute-done.9.refs_4_), channel_id=1, source_target_pairs={{0,1},{1,2},{2,3},{3,4},{4,5},{5,6},{6,7},{7,0},{8,15},{9,8},{10,9... | collective-permute-start | bytes 786440 | tf_op jit(solution)/shard_map/ppermute | solution.py:30
  27.7 1.3 %collective-permute-done.8.refs_3_ = bf16[256,512]{1,0:T(8,128)(2,1)S(1)} collective-permute-done((bf16[256,512]{1,0:T(8,128)(2,1)S(1)}, bf16[256,512]{1,0:T(8,128)(2,1)S(1)}, u32[]{:S(2)}, u32[]{:S(2)}) %collective-permute-start.8) | collective-permute-done | bytes 262176 | tf_op jit(solution)/shard_map/ppermute | solution.py:30
  29.2 2.9 %collective-permute-done.3.refs_4_ = bf16[4,128,512]{2,1,0:T(8,128)(2,1)S(1)} collective-permute-done((bf16[4,128,512]{2,1,0:T(8,128)(2,1)S(1)}, bf16[4,128,512]{2,1,0:T(8,128)(2,1)S(1)}, u32[]{:S(2)}, u32[]{:S(2)}) %collective-permute-start.3) | collective-permute-done | bytes 524320 | tf_op jit(solution)/shard_map/ppermute | solution.py:46
  32.1 4.0 %collective-permute-done.5.refs_6_ = bf16[4,128,512]{2,1,0:T(8,128)(2,1)S(1)} collective-permute-done((bf16[4,128,512]{2,1,0:T(8,128)(2,1)S(1)}, bf16[4,128,512]{2,1,0:T(8,128)(2,1)S(1)}, u32[]{:S(2)}, u32[]{:S(2)}) %collective-permute-start.5) | collective-permute-done | bytes 524320 | tf_op jit(solution)/shard_map/ppermute | solution.py:46
  36.1 1.0 collective-permute-start.16
  39.4 3.0 %collective-permute-done.16.refs_2_ = bf16[256,512]{1,0:T(8,128)(2,1)S(1)} collective-permute-done((bf16[256,512]{1,0:T(8,128)(2,1)S(1)}, bf16[256,512]{1,0:T(8,128)(2,1)S(1)}, u32[]{:S(2)}, u32[]{:S(2)}) %collective-permute-start.16) | collective-permute-done | bytes 262176 | tf_op jit(solution)/shard_map/ppermute | solution.py:30
  42.4 1.6 %project_own.1 = (f32[256,512]{1,0:T(8,128)S(1)}, bf16[4,4,2,128,512]{4,3,2,1,0:T(8,128)(2,1)S(1)}, bf16[8,256,256]{2,1,0:T(8,128)(2,1)S(1)}, bf16[10,256,256]{2,1,0:T(8,128)(2,1)S(1)}) custom-call(s32[4]{0:T(128)S(1)} %pad_add_fusion.ids, bf16[256,512]{1,0:T(8,128)(2,1)S(1)} %collective-permute-done.14.refs_0_, ...), custom_call_target="tpu_custom_call", output_to_operand_aliasing={{2}: (8, {}), {3}: (9, {})} | custom-call | flops 4294967296 | bytes 4194304 | tf_op jit(solution)/shard_map/project_own/pallas_call | solution.py:224
  44.1 1.5 %project_other.1 = (bf16[256,512]{1,0:T(8,128)(2,1)S(1)}, bf16[128,512]{1,0:T(8,128)(2,1)S(1)}, bf16[128,512]{1,0:T(8,128)(2,1)S(1)}, bf16[4,4,2,128,512]{4,3,2,1,0:T(8,128)(2,1)S(1)}) custom-call(s32[4]{0:T(128)S(1)} %pad_add_fusion.ids, bf16[4,128,512]{2,1,0:T(8,128)(2,1)S(1)} %collective-permute-done.10.refs_0_, ...), custom_call_target="tpu_custom_call", output_to_operand_aliasing={{3}: (7, {})} | custom-call | flops 1073741824 | bytes 4194304 | tf_op jit(solution)/shard_map/project_other/pallas_call | solution.py:255
  45.8 5.1 %collective-permute-start.18 = (bf16[128,512]{1,0:T(8,128)(2,1)S(1)}, bf16[128,512]{1,0:T(8,128)(2,1)S(1)}, u32[]{:S(2)}, u32[]{:S(2)}) collective-permute-start(bf16[128,512]{1,0:T(8,128)(2,1)S(1)} %get-tuple-element.69), channel_id=1, source_target_pairs={{0,248},{8,0},{16,8},{24,16},{32,24},{40,32},{48,40},{56,48},{64,5... | collective-permute-start | bytes 393224 | tf_op jit(solution)/shard_map/ppermute | solution.py:55
  50.8 7.5 %inside.1 = (bf16[128,512]{1,0:T(8,128)(2,1)S(1)}, f32[128,512]{1,0:T(8,128)S(1)}, f32[128,512]{1,0:T(8,128)S(1)}, f32[128,512]{1,0:T(8,128)S(1)}) custom-call(bf16[256,512]{1,0:T(8,128)(2,1)S(1)} %get-tuple-element.67.p_ref, bf16[256,512]{1,0:T(8,128)(2,1)S(1)} %copy-done.1, bf16[8,16,16,512]{3,2,1,0:T(8,128)(2,1)S(1)} %broadcast_in_dim.46.taps_ref, ...), custom_call_target="tpu_custom_call" | custom-call | flops 4294967296 | bytes 4194304 | tf_op jit(solution)/shard_map/inside/pallas_call | solution.py:343
  58.3 9.0 %edges.1 = (bf16[256,512]{1,0:T(8,128)(2,1)}, bf16[256,512]{1,0:T(8,128)(2,1)S(1)}, bf16[256,512]{1,0:T(8,128)(2,1)S(1)}, bf16[4,4,2,128,512]{4,3,2,1,0:T(8,128)(2,1)S(1)}, bf16[10,256,256]{2,1,0:T(8,128)(2,1)S(1)}) custom-call(bf16[256,512]{1,0:T(8,128)(2,1)S(1)} %get-tuple-element.67.p_ref, ...), custom_call_target="tpu_custom_call", output_to_operand_aliasing={{4}: (13, {})} | custom-call | flops 4294967296 | bytes 4194304 | tf_op jit(solution)/shard_map/edges/pallas_call | solution.py:343
  67.4 2.3 %collective-permute-start.20 = (bf16[256,512]{1,0:T(8,128)(2,1)S(1)}, bf16[256,512]{1,0:T(8,128)(2,1)S(1)}, u32[]{:S(2)}, u32[]{:S(2)}) collective-permute-start(bf16[256,512]{1,0:T(8,128)(2,1)S(1)} %get-tuple-element.87), channel_id=1, source_target_pairs={{0,1},{1,2},{2,3},{3,4},{4,5},{5,6},{6,7},{7,0},{8,15},{9,8},{10,9... | collective-permute-start | bytes 786440 | tf_op jit(solution)/shard_map/ppermute | solution.py:30
  69.7 1.7 %near_terms.1 = (bf16[256,512]{1,0:T(8,128)(2,1)S(1)}, bf16[256,512]{1,0:T(8,128)(2,1)S(1)}, bf16[256,512]{1,0:T(8,128)(2,1)S(1)}, bf16[256,512]{1,0:T(8,128)(2,...) custom-call(s32[4]{0:T(128)S(1)} %pad_add_fusion.ids, ...), custom_call_target="tpu_custom_call" | custom-call | flops 939524096 | bytes 6291456 | tf_op jit(solution)/shard_map/near_terms/pallas_call | solution.py:385
  71.5 2.0 %weight_terms.1 = (bf16[4,128,512]{2,1,0:T(8,128)(2,1)S(1)}, bf16[4,128,512]{2,1,0:T(8,128)(2,1)S(1)}, bf16[4,128,512]{2,1,0:T(8,128)(2,1)S(1)}, bf16[4,128,512]{2,1,0:T(8,128)(2,1)S(1)}) custom-call(s32[4]{0:T(128)S(1)} %pad_add_fusion.ids, bf16[8,256,256]{2,1,0:T(8,128)(2,1)S(1)} %get-tuple-element.82.mine, ...), custom_call_target="tpu_custom_call" | custom-call | flops 1073741824 | bytes 5242880 | tf_op jit(solution)/shard_map/weight_terms/pallas_call | solution.py:432
  73.5 1.1 %collective-permute-done.20.b = bf16[256,512]{1,0:T(8,128)(2,1)S(1)} collective-permute-done((bf16[256,512]{1,0:T(8,128)(2,1)S(1)}, bf16[256,512]{1,0:T(8,128)(2,1)S(1)}, u32[]{:S(2)}, u32[]{:S(2)}) %collective-permute-start.20) | collective-permute-done | bytes 262176 | tf_op jit(solution)/shard_map/ppermute | solution.py:30
  74.7 3.5 %collective-permute-start.21 = (bf16[256,512]{1,0:T(8,128)(2,1)S(1)}, bf16[256,512]{1,0:T(8,128)(2,1)S(1)}, u32[]{:S(2)}, u32[]{:S(2)}) collective-permute-start(bf16[256,512]{1,0:T(8,128)(2,1)S(1)} %add.69), channel_id=1, source_target_pairs={{0,1},{1,2},{2,3},{3,4},{4,5},{5,6},{6,7},{7,0},{8,15},{9,8},{10,9... | collective-permute-start | bytes 786440 | tf_op jit(solution)/shard_map/ppermute | solution.py:30
  79.1 2.4 %collective-permute-start.29 = (bf16[4,128,512]{2,1,0:T(8,128)(2,1)S(1)}, bf16[4,128,512]{2,1,0:T(8,128)(2,1)S(1)}, u32[]{:S(2)}, u32[]{:S(2)}) collective-permute-start(bf16[4,128,512]{2,1,0:T(8,128)(2,1)S(1)} %get-tuple-element.94), channel_id=1, source_target_pairs={{0,192},{8,56},{16,208},{24,8},{32,224},{40,24},{48,240},{56,40},{... | collective-permute-start | bytes 1572872 | tf_op jit(solution)/shard_map/ppermute | solution.py:46
  81.6 2.2 %collective-permute-done.21.b = bf16[256,512]{1,0:T(8,128)(2,1)S(1)} collective-permute-done((bf16[256,512]{1,0:T(8,128)(2,1)S(1)}, bf16[256,512]{1,0:T(8,128)(2,1)S(1)}, u32[]{:S(2)}, u32[]{:S(2)}) %collective-permute-start.21) | collective-permute-done | bytes 262176 | tf_op jit(solution)/shard_map/ppermute | solution.py:30
  83.9 3.8 %collective-permute-start.22 = (bf16[256,512]{1,0:T(8,128)(2,1)S(1)}, bf16[256,512]{1,0:T(8,128)(2,1)S(1)}, u32[]{:S(2)}, u32[]{:S(2)}) collective-permute-start(bf16[256,512]{1,0:T(8,128)(2,1)S(1)} %add.70), channel_id=1, source_target_pairs={{0,1},{1,2},{2,3},{3,4},{4,5},{5,6},{6,7},{7,0},{8,15},{9,8},{10,9... | collective-permute-start | bytes 786440 | tf_op jit(solution)/shard_map/ppermute | solution.py:30
  87.6 3.7 %collective-permute-done.25.b = bf16[256,512]{1,0:T(8,128)(2,1)S(1)} collective-permute-done((bf16[256,512]{1,0:T(8,128)(2,1)S(1)}, bf16[256,512]{1,0:T(8,128)(2,1)S(1)}, u32[]{:S(2)}, u32[]{:S(2)}) %collective-permute-start.25) | collective-permute-done | bytes 262176 | tf_op jit(solution)/shard_map/ppermute | solution.py:30
  91.4 2.6 %collective-permute-done.22.b = bf16[256,512]{1,0:T(8,128)(2,1)S(1)} collective-permute-done((bf16[256,512]{1,0:T(8,128)(2,1)S(1)}, bf16[256,512]{1,0:T(8,128)(2,1)S(1)}, u32[]{:S(2)}, u32[]{:S(2)}) %collective-permute-start.22) | collective-permute-done | bytes 262176 | tf_op jit(solution)/shard_map/ppermute | solution.py:30
  94.1 3.8 %collective-permute-start.23 = (bf16[256,512]{1,0:T(8,128)(2,1)S(1)}, bf16[256,512]{1,0:T(8,128)(2,1)S(1)}, u32[]{:S(2)}, u32[]{:S(2)}) collective-permute-start(bf16[256,512]{1,0:T(8,128)(2,1)S(1)} %add.71), channel_id=1, source_target_pairs={{0,1},{1,2},{2,3},{3,4},{4,5},{5,6},{6,7},{7,0},{8,15},{9,8},{10,9... | collective-permute-start | bytes 786440 | tf_op jit(solution)/shard_map/ppermute | solution.py:30
  98.4 3.1 %collective-permute-start.32 = (bf16[128,512]{1,0:T(8,128)(2,1)S(1)}, bf16[128,512]{1,0:T(8,128)(2,1)S(1)}, u32[]{:S(2)}, u32[]{:S(2)}) collective-permute-start(bf16[128,512]{1,0:T(8,128)(2,1)S(1)} %get-tuple-element.98), channel_id=1, source_target_pairs={{0,48},{8,200},{16,0},{24,216},{32,16},{40,232},{48,32},{56,248},{... | collective-permute-start | bytes 393224 | tf_op jit(solution)/shard_map/ppermute | solution.py:38
  102.6 3.2 %collective-permute-done.30 = bf16[128,512]{1,0:T(8,128)(2,1)S(1)} collective-permute-done((bf16[128,512]{1,0:T(8,128)(2,1)S(1)}, bf16[128,512]{1,0:T(8,128)(2,1)S(1)}, u32[]{:S(2)}, u32[]{:S(2)}) %collective-permute-start.30) | collective-permute-done | bytes 131104 | tf_op jit(solution)/shard_map/ppermute | solution.py:38
  (69 shorter events, 14.2 us)
Async XLA Ops:
  0.6 15.0 %collective-permute-start.7 = (bf16[256,512]{1,0:T(8,128)(2,1)}, bf16[256,512]{1,0:T(8,128)(2,1)S(1)}, u32[]{:S(2)}, u32[]{:S(2)}) collective-permute-start(bf16[256,512]{1,0:T(8,128)(2,1)} %refs_0_.3), channel_id=1, source_target_pairs={{0,1},{1,2},{2,3},{3,4},{4,5},{5,6},{6,7},{7,0},{8,15},{9,8},{10,9... | collective-permute-start | bytes 786440 | tf_op jit(solution)/shard_map/ppermute | solution.py:30
  3.8 7.0 %collective-permute-start = (bf16[128,512]{1,0:T(8,128)(2,1)}, bf16[128,512]{1,0:T(8,128)(2,1)S(1)}, u32[]{:S(2)}, u32[]{:S(2)}) collective-permute-start(bf16[128,512]{1,0:T(8,128)(2,1)} %refs_0_.2), channel_id=1, source_target_pairs={{0,48},{8,200},{16,0},{24,216},{32,16},{40,232},{48,32},{56,248},{... | collective-permute-start | bytes 393224 | tf_op jit(solution)/shard_map/ppermute | solution.py:38
  6.6 6.8 %collective-permute-start.1 = (bf16[128,512]{1,0:T(8,128)(2,1)}, bf16[128,512]{1,0:T(8,128)(2,1)S(1)}, u32[]{:S(2)}, u32[]{:S(2)}) collective-permute-start(bf16[128,512]{1,0:T(8,128)(2,1)} %refs_0_.2), channel_id=1, source_target_pairs={{0,32},{8,136},{16,48},{24,152},{32,0},{40,168},{48,16},{56,184},{... | collective-permute-start | bytes 393224 | tf_op jit(solution)/shard_map/ppermute | solution.py:38
  7.4 7.3 %collective-permute-start.2 = (bf16[128,512]{1,0:T(8,128)(2,1)}, bf16[128,512]{1,0:T(8,128)(2,1)S(1)}, u32[]{:S(2)}, u32[]{:S(2)}) collective-permute-start(bf16[128,512]{1,0:T(8,128)(2,1)} %refs_0_.2), channel_id=1, source_target_pairs={{0,16},{8,72},{16,32},{24,88},{32,48},{40,104},{48,0},{56,120},{64... | collective-permute-start | bytes 393224 | tf_op jit(solution)/shard_map/ppermute | solution.py:38
  8.3 13.1 %collective-permute-start.6 = (bf16[256,512]{1,0:T(8,128)(2,1)}, bf16[256,512]{1,0:T(8,128)(2,1)S(1)}, u32[]{:S(2)}, u32[]{:S(2)}) collective-permute-start(bf16[256,512]{1,0:T(8,128)(2,1)} %refs_0_.3), channel_id=1, source_target_pairs={{0,7},{1,0},{2,1},{3,2},{4,3},{5,4},{6,5},{7,6},{8,9},{9,10},{10,1... | collective-permute-start | bytes 786440 | tf_op jit(solution)/shard_map/ppermute | solution.py:30
  15.6 8.4 %collective-permute-start.9 = (bf16[256,512]{1,0:T(8,128)(2,1)S(1)}, bf16[256,512]{1,0:T(8,128)(2,1)S(1)}, u32[]{:S(2)}, u32[]{:S(2)}) collective-permute-start(bf16[256,512]{1,0:T(8,128)(2,1)S(1)} %collective-permute-done.7.refs_2_), channel_id=1, source_target_pairs={{0,1},{1,2},{2,3},{3,4},{4,5},{5,6},{6,7},{7,0},{8,15},{9,8},{10,9... | collective-permute-start | bytes 786440 | tf_op jit(solution)/shard_map/ppermute | solution.py:30
  16.7 15.3 %collective-permute-start.3 = (bf16[4,128,512]{2,1,0:T(8,128)(2,1)S(1)}, bf16[4,128,512]{2,1,0:T(8,128)(2,1)S(1)}, u32[]{:S(2)}, u32[]{:S(2)}) collective-permute-start(bf16[4,128,512]{2,1,0:T(8,128)(2,1)S(1)} %stack.21.refs_3_), channel_id=1, source_target_pairs={{0,192},{8,56},{16,208},{24,8},{32,224},{40,24},{48,240},{56,40},{... | collective-permute-start | bytes 1572872 | tf_op jit(solution)/shard_map/ppermute | solution.py:46
  19.8 12.3 %collective-permute-start.4 = (bf16[4,128,512]{2,1,0:T(8,128)(2,1)S(1)}, bf16[4,128,512]{2,1,0:T(8,128)(2,1)S(1)}, u32[]{:S(2)}, u32[]{:S(2)}) collective-permute-start(bf16[4,128,512]{2,1,0:T(8,128)(2,1)S(1)} %stack.21.refs_3_), channel_id=1, source_target_pairs={{0,128},{8,40},{16,144},{24,56},{32,160},{40,8},{48,176},{56,24},{... | collective-permute-start | bytes 1572872 | tf_op jit(solution)/shard_map/ppermute | solution.py:46
  20.4 15.7 %collective-permute-start.5 = (bf16[4,128,512]{2,1,0:T(8,128)(2,1)S(1)}, bf16[4,128,512]{2,1,0:T(8,128)(2,1)S(1)}, u32[]{:S(2)}, u32[]{:S(2)}) collective-permute-start(bf16[4,128,512]{2,1,0:T(8,128)(2,1)S(1)} %stack.21.refs_3_), channel_id=1, source_target_pairs={{0,64},{8,24},{16,80},{24,40},{32,96},{40,56},{48,112},{56,8},{64,... | collective-permute-start | bytes 1572872 | tf_op jit(solution)/shard_map/ppermute | solution.py:46
  21.4 7.7 %collective-permute-start.8 = (bf16[256,512]{1,0:T(8,128)(2,1)S(1)}, bf16[256,512]{1,0:T(8,128)(2,1)S(1)}, u32[]{:S(2)}, u32[]{:S(2)}) collective-permute-start(bf16[256,512]{1,0:T(8,128)(2,1)S(1)} %collective-permute-done.6.refs_1_), channel_id=1, source_target_pairs={{0,7},{1,0},{2,1},{3,2},{4,3},{5,4},{6,5},{7,6},{8,9},{9,10},{10,1... | collective-permute-start | bytes 786440 | tf_op jit(solution)/shard_map/ppermute | solution.py:30
  24.1 12.0 %collective-permute-start.15 = (bf16[256,512]{1,0:T(8,128)(2,1)S(1)}, bf16[256,512]{1,0:T(8,128)(2,1)S(1)}, u32[]{:S(2)}, u32[]{:S(2)}) collective-permute-start(bf16[256,512]{1,0:T(8,128)(2,1)S(1)} %collective-permute-done.9.refs_4_), channel_id=1, source_target_pairs={{0,1},{1,2},{2,3},{3,4},{4,5},{5,6},{6,7},{7,0},{8,15},{9,8},{10,9... | collective-permute-start | bytes 786440 | tf_op jit(solution)/shard_map/ppermute | solution.py:30
  29.0 10.1 %collective-permute-start.14 = (bf16[256,512]{1,0:T(8,128)(2,1)S(1)}, bf16[256,512]{1,0:T(8,128)(2,1)S(1)}, u32[]{:S(2)}, u32[]{:S(2)}) collective-permute-start(bf16[256,512]{1,0:T(8,128)(2,1)S(1)} %collective-permute-done.8.refs_3_), channel_id=1, source_target_pairs={{0,7},{1,0},{2,1},{3,2},{4,3},{5,4},{6,5},{7,6},{8,9},{9,10},{10,1... | collective-permute-start | bytes 786440 | tf_op jit(solution)/shard_map/ppermute | solution.py:30
  36.1 6.4 %collective-permute-start.16 = (bf16[256,512]{1,0:T(8,128)(2,1)S(1)}, bf16[256,512]{1,0:T(8,128)(2,1)S(1)}, u32[]{:S(2)}, u32[]{:S(2)}) collective-permute-start(bf16[256,512]{1,0:T(8,128)(2,1)S(1)} %collective-permute-done.15.refs_1_), channel_id=1, source_target_pairs={{0,1},{1,2},{2,3},{3,4},{4,5},{5,6},{6,7},{7,0},{8,15},{9,8},{10,9... | collective-permute-start | bytes 786440 | tf_op jit(solution)/shard_map/ppermute | solution.py:30
  38.3 5.8 %collective-permute-start.10 = (bf16[4,128,512]{2,1,0:T(8,128)(2,1)S(1)}, bf16[4,128,512]{2,1,0:T(8,128)(2,1)S(1)}, u32[]{:S(2)}, u32[]{:S(2)}) collective-permute-start(bf16[4,128,512]{2,1,0:T(8,128)(2,1)S(1)} %stack.21.refs_3_), channel_id=1, source_target_pairs={{0,8},{8,0},{16,24},{24,16},{32,40},{40,32},{48,56},{56,48},{64,72... | collective-permute-start | bytes 1572872 | tf_op jit(solution)/shard_map/ppermute | solution.py:50
  38.4 5.7 %collective-permute-start.11 = (bf16[4,128,512]{2,1,0:T(8,128)(2,1)S(1)}, bf16[4,128,512]{2,1,0:T(8,128)(2,1)S(1)}, u32[]{:S(2)}, u32[]{:S(2)}) collective-permute-start(bf16[4,128,512]{2,1,0:T(8,128)(2,1)S(1)} %collective-permute-done.3.refs_4_), channel_id=1, source_target_pairs={{0,8},{8,0},{16,24},{24,16},{32,40},{40,32},{48,56},{56,48},{64,72... | collective-permute-start | bytes 1572872 | tf_op jit(solution)/shard_map/ppermute | solution.py:50
  38.9 5.2 %collective-permute-start.12 = (bf16[4,128,512]{2,1,0:T(8,128)(2,1)S(1)}, bf16[4,128,512]{2,1,0:T(8,128)(2,1)S(1)}, u32[]{:S(2)}, u32[]{:S(2)}) collective-permute-start(bf16[4,128,512]{2,1,0:T(8,128)(2,1)S(1)} %collective-permute-done.4.refs_5_), channel_id=1, source_target_pairs={{0,8},{8,0},{16,24},{24,16},{32,40},{40,32},{48,56},{56,48},{64,72... | collective-permute-start | bytes 1572872 | tf_op jit(solution)/shard_map/ppermute | solution.py:50
  39.1 5.0 %collective-permute-start.13 = (bf16[4,128,512]{2,1,0:T(8,128)(2,1)S(1)}, bf16[4,128,512]{2,1,0:T(8,128)(2,1)S(1)}, u32[]{:S(2)}, u32[]{:S(2)}) collective-permute-start(bf16[4,128,512]{2,1,0:T(8,128)(2,1)S(1)} %collective-permute-done.5.refs_6_), channel_id=1, source_target_pairs={{0,8},{8,0},{16,24},{24,16},{32,40},{40,32},{48,56},{56,48},{64,72... | collective-permute-start | bytes 1572872 | tf_op jit(solution)/shard_map/ppermute | solution.py:50
  45.7 12.6 %collective-permute-start.17 = (bf16[128,512]{1,0:T(8,128)(2,1)S(1)}, bf16[128,512]{1,0:T(8,128)(2,1)S(1)}, u32[]{:S(2)}, u32[]{:S(2)}) collective-permute-start(bf16[128,512]{1,0:T(8,128)(2,1)S(1)} %get-tuple-element.68), channel_id=1, source_target_pairs={{0,8},{8,16},{16,24},{24,32},{32,40},{40,48},{48,56},{56,64},{64,7... | collective-permute-start | bytes 393224 | tf_op jit(solution)/shard_map/ppermute | solution.py:55
  45.8 12.5 %collective-permute-start.18 = (bf16[128,512]{1,0:T(8,128)(2,1)S(1)}, bf16[128,512]{1,0:T(8,128)(2,1)S(1)}, u32[]{:S(2)}, u32[]{:S(2)}) collective-permute-start(bf16[128,512]{1,0:T(8,128)(2,1)S(1)} %get-tuple-element.69), channel_id=1, source_target_pairs={{0,248},{8,0},{16,8},{24,16},{32,24},{40,32},{48,40},{56,48},{64,5... | collective-permute-start | bytes 393224 | tf_op jit(solution)/shard_map/ppermute | solution.py:55
  67.4 7.2 %collective-permute-start.20 = (bf16[256,512]{1,0:T(8,128)(2,1)S(1)}, bf16[256,512]{1,0:T(8,128)(2,1)S(1)}, u32[]{:S(2)}, u32[]{:S(2)}) collective-permute-start(bf16[256,512]{1,0:T(8,128)(2,1)S(1)} %get-tuple-element.87), channel_id=1, source_target_pairs={{0,1},{1,2},{2,3},{3,4},{4,5},{5,6},{6,7},{7,0},{8,15},{9,8},{10,9... | collective-permute-start | bytes 786440 | tf_op jit(solution)/shard_map/ppermute | solution.py:30
  71.4 10.0 %collective-permute-start.24 = (bf16[256,512]{1,0:T(8,128)(2,1)S(1)}, bf16[256,512]{1,0:T(8,128)(2,1)S(1)}, u32[]{:S(2)}, u32[]{:S(2)}) collective-permute-start(bf16[256,512]{1,0:T(8,128)(2,1)S(1)} %get-tuple-element.90), channel_id=1, source_target_pairs={{0,7},{1,0},{2,1},{3,2},{4,3},{5,4},{6,5},{7,6},{8,9},{9,10},{10,1... | collective-permute-start | bytes 786440 | tf_op jit(solution)/shard_map/ppermute | solution.py:30
  74.7 9.1 %collective-permute-start.21 = (bf16[256,512]{1,0:T(8,128)(2,1)S(1)}, bf16[256,512]{1,0:T(8,128)(2,1)S(1)}, u32[]{:S(2)}, u32[]{:S(2)}) collective-permute-start(bf16[256,512]{1,0:T(8,128)(2,1)S(1)} %add.69), channel_id=1, source_target_pairs={{0,1},{1,2},{2,3},{3,4},{4,5},{5,6},{6,7},{7,0},{8,15},{9,8},{10,9... | collective-permute-start | bytes 786440 | tf_op jit(solution)/shard_map/ppermute | solution.py:30
  78.2 19.7 %collective-permute-start.27 = (bf16[4,128,512]{2,1,0:T(8,128)(2,1)S(1)}, bf16[4,128,512]{2,1,0:T(8,128)(2,1)S(1)}, u32[]{:S(2)}, u32[]{:S(2)}) collective-permute-start(bf16[4,128,512]{2,1,0:T(8,128)(2,1)S(1)} %get-tuple-element.92), channel_id=1, source_target_pairs={{0,64},{8,24},{16,80},{24,40},{32,96},{40,56},{48,112},{56,8},{64,... | collective-permute-start | bytes 1572872 | tf_op jit(solution)/shard_map/ppermute | solution.py:46
  78.2 19.7 %collective-permute-start.28 = (bf16[4,128,512]{2,1,0:T(8,128)(2,1)S(1)}, bf16[4,128,512]{2,1,0:T(8,128)(2,1)S(1)}, u32[]{:S(2)}, u32[]{:S(2)}) collective-permute-start(bf16[4,128,512]{2,1,0:T(8,128)(2,1)S(1)} %get-tuple-element.93), channel_id=1, source_target_pairs={{0,128},{8,40},{16,144},{24,56},{32,160},{40,8},{48,176},{56,24},{... | collective-permute-start | bytes 1572872 | tf_op jit(solution)/shard_map/ppermute | solution.py:46
  79.1 18.8 %collective-permute-start.29 = (bf16[4,128,512]{2,1,0:T(8,128)(2,1)S(1)}, bf16[4,128,512]{2,1,0:T(8,128)(2,1)S(1)}, u32[]{:S(2)}, u32[]{:S(2)}) collective-permute-start(bf16[4,128,512]{2,1,0:T(8,128)(2,1)S(1)} %get-tuple-element.94), channel_id=1, source_target_pairs={{0,192},{8,56},{16,208},{24,8},{32,224},{40,24},{48,240},{56,40},{... | collective-permute-start | bytes 1572872 | tf_op jit(solution)/shard_map/ppermute | solution.py:46
  81.5 9.8 %collective-permute-start.25 = (bf16[256,512]{1,0:T(8,128)(2,1)S(1)}, bf16[256,512]{1,0:T(8,128)(2,1)S(1)}, u32[]{:S(2)}, u32[]{:S(2)}) collective-permute-start(bf16[256,512]{1,0:T(8,128)(2,1)S(1)} %add.72), channel_id=1, source_target_pairs={{0,7},{1,0},{2,1},{3,2},{4,3},{5,4},{6,5},{7,6},{8,9},{9,10},{10,1... | collective-permute-start | bytes 786440 | tf_op jit(solution)/shard_map/ppermute | solution.py:30
  83.9 10.2 %collective-permute-start.22 = (bf16[256,512]{1,0:T(8,128)(2,1)S(1)}, bf16[256,512]{1,0:T(8,128)(2,1)S(1)}, u32[]{:S(2)}, u32[]{:S(2)}) collective-permute-start(bf16[256,512]{1,0:T(8,128)(2,1)S(1)} %add.70), channel_id=1, source_target_pairs={{0,1},{1,2},{2,3},{3,4},{4,5},{5,6},{6,7},{7,0},{8,15},{9,8},{10,9... | collective-permute-start | bytes 786440 | tf_op jit(solution)/shard_map/ppermute | solution.py:30
  91.3 10.1 %collective-permute-start.26 = (bf16[256,512]{1,0:T(8,128)(2,1)S(1)}, bf16[256,512]{1,0:T(8,128)(2,1)S(1)}, u32[]{:S(2)}, u32[]{:S(2)}) collective-permute-start(bf16[256,512]{1,0:T(8,128)(2,1)S(1)} %add.73), channel_id=1, source_target_pairs={{0,7},{1,0},{2,1},{3,2},{4,3},{5,4},{6,5},{7,6},{8,9},{9,10},{10,1... | collective-permute-start | bytes 786440 | tf_op jit(solution)/shard_map/ppermute | solution.py:30
  94.1 7.7 %collective-permute-start.23 = (bf16[256,512]{1,0:T(8,128)(2,1)S(1)}, bf16[256,512]{1,0:T(8,128)(2,1)S(1)}, u32[]{:S(2)}, u32[]{:S(2)}) collective-permute-start(bf16[256,512]{1,0:T(8,128)(2,1)S(1)} %add.71), channel_id=1, source_target_pairs={{0,1},{1,2},{2,3},{3,4},{4,5},{5,6},{6,7},{7,0},{8,15},{9,8},{10,9... | collective-permute-start | bytes 786440 | tf_op jit(solution)/shard_map/ppermute | solution.py:30
  98.2 7.7 %collective-permute-start.30 = (bf16[128,512]{1,0:T(8,128)(2,1)S(1)}, bf16[128,512]{1,0:T(8,128)(2,1)S(1)}, u32[]{:S(2)}, u32[]{:S(2)}) collective-permute-start(bf16[128,512]{1,0:T(8,128)(2,1)S(1)} %get-tuple-element.96), channel_id=1, source_target_pairs={{0,16},{8,72},{16,32},{24,88},{32,48},{40,104},{48,0},{56,120},{64... | collective-permute-start | bytes 393224 | tf_op jit(solution)/shard_map/ppermute | solution.py:38
  98.3 7.6 %collective-permute-start.31 = (bf16[128,512]{1,0:T(8,128)(2,1)S(1)}, bf16[128,512]{1,0:T(8,128)(2,1)S(1)}, u32[]{:S(2)}, u32[]{:S(2)}) collective-permute-start(bf16[128,512]{1,0:T(8,128)(2,1)S(1)} %get-tuple-element.97), channel_id=1, source_target_pairs={{0,32},{8,136},{16,48},{24,152},{32,0},{40,168},{48,16},{56,184},{... | collective-permute-start | bytes 393224 | tf_op jit(solution)/shard_map/ppermute | solution.py:38
  98.4 8.4 %collective-permute-start.32 = (bf16[128,512]{1,0:T(8,128)(2,1)S(1)}, bf16[128,512]{1,0:T(8,128)(2,1)S(1)}, u32[]{:S(2)}, u32[]{:S(2)}) collective-permute-start(bf16[128,512]{1,0:T(8,128)(2,1)S(1)} %get-tuple-element.98), channel_id=1, source_target_pairs={{0,48},{8,200},{16,0},{24,216},{32,16},{40,232},{48,32},{56,248},{... | collective-permute-start | bytes 393224 | tf_op jit(solution)/shard_map/ppermute | solution.py:38
  (4 other events, 43.3 us)

commit v4 on v3

--- a/solution.py
+++ b/solution.py
@@ -278,14 +278,18 @@
         for u in range(8):
             at = slice(TILE * u, TILE * u + TILE)
             live = live_ref[at] - b.astype(F32).astype(BF)
-            total = None
+            sums = []
             for k in range(16):
                 v = u + k // 2 if reverse else u + 8 - k // 2
                 source = (odd if k % 2 else even)[TILE * v : TILE * v + TILE]
                 m = jnp.minimum(jnp.maximum(live - jnp.array(8 * k - 1, BF), zero), one)
                 term = source * taps_ref[b, k] * jnp.concatenate([m] * 4, 1)
-                total = term if total is None else total + term
-            acc[at] += total.astype(F32)
+                level = k
+                while level % 2:
+                    term = sums.pop() + term
+                    level //= 2
+                sums.append(term)
+            acc[at] += sums[0].astype(F32)
 
     loop(8, shift)
 

time: 108 us -> 108 us (level)
  no operation moved by 1% of the time
where the time goes in v4:
time: 108 us; the launch traced here: 107 us
  starting transfers between devices  44.4 us (41%)
  waiting for transfers between devices  31.8 us (29%)
  Pallas kernels  25.4 us (24%)
  other arithmetic  2.8 us (3%)
  local copies, waits for them, and re-layouts  2.08 us (2%)
    ppermute x14, starting transfers between devices, around_z(): return lax.ppermute(value, ('row', 'col'), pairs)  22.6 us
    pallas_call x2, Pallas kernels, mix_call(): pl.pallas_call(kernel, in_specs=specs or [VMEM] * len(operands), out_spec...  16.4 us
    ppermute x14, waiting for transfers between devices, around_z(): return lax.ppermute(value, ('row', 'col'), pairs)  14.3 us
    ppermute x6, waiting for transfers between devices, narrow(): return lax.ppermute(value, 'row', pairs)  10.5 us
    ppermute x6, starting transfers between devices, wide(): return lax.ppermute(value, 'row', pairs)  7.85 us
    ppermute x6, starting transfers between devices, narrow(): return lax.ppermute(value, 'row', pairs)  7.75 us
    ppermute x6, waiting for transfers between devices, wide(): return lax.ppermute(value, 'row', pairs)  6.89 us
    ppermute x2, starting transfers between devices, next_row(): lax.ppermute(value, 'row', [(r, (r + steps) % count) for r in range(count)])  5.14 us
  transfers between devices with their start and end apart: 33, of which 15 were waited for; matrix products, arithmetic and copies ran while one was open for 3% of the time, Pallas kernels for 14%

profile of v4, /device:TPU:96, one launch (start us, length us, event | category | flops | bytes accessed | tf_op | source)
XLA Modules:
  0.0 107.4 jit_solution(15644863253895101302)
XLA Ops:
  0.6 3.2 %collective-permute-start.7 = (bf16[256,512]{1,0:T(8,128)(2,1)}, bf16[256,512]{1,0:T(8,128)(2,1)S(1)}, u32[]{:S(2)}, u32[]{:S(2)}) collective-permute-start(bf16[256,512]{1,0:T(8,128)(2,1)} %refs_0_.3), channel_id=1, source_target_pairs={{0,1},{1,2},{2,3},{3,4},{4,5},{5,6},{6,7},{7,0},{8,15},{9,8},{10,9... | collective-permute-start | bytes 786440 | tf_op jit(solution)/shard_map/ppermute | solution.py:30
  3.8 2.8 %collective-permute-start = (bf16[128,512]{1,0:T(8,128)(2,1)}, bf16[128,512]{1,0:T(8,128)(2,1)S(1)}, u32[]{:S(2)}, u32[]{:S(2)}) collective-permute-start(bf16[128,512]{1,0:T(8,128)(2,1)} %refs_0_.2), channel_id=1, source_target_pairs={{0,48},{8,200},{16,0},{24,216},{32,16},{40,232},{48,32},{56,248},{... | collective-permute-start | bytes 393224 | tf_op jit(solution)/shard_map/ppermute | solution.py:38
  8.3 2.5 %collective-permute-done.refs_1_ = bf16[128,512]{1,0:T(8,128)(2,1)S(1)} collective-permute-done((bf16[128,512]{1,0:T(8,128)(2,1)}, bf16[128,512]{1,0:T(8,128)(2,1)S(1)}, u32[]{:S(2)}, u32[]{:S(2)}) %collective-permute-start) | collective-permute-done | bytes 131104 | tf_op jit(solution)/shard_map/ppermute | solution.py:38
  10.8 2.5 %collective-permute-done.1.refs_2_ = bf16[128,512]{1,0:T(8,128)(2,1)S(1)} collective-permute-done((bf16[128,512]{1,0:T(8,128)(2,1)}, bf16[128,512]{1,0:T(8,128)(2,1)S(1)}, u32[]{:S(2)}, u32[]{:S(2)}) %collective-permute-start.1) | collective-permute-done | bytes 131104 | tf_op jit(solution)/shard_map/ppermute | solution.py:38
  13.4 1.3 %collective-permute-done.2.refs_3_ = bf16[128,512]{1,0:T(8,128)(2,1)S(1)} collective-permute-done((bf16[128,512]{1,0:T(8,128)(2,1)}, bf16[128,512]{1,0:T(8,128)(2,1)S(1)}, u32[]{:S(2)}, u32[]{:S(2)}) %collective-permute-start.2) | collective-permute-done | bytes 131104 | tf_op jit(solution)/shard_map/ppermute | solution.py:38
  15.6 1.1 %collective-permute-start.9 = (bf16[256,512]{1,0:T(8,128)(2,1)S(1)}, bf16[256,512]{1,0:T(8,128)(2,1)S(1)}, u32[]{:S(2)}, u32[]{:S(2)}) collective-permute-start(bf16[256,512]{1,0:T(8,128)(2,1)S(1)} %collective-permute-done.7.refs_2_), channel_id=1, source_target_pairs={{0,1},{1,2},{2,3},{3,4},{4,5},{5,6},{6,7},{7,0},{8,15},{9,8},{10,9... | collective-permute-start | bytes 786440 | tf_op jit(solution)/shard_map/ppermute | solution.py:30
  16.7 3.0 %collective-permute-start.3 = (bf16[4,128,512]{2,1,0:T(8,128)(2,1)S(1)}, bf16[4,128,512]{2,1,0:T(8,128)(2,1)S(1)}, u32[]{:S(2)}, u32[]{:S(2)}) collective-permute-start(bf16[4,128,512]{2,1,0:T(8,128)(2,1)S(1)} %stack.21.refs_3_), channel_id=1, source_target_pairs={{0,192},{8,56},{16,208},{24,8},{32,224},{40,24},{48,240},{56,40},{... | collective-permute-start | bytes 1572872 | tf_op jit(solution)/shard_map/ppermute | solution.py:46
  21.4 1.0 collective-permute-start.8
  24.1 2.7 %collective-permute-start.15 = (bf16[256,512]{1,0:T(8,128)(2,1)S(1)}, bf16[256,512]{1,0:T(8,128)(2,1)S(1)}, u32[]{:S(2)}, u32[]{:S(2)}) collective-permute-start(bf16[256,512]{1,0:T(8,128)(2,1)S(1)} %collective-permute-done.9.refs_4_), channel_id=1, source_target_pairs={{0,1},{1,2},{2,3},{3,4},{4,5},{5,6},{6,7},{7,0},{8,15},{9,8},{10,9... | collective-permute-start | bytes 786440 | tf_op jit(solution)/shard_map/ppermute | solution.py:30
  27.7 1.3 %collective-permute-done.8.refs_3_ = bf16[256,512]{1,0:T(8,128)(2,1)S(1)} collective-permute-done((bf16[256,512]{1,0:T(8,128)(2,1)S(1)}, bf16[256,512]{1,0:T(8,128)(2,1)S(1)}, u32[]{:S(2)}, u32[]{:S(2)}) %collective-permute-start.8) | collective-permute-done | bytes 262176 | tf_op jit(solution)/shard_map/ppermute | solution.py:30
  29.2 2.9 %collective-permute-done.3.refs_4_ = bf16[4,128,512]{2,1,0:T(8,128)(2,1)S(1)} collective-permute-done((bf16[4,128,512]{2,1,0:T(8,128)(2,1)S(1)}, bf16[4,128,512]{2,1,0:T(8,128)(2,1)S(1)}, u32[]{:S(2)}, u32[]{:S(2)}) %collective-permute-start.3) | collective-permute-done | bytes 524320 | tf_op jit(solution)/shard_map/ppermute | solution.py:46
  32.1 4.0 %collective-permute-done.5.refs_6_ = bf16[4,128,512]{2,1,0:T(8,128)(2,1)S(1)} collective-permute-done((bf16[4,128,512]{2,1,0:T(8,128)(2,1)S(1)}, bf16[4,128,512]{2,1,0:T(8,128)(2,1)S(1)}, u32[]{:S(2)}, u32[]{:S(2)}) %collective-permute-start.5) | collective-permute-done | bytes 524320 | tf_op jit(solution)/shard_map/ppermute | solution.py:46
  36.1 1.0 collective-permute-start.16
  39.4 3.0 %collective-permute-done.16.refs_2_ = bf16[256,512]{1,0:T(8,128)(2,1)S(1)} collective-permute-done((bf16[256,512]{1,0:T(8,128)(2,1)S(1)}, bf16[256,512]{1,0:T(8,128)(2,1)S(1)}, u32[]{:S(2)}, u32[]{:S(2)}) %collective-permute-start.16) | collective-permute-done | bytes 262176 | tf_op jit(solution)/shard_map/ppermute | solution.py:30
  42.4 1.6 %project_own.1 = (f32[256,512]{1,0:T(8,128)S(1)}, bf16[4,4,2,128,512]{4,3,2,1,0:T(8,128)(2,1)S(1)}, bf16[8,256,256]{2,1,0:T(8,128)(2,1)S(1)}, bf16[10,256,256]{2,1,0:T(8,128)(2,1)S(1)}) custom-call(s32[4]{0:T(128)S(1)} %pad_add_fusion.ids, bf16[256,512]{1,0:T(8,128)(2,1)S(1)} %collective-permute-done.14.refs_0_, ...), custom_call_target="tpu_custom_call", output_to_operand_aliasing={{2}: (8, {}), {3}: (9, {})} | custom-call | flops 4294967296 | bytes 4194304 | tf_op jit(solution)/shard_map/project_own/pallas_call | solution.py:224
  44.1 1.5 %project_other.1 = (bf16[256,512]{1,0:T(8,128)(2,1)S(1)}, bf16[128,512]{1,0:T(8,128)(2,1)S(1)}, bf16[128,512]{1,0:T(8,128)(2,1)S(1)}, bf16[4,4,2,128,512]{4,3,2,1,0:T(8,128)(2,1)S(1)}) custom-call(s32[4]{0:T(128)S(1)} %pad_add_fusion.ids, bf16[4,128,512]{2,1,0:T(8,128)(2,1)S(1)} %collective-permute-done.10.refs_0_, ...), custom_call_target="tpu_custom_call", output_to_operand_aliasing={{3}: (7, {})} | custom-call | flops 1073741824 | bytes 4194304 | tf_op jit(solution)/shard_map/project_other/pallas_call | solution.py:255
  45.8 5.1 %collective-permute-start.18 = (bf16[128,512]{1,0:T(8,128)(2,1)S(1)}, bf16[128,512]{1,0:T(8,128)(2,1)S(1)}, u32[]{:S(2)}, u32[]{:S(2)}) collective-permute-start(bf16[128,512]{1,0:T(8,128)(2,1)S(1)} %get-tuple-element.69), channel_id=1, source_target_pairs={{0,248},{8,0},{16,8},{24,16},{32,24},{40,32},{48,40},{56,48},{64,5... | collective-permute-start | bytes 393224 | tf_op jit(solution)/shard_map/ppermute | solution.py:55
  50.8 7.5 %inside.1 = (bf16[128,512]{1,0:T(8,128)(2,1)S(1)}, f32[128,512]{1,0:T(8,128)S(1)}, f32[128,512]{1,0:T(8,128)S(1)}, f32[128,512]{1,0:T(8,128)S(1)}) custom-call(bf16[256,512]{1,0:T(8,128)(2,1)S(1)} %get-tuple-element.67.p_ref, bf16[256,512]{1,0:T(8,128)(2,1)S(1)} %copy-done.1, bf16[8,16,16,512]{3,2,1,0:T(8,128)(2,1)S(1)} %broadcast_in_dim.46.taps_ref, ...), custom_call_target="tpu_custom_call" | custom-call | flops 4294967296 | bytes 4194304 | tf_op jit(solution)/shard_map/inside/pallas_call | solution.py:347
  58.3 8.9 %edges.1 = (bf16[256,512]{1,0:T(8,128)(2,1)}, bf16[256,512]{1,0:T(8,128)(2,1)S(1)}, bf16[256,512]{1,0:T(8,128)(2,1)S(1)}, bf16[4,4,2,128,512]{4,3,2,1,0:T(8,128)(2,1)S(1)}, bf16[10,256,256]{2,1,0:T(8,128)(2,1)S(1)}) custom-call(bf16[256,512]{1,0:T(8,128)(2,1)S(1)} %get-tuple-element.67.p_ref, ...), custom_call_target="tpu_custom_call", output_to_operand_aliasing={{4}: (13, {})} | custom-call | flops 4294967296 | bytes 4194304 | tf_op jit(solution)/shard_map/edges/pallas_call | solution.py:347
  67.3 2.3 %collective-permute-start.20 = (bf16[256,512]{1,0:T(8,128)(2,1)S(1)}, bf16[256,512]{1,0:T(8,128)(2,1)S(1)}, u32[]{:S(2)}, u32[]{:S(2)}) collective-permute-start(bf16[256,512]{1,0:T(8,128)(2,1)S(1)} %get-tuple-element.87), channel_id=1, source_target_pairs={{0,1},{1,2},{2,3},{3,4},{4,5},{5,6},{6,7},{7,0},{8,15},{9,8},{10,9... | collective-permute-start | bytes 786440 | tf_op jit(solution)/shard_map/ppermute | solution.py:30
  69.6 1.7 %near_terms.1 = (bf16[256,512]{1,0:T(8,128)(2,1)S(1)}, bf16[256,512]{1,0:T(8,128)(2,1)S(1)}, bf16[256,512]{1,0:T(8,128)(2,1)S(1)}, bf16[256,512]{1,0:T(8,128)(2,...) custom-call(s32[4]{0:T(128)S(1)} %pad_add_fusion.ids, ...), custom_call_target="tpu_custom_call" | custom-call | flops 939524096 | bytes 6291456 | tf_op jit(solution)/shard_map/near_terms/pallas_call | solution.py:389
  71.5 2.0 %weight_terms.1 = (bf16[4,128,512]{2,1,0:T(8,128)(2,1)S(1)}, bf16[4,128,512]{2,1,0:T(8,128)(2,1)S(1)}, bf16[4,128,512]{2,1,0:T(8,128)(2,1)S(1)}, bf16[4,128,512]{2,1,0:T(8,128)(2,1)S(1)}) custom-call(s32[4]{0:T(128)S(1)} %pad_add_fusion.ids, bf16[8,256,256]{2,1,0:T(8,128)(2,1)S(1)} %get-tuple-element.82.mine, ...), custom_call_target="tpu_custom_call" | custom-call | flops 1073741824 | bytes 5242880 | tf_op jit(solution)/shard_map/weight_terms/pallas_call | solution.py:436
  73.4 1.1 %collective-permute-done.20.b = bf16[256,512]{1,0:T(8,128)(2,1)S(1)} collective-permute-done((bf16[256,512]{1,0:T(8,128)(2,1)S(1)}, bf16[256,512]{1,0:T(8,128)(2,1)S(1)}, u32[]{:S(2)}, u32[]{:S(2)}) %collective-permute-start.20) | collective-permute-done | bytes 262176 | tf_op jit(solution)/shard_map/ppermute | solution.py:30
  74.6 3.5 %collective-permute-start.21 = (bf16[256,512]{1,0:T(8,128)(2,1)S(1)}, bf16[256,512]{1,0:T(8,128)(2,1)S(1)}, u32[]{:S(2)}, u32[]{:S(2)}) collective-permute-start(bf16[256,512]{1,0:T(8,128)(2,1)S(1)} %add.69), channel_id=1, source_target_pairs={{0,1},{1,2},{2,3},{3,4},{4,5},{5,6},{6,7},{7,0},{8,15},{9,8},{10,9... | collective-permute-start | bytes 786440 | tf_op jit(solution)/shard_map/ppermute | solution.py:30
  79.0 2.4 %collective-permute-start.29 = (bf16[4,128,512]{2,1,0:T(8,128)(2,1)S(1)}, bf16[4,128,512]{2,1,0:T(8,128)(2,1)S(1)}, u32[]{:S(2)}, u32[]{:S(2)}) collective-permute-start(bf16[4,128,512]{2,1,0:T(8,128)(2,1)S(1)} %get-tuple-element.94), channel_id=1, source_target_pairs={{0,192},{8,56},{16,208},{24,8},{32,224},{40,24},{48,240},{56,40},{... | collective-permute-start | bytes 1572872 | tf_op jit(solution)/shard_map/ppermute | solution.py:46
  81.5 2.2 %collective-permute-done.21.b = bf16[256,512]{1,0:T(8,128)(2,1)S(1)} collective-permute-done((bf16[256,512]{1,0:T(8,128)(2,1)S(1)}, bf16[256,512]{1,0:T(8,128)(2,1)S(1)}, u32[]{:S(2)}, u32[]{:S(2)}) %collective-permute-start.21) | collective-permute-done | bytes 262176 | tf_op jit(solution)/shard_map/ppermute | solution.py:30
  83.8 3.8 %collective-permute-start.22 = (bf16[256,512]{1,0:T(8,128)(2,1)S(1)}, bf16[256,512]{1,0:T(8,128)(2,1)S(1)}, u32[]{:S(2)}, u32[]{:S(2)}) collective-permute-start(bf16[256,512]{1,0:T(8,128)(2,1)S(1)} %add.70), channel_id=1, source_target_pairs={{0,1},{1,2},{2,3},{3,4},{4,5},{5,6},{6,7},{7,0},{8,15},{9,8},{10,9... | collective-permute-start | bytes 786440 | tf_op jit(solution)/shard_map/ppermute | solution.py:30
  87.6 3.6 %collective-permute-done.25.b = bf16[256,512]{1,0:T(8,128)(2,1)S(1)} collective-permute-done((bf16[256,512]{1,0:T(8,128)(2,1)S(1)}, bf16[256,512]{1,0:T(8,128)(2,1)S(1)}, u32[]{:S(2)}, u32[]{:S(2)}) %collective-permute-start.25) | collective-permute-done | bytes 262176 | tf_op jit(solution)/shard_map/ppermute | solution.py:30
  91.4 2.6 %collective-permute-done.22.b = bf16[256,512]{1,0:T(8,128)(2,1)S(1)} collective-permute-done((bf16[256,512]{1,0:T(8,128)(2,1)S(1)}, bf16[256,512]{1,0:T(8,128)(2,1)S(1)}, u32[]{:S(2)}, u32[]{:S(2)}) %collective-permute-start.22) | collective-permute-done | bytes 262176 | tf_op jit(solution)/shard_map/ppermute | solution.py:30
  94.1 3.8 %collective-permute-start.23 = (bf16[256,512]{1,0:T(8,128)(2,1)S(1)}, bf16[256,512]{1,0:T(8,128)(2,1)S(1)}, u32[]{:S(2)}, u32[]{:S(2)}) collective-permute-start(bf16[256,512]{1,0:T(8,128)(2,1)S(1)} %add.71), channel_id=1, source_target_pairs={{0,1},{1,2},{2,3},{3,4},{4,5},{5,6},{6,7},{7,0},{8,15},{9,8},{10,9... | collective-permute-start | bytes 786440 | tf_op jit(solution)/shard_map/ppermute | solution.py:30
  98.3 3.1 %collective-permute-start.32 = (bf16[128,512]{1,0:T(8,128)(2,1)S(1)}, bf16[128,512]{1,0:T(8,128)(2,1)S(1)}, u32[]{:S(2)}, u32[]{:S(2)}) collective-permute-start(bf16[128,512]{1,0:T(8,128)(2,1)S(1)} %get-tuple-element.98), channel_id=1, source_target_pairs={{0,48},{8,200},{16,0},{24,216},{32,16},{40,232},{48,32},{56,248},{... | collective-permute-start | bytes 393224 | tf_op jit(solution)/shard_map/ppermute | solution.py:38
  102.5 3.2 %collective-permute-done.30 = bf16[128,512]{1,0:T(8,128)(2,1)S(1)} collective-permute-done((bf16[128,512]{1,0:T(8,128)(2,1)S(1)}, bf16[128,512]{1,0:T(8,128)(2,1)S(1)}, u32[]{:S(2)}, u32[]{:S(2)}) %collective-permute-start.30) | collective-permute-done | bytes 131104 | tf_op jit(solution)/shard_map/ppermute | solution.py:38
  (69 shorter events, 14.2 us)
Async XLA Ops:
  0.6 15.0 %collective-permute-start.7 = (bf16[256,512]{1,0:T(8,128)(2,1)}, bf16[256,512]{1,0:T(8,128)(2,1)S(1)}, u32[]{:S(2)}, u32[]{:S(2)}) collective-permute-start(bf16[256,512]{1,0:T(8,128)(2,1)} %refs_0_.3), channel_id=1, source_target_pairs={{0,1},{1,2},{2,3},{3,4},{4,5},{5,6},{6,7},{7,0},{8,15},{9,8},{10,9... | collective-permute-start | bytes 786440 | tf_op jit(solution)/shard_map/ppermute | solution.py:30
  3.8 7.0 %collective-permute-start = (bf16[128,512]{1,0:T(8,128)(2,1)}, bf16[128,512]{1,0:T(8,128)(2,1)S(1)}, u32[]{:S(2)}, u32[]{:S(2)}) collective-permute-start(bf16[128,512]{1,0:T(8,128)(2,1)} %refs_0_.2), channel_id=1, source_target_pairs={{0,48},{8,200},{16,0},{24,216},{32,16},{40,232},{48,32},{56,248},{... | collective-permute-start | bytes 393224 | tf_op jit(solution)/shard_map/ppermute | solution.py:38
  6.6 6.8 %collective-permute-start.1 = (bf16[128,512]{1,0:T(8,128)(2,1)}, bf16[128,512]{1,0:T(8,128)(2,1)S(1)}, u32[]{:S(2)}, u32[]{:S(2)}) collective-permute-start(bf16[128,512]{1,0:T(8,128)(2,1)} %refs_0_.2), channel_id=1, source_target_pairs={{0,32},{8,136},{16,48},{24,152},{32,0},{40,168},{48,16},{56,184},{... | collective-permute-start | bytes 393224 | tf_op jit(solution)/shard_map/ppermute | solution.py:38
  7.4 7.3 %collective-permute-start.2 = (bf16[128,512]{1,0:T(8,128)(2,1)}, bf16[128,512]{1,0:T(8,128)(2,1)S(1)}, u32[]{:S(2)}, u32[]{:S(2)}) collective-permute-start(bf16[128,512]{1,0:T(8,128)(2,1)} %refs_0_.2), channel_id=1, source_target_pairs={{0,16},{8,72},{16,32},{24,88},{32,48},{40,104},{48,0},{56,120},{64... | collective-permute-start | bytes 393224 | tf_op jit(solution)/shard_map/ppermute | solution.py:38
  8.3 13.1 %collective-permute-start.6 = (bf16[256,512]{1,0:T(8,128)(2,1)}, bf16[256,512]{1,0:T(8,128)(2,1)S(1)}, u32[]{:S(2)}, u32[]{:S(2)}) collective-permute-start(bf16[256,512]{1,0:T(8,128)(2,1)} %refs_0_.3), channel_id=1, source_target_pairs={{0,7},{1,0},{2,1},{3,2},{4,3},{5,4},{6,5},{7,6},{8,9},{9,10},{10,1... | collective-permute-start | bytes 786440 | tf_op jit(solution)/shard_map/ppermute | solution.py:30
  15.6 8.4 %collective-permute-start.9 = (bf16[256,512]{1,0:T(8,128)(2,1)S(1)}, bf16[256,512]{1,0:T(8,128)(2,1)S(1)}, u32[]{:S(2)}, u32[]{:S(2)}) collective-permute-start(bf16[256,512]{1,0:T(8,128)(2,1)S(1)} %collective-permute-done.7.refs_2_), channel_id=1, source_target_pairs={{0,1},{1,2},{2,3},{3,4},{4,5},{5,6},{6,7},{7,0},{8,15},{9,8},{10,9... | collective-permute-start | bytes 786440 | tf_op jit(solution)/shard_map/ppermute | solution.py:30
  16.7 15.3 %collective-permute-start.3 = (bf16[4,128,512]{2,1,0:T(8,128)(2,1)S(1)}, bf16[4,128,512]{2,1,0:T(8,128)(2,1)S(1)}, u32[]{:S(2)}, u32[]{:S(2)}) collective-permute-start(bf16[4,128,512]{2,1,0:T(8,128)(2,1)S(1)} %stack.21.refs_3_), channel_id=1, source_target_pairs={{0,192},{8,56},{16,208},{24,8},{32,224},{40,24},{48,240},{56,40},{... | collective-permute-start | bytes 1572872 | tf_op jit(solution)/shard_map/ppermute | solution.py:46
  19.8 12.3 %collective-permute-start.4 = (bf16[4,128,512]{2,1,0:T(8,128)(2,1)S(1)}, bf16[4,128,512]{2,1,0:T(8,128)(2,1)S(1)}, u32[]{:S(2)}, u32[]{:S(2)}) collective-permute-start(bf16[4,128,512]{2,1,0:T(8,128)(2,1)S(1)} %stack.21.refs_3_), channel_id=1, source_target_pairs={{0,128},{8,40},{16,144},{24,56},{32,160},{40,8},{48,176},{56,24},{... | collective-permute-start | bytes 1572872 | tf_op jit(solution)/shard_map/ppermute | solution.py:46
  20.4 15.7 %collective-permute-start.5 = (bf16[4,128,512]{2,1,0:T(8,128)(2,1)S(1)}, bf16[4,128,512]{2,1,0:T(8,128)(2,1)S(1)}, u32[]{:S(2)}, u32[]{:S(2)}) collective-permute-start(bf16[4,128,512]{2,1,0:T(8,128)(2,1)S(1)} %stack.21.refs_3_), channel_id=1, source_target_pairs={{0,64},{8,24},{16,80},{24,40},{32,96},{40,56},{48,112},{56,8},{64,... | collective-permute-start | bytes 1572872 | tf_op jit(solution)/shard_map/ppermute | solution.py:46
  21.4 7.7 %collective-permute-start.8 = (bf16[256,512]{1,0:T(8,128)(2,1)S(1)}, bf16[256,512]{1,0:T(8,128)(2,1)S(1)}, u32[]{:S(2)}, u32[]{:S(2)}) collective-permute-start(bf16[256,512]{1,0:T(8,128)(2,1)S(1)} %collective-permute-done.6.refs_1_), channel_id=1, source_target_pairs={{0,7},{1,0},{2,1},{3,2},{4,3},{5,4},{6,5},{7,6},{8,9},{9,10},{10,1... | collective-permute-start | bytes 786440 | tf_op jit(solution)/shard_map/ppermute | solution.py:30
  24.1 12.0 %collective-permute-start.15 = (bf16[256,512]{1,0:T(8,128)(2,1)S(1)}, bf16[256,512]{1,0:T(8,128)(2,1)S(1)}, u32[]{:S(2)}, u32[]{:S(2)}) collective-permute-start(bf16[256,512]{1,0:T(8,128)(2,1)S(1)} %collective-permute-done.9.refs_4_), channel_id=1, source_target_pairs={{0,1},{1,2},{2,3},{3,4},{4,5},{5,6},{6,7},{7,0},{8,15},{9,8},{10,9... | collective-permute-start | bytes 786440 | tf_op jit(solution)/shard_map/ppermute | solution.py:30
  29.0 10.1 %collective-permute-start.14 = (bf16[256,512]{1,0:T(8,128)(2,1)S(1)}, bf16[256,512]{1,0:T(8,128)(2,1)S(1)}, u32[]{:S(2)}, u32[]{:S(2)}) collective-permute-start(bf16[256,512]{1,0:T(8,128)(2,1)S(1)} %collective-permute-done.8.refs_3_), channel_id=1, source_target_pairs={{0,7},{1,0},{2,1},{3,2},{4,3},{5,4},{6,5},{7,6},{8,9},{9,10},{10,1... | collective-permute-start | bytes 786440 | tf_op jit(solution)/shard_map/ppermute | solution.py:30
  36.1 6.4 %collective-permute-start.16 = (bf16[256,512]{1,0:T(8,128)(2,1)S(1)}, bf16[256,512]{1,0:T(8,128)(2,1)S(1)}, u32[]{:S(2)}, u32[]{:S(2)}) collective-permute-start(bf16[256,512]{1,0:T(8,128)(2,1)S(1)} %collective-permute-done.15.refs_1_), channel_id=1, source_target_pairs={{0,1},{1,2},{2,3},{3,4},{4,5},{5,6},{6,7},{7,0},{8,15},{9,8},{10,9... | collective-permute-start | bytes 786440 | tf_op jit(solution)/shard_map/ppermute | solution.py:30
  38.3 5.8 %collective-permute-start.10 = (bf16[4,128,512]{2,1,0:T(8,128)(2,1)S(1)}, bf16[4,128,512]{2,1,0:T(8,128)(2,1)S(1)}, u32[]{:S(2)}, u32[]{:S(2)}) collective-permute-start(bf16[4,128,512]{2,1,0:T(8,128)(2,1)S(1)} %stack.21.refs_3_), channel_id=1, source_target_pairs={{0,8},{8,0},{16,24},{24,16},{32,40},{40,32},{48,56},{56,48},{64,72... | collective-permute-start | bytes 1572872 | tf_op jit(solution)/shard_map/ppermute | solution.py:50
  38.4 5.7 %collective-permute-start.11 = (bf16[4,128,512]{2,1,0:T(8,128)(2,1)S(1)}, bf16[4,128,512]{2,1,0:T(8,128)(2,1)S(1)}, u32[]{:S(2)}, u32[]{:S(2)}) collective-permute-start(bf16[4,128,512]{2,1,0:T(8,128)(2,1)S(1)} %collective-permute-done.3.refs_4_), channel_id=1, source_target_pairs={{0,8},{8,0},{16,24},{24,16},{32,40},{40,32},{48,56},{56,48},{64,72... | collective-permute-start | bytes 1572872 | tf_op jit(solution)/shard_map/ppermute | solution.py:50
  38.9 5.2 %collective-permute-start.12 = (bf16[4,128,512]{2,1,0:T(8,128)(2,1)S(1)}, bf16[4,128,512]{2,1,0:T(8,128)(2,1)S(1)}, u32[]{:S(2)}, u32[]{:S(2)}) collective-permute-start(bf16[4,128,512]{2,1,0:T(8,128)(2,1)S(1)} %collective-permute-done.4.refs_5_), channel_id=1, source_target_pairs={{0,8},{8,0},{16,24},{24,16},{32,40},{40,32},{48,56},{56,48},{64,72... | collective-permute-start | bytes 1572872 | tf_op jit(solution)/shard_map/ppermute | solution.py:50
  39.1 5.0 %collective-permute-start.13 = (bf16[4,128,512]{2,1,0:T(8,128)(2,1)S(1)}, bf16[4,128,512]{2,1,0:T(8,128)(2,1)S(1)}, u32[]{:S(2)}, u32[]{:S(2)}) collective-permute-start(bf16[4,128,512]{2,1,0:T(8,128)(2,1)S(1)} %collective-permute-done.5.refs_6_), channel_id=1, source_target_pairs={{0,8},{8,0},{16,24},{24,16},{32,40},{40,32},{48,56},{56,48},{64,72... | collective-permute-start | bytes 1572872 | tf_op jit(solution)/shard_map/ppermute | solution.py:50
  45.7 12.6 %collective-permute-start.17 = (bf16[128,512]{1,0:T(8,128)(2,1)S(1)}, bf16[128,512]{1,0:T(8,128)(2,1)S(1)}, u32[]{:S(2)}, u32[]{:S(2)}) collective-permute-start(bf16[128,512]{1,0:T(8,128)(2,1)S(1)} %get-tuple-element.68), channel_id=1, source_target_pairs={{0,8},{8,16},{16,24},{24,32},{32,40},{40,48},{48,56},{56,64},{64,7... | collective-permute-start | bytes 393224 | tf_op jit(solution)/shard_map/ppermute | solution.py:55
  45.8 12.6 %collective-permute-start.18 = (bf16[128,512]{1,0:T(8,128)(2,1)S(1)}, bf16[128,512]{1,0:T(8,128)(2,1)S(1)}, u32[]{:S(2)}, u32[]{:S(2)}) collective-permute-start(bf16[128,512]{1,0:T(8,128)(2,1)S(1)} %get-tuple-element.69), channel_id=1, source_target_pairs={{0,248},{8,0},{16,8},{24,16},{32,24},{40,32},{48,40},{56,48},{64,5... | collective-permute-start | bytes 393224 | tf_op jit(solution)/shard_map/ppermute | solution.py:55
  67.3 7.2 %collective-permute-start.20 = (bf16[256,512]{1,0:T(8,128)(2,1)S(1)}, bf16[256,512]{1,0:T(8,128)(2,1)S(1)}, u32[]{:S(2)}, u32[]{:S(2)}) collective-permute-start(bf16[256,512]{1,0:T(8,128)(2,1)S(1)} %get-tuple-element.87), channel_id=1, source_target_pairs={{0,1},{1,2},{2,3},{3,4},{4,5},{5,6},{6,7},{7,0},{8,15},{9,8},{10,9... | collective-permute-start | bytes 786440 | tf_op jit(solution)/shard_map/ppermute | solution.py:30
  71.3 10.0 %collective-permute-start.24 = (bf16[256,512]{1,0:T(8,128)(2,1)S(1)}, bf16[256,512]{1,0:T(8,128)(2,1)S(1)}, u32[]{:S(2)}, u32[]{:S(2)}) collective-permute-start(bf16[256,512]{1,0:T(8,128)(2,1)S(1)} %get-tuple-element.90), channel_id=1, source_target_pairs={{0,7},{1,0},{2,1},{3,2},{4,3},{5,4},{6,5},{7,6},{8,9},{9,10},{10,1... | collective-permute-start | bytes 786440 | tf_op jit(solution)/shard_map/ppermute | solution.py:30
  74.6 9.1 %collective-permute-start.21 = (bf16[256,512]{1,0:T(8,128)(2,1)S(1)}, bf16[256,512]{1,0:T(8,128)(2,1)S(1)}, u32[]{:S(2)}, u32[]{:S(2)}) collective-permute-start(bf16[256,512]{1,0:T(8,128)(2,1)S(1)} %add.69), channel_id=1, source_target_pairs={{0,1},{1,2},{2,3},{3,4},{4,5},{5,6},{6,7},{7,0},{8,15},{9,8},{10,9... | collective-permute-start | bytes 786440 | tf_op jit(solution)/shard_map/ppermute | solution.py:30
  78.1 19.7 %collective-permute-start.27 = (bf16[4,128,512]{2,1,0:T(8,128)(2,1)S(1)}, bf16[4,128,512]{2,1,0:T(8,128)(2,1)S(1)}, u32[]{:S(2)}, u32[]{:S(2)}) collective-permute-start(bf16[4,128,512]{2,1,0:T(8,128)(2,1)S(1)} %get-tuple-element.92), channel_id=1, source_target_pairs={{0,64},{8,24},{16,80},{24,40},{32,96},{40,56},{48,112},{56,8},{64,... | collective-permute-start | bytes 1572872 | tf_op jit(solution)/shard_map/ppermute | solution.py:46
  78.1 19.7 %collective-permute-start.28 = (bf16[4,128,512]{2,1,0:T(8,128)(2,1)S(1)}, bf16[4,128,512]{2,1,0:T(8,128)(2,1)S(1)}, u32[]{:S(2)}, u32[]{:S(2)}) collective-permute-start(bf16[4,128,512]{2,1,0:T(8,128)(2,1)S(1)} %get-tuple-element.93), channel_id=1, source_target_pairs={{0,128},{8,40},{16,144},{24,56},{32,160},{40,8},{48,176},{56,24},{... | collective-permute-start | bytes 1572872 | tf_op jit(solution)/shard_map/ppermute | solution.py:46
  79.0 18.8 %collective-permute-start.29 = (bf16[4,128,512]{2,1,0:T(8,128)(2,1)S(1)}, bf16[4,128,512]{2,1,0:T(8,128)(2,1)S(1)}, u32[]{:S(2)}, u32[]{:S(2)}) collective-permute-start(bf16[4,128,512]{2,1,0:T(8,128)(2,1)S(1)} %get-tuple-element.94), channel_id=1, source_target_pairs={{0,192},{8,56},{16,208},{24,8},{32,224},{40,24},{48,240},{56,40},{... | collective-permute-start | bytes 1572872 | tf_op jit(solution)/shard_map/ppermute | solution.py:46
  81.5 9.8 %collective-permute-start.25 = (bf16[256,512]{1,0:T(8,128)(2,1)S(1)}, bf16[256,512]{1,0:T(8,128)(2,1)S(1)}, u32[]{:S(2)}, u32[]{:S(2)}) collective-permute-start(bf16[256,512]{1,0:T(8,128)(2,1)S(1)} %add.72), channel_id=1, source_target_pairs={{0,7},{1,0},{2,1},{3,2},{4,3},{5,4},{6,5},{7,6},{8,9},{9,10},{10,1... | collective-permute-start | bytes 786440 | tf_op jit(solution)/shard_map/ppermute | solution.py:30
  83.8 10.2 %collective-permute-start.22 = (bf16[256,512]{1,0:T(8,128)(2,1)S(1)}, bf16[256,512]{1,0:T(8,128)(2,1)S(1)}, u32[]{:S(2)}, u32[]{:S(2)}) collective-permute-start(bf16[256,512]{1,0:T(8,128)(2,1)S(1)} %add.70), channel_id=1, source_target_pairs={{0,1},{1,2},{2,3},{3,4},{4,5},{5,6},{6,7},{7,0},{8,15},{9,8},{10,9... | collective-permute-start | bytes 786440 | tf_op jit(solution)/shard_map/ppermute | solution.py:30
  91.3 10.2 %collective-permute-start.26 = (bf16[256,512]{1,0:T(8,128)(2,1)S(1)}, bf16[256,512]{1,0:T(8,128)(2,1)S(1)}, u32[]{:S(2)}, u32[]{:S(2)}) collective-permute-start(bf16[256,512]{1,0:T(8,128)(2,1)S(1)} %add.73), channel_id=1, source_target_pairs={{0,7},{1,0},{2,1},{3,2},{4,3},{5,4},{6,5},{7,6},{8,9},{9,10},{10,1... | collective-permute-start | bytes 786440 | tf_op jit(solution)/shard_map/ppermute | solution.py:30
  94.1 7.7 %collective-permute-start.23 = (bf16[256,512]{1,0:T(8,128)(2,1)S(1)}, bf16[256,512]{1,0:T(8,128)(2,1)S(1)}, u32[]{:S(2)}, u32[]{:S(2)}) collective-permute-start(bf16[256,512]{1,0:T(8,128)(2,1)S(1)} %add.71), channel_id=1, source_target_pairs={{0,1},{1,2},{2,3},{3,4},{4,5},{5,6},{6,7},{7,0},{8,15},{9,8},{10,9... | collective-permute-start | bytes 786440 | tf_op jit(solution)/shard_map/ppermute | solution.py:30
  98.1 7.7 %collective-permute-start.30 = (bf16[128,512]{1,0:T(8,128)(2,1)S(1)}, bf16[128,512]{1,0:T(8,128)(2,1)S(1)}, u32[]{:S(2)}, u32[]{:S(2)}) collective-permute-start(bf16[128,512]{1,0:T(8,128)(2,1)S(1)} %get-tuple-element.96), channel_id=1, source_target_pairs={{0,16},{8,72},{16,32},{24,88},{32,48},{40,104},{48,0},{56,120},{64... | collective-permute-start | bytes 393224 | tf_op jit(solution)/shard_map/ppermute | solution.py:38
  98.2 7.6 %collective-permute-start.31 = (bf16[128,512]{1,0:T(8,128)(2,1)S(1)}, bf16[128,512]{1,0:T(8,128)(2,1)S(1)}, u32[]{:S(2)}, u32[]{:S(2)}) collective-permute-start(bf16[128,512]{1,0:T(8,128)(2,1)S(1)} %get-tuple-element.97), channel_id=1, source_target_pairs={{0,32},{8,136},{16,48},{24,152},{32,0},{40,168},{48,16},{56,184},{... | collective-permute-start | bytes 393224 | tf_op jit(solution)/shard_map/ppermute | solution.py:38
  98.3 8.4 %collective-permute-start.32 = (bf16[128,512]{1,0:T(8,128)(2,1)S(1)}, bf16[128,512]{1,0:T(8,128)(2,1)S(1)}, u32[]{:S(2)}, u32[]{:S(2)}) collective-permute-start(bf16[128,512]{1,0:T(8,128)(2,1)S(1)} %get-tuple-element.98), channel_id=1, source_target_pairs={{0,48},{8,200},{16,0},{24,216},{32,16},{40,232},{48,32},{56,248},{... | collective-permute-start | bytes 393224 | tf_op jit(solution)/shard_map/ppermute | solution.py:38
  (4 other events, 43.3 us)

commit v5 on v4

--- a/solution.py
+++ b/solution.py
@@ -50,9 +50,10 @@
     return lax.ppermute(value, "row", [(row_of(y, x, c), row_of(y, x, c + 1)) for y, x in CHIPS for c in range(NC)])
 
 
-def next_row(value, steps):
+def to_next_chip(value):
     count = NY * NX * NC
-    return lax.ppermute(value, "row", [(r, (r + steps) % count) for r in range(count)])
+    pairs = [(r, (r + 1) % count) for r in range(1, count, 2)] + [(r, (r - 1) % count) for r in range(0, count, 2)]
+    return lax.ppermute(value, "row", pairs)
 
 
 def live_taps(contig_lengths, first_row, rows):
@@ -240,14 +241,22 @@
 
 
 def other_kernel(ids, *refs):
-    other, (cross, acc, _, dg_ref, p_ref, tail_ref, head_ref, w, sems) = refs[0:4], refs[4:]
+    other, (cross, acc, _, dg_ref, p_ref, chip_ref, next_ref, w, sems) = refs[0:4], refs[4:]
     load_weight(ids, 1 - ids[2], other, w, sems, start)
     load_weight(ids, 1 - ids[2], other, w, sems, wait)
     p = (acc[...] + core_term(ids, 1 - ids[2], cross, w)).astype(BF)
     p_ref[...] = p
-    tail_ref[...] = p[128:256]
+    tail = p[128:256]
     top = p[0:128].astype(F32)
-    head_ref[...] = (dg_ref[0:128].astype(F32) * (top * jax.nn.sigmoid(top))).astype(BF)
+    head = (dg_ref[0:128].astype(F32) * (top * jax.nn.sigmoid(top))).astype(BF)
+
+    @pl.when(ids[2] == 0)
+    def _():
+        chip_ref[...], next_ref[...] = tail, head
+
+    @pl.when(ids[2] == 1)
+    def _():
+        chip_ref[...], next_ref[...] = head, tail
 
 
 def project_other(ids, other, cross, acc, w, d_gated):
@@ -317,20 +326,22 @@
 
 
 def edges_kernel(
-    p_ref, dg_ref, taps_ref, back_ref, ahead_ref, tail_ref, head_ref, gated_hi, dgate_ref, part_ref, dconv_ref,
+    p_ref, dg_ref, taps_ref, back_ref, ahead_ref, chip_ref, next_ref, gated_hi, dgate_ref, part_ref, dconv_ref,
     ids, w_ref, _, gated_ref, dproj_ref, far_ref, w, cross_ref, ext, even, odd, acc, sem,
 ):
     load = pltpu.make_async_copy(w_ref, w, sem)
     load.start()
     p, up = p_ref[LOW].astype(F32), dg_ref[LOW].astype(F32)
-    ext[LOW] = tail_ref[...].astype(F32)
+    from_chip, from_next = chip_ref[...].astype(F32), next_ref[...].astype(F32)
+    ext[LOW] = jnp.where(ids[2] == 0, from_next, from_chip)
     ext[HIGH] = p
     mix(ext, back_ref.at[LOW], taps_ref, even, odd, acc, False)
     gated_ref[LOW], d_gate, _ = gates(p, up, acc[...])
     gated_ref[HIGH] = gated_hi[...]
     dproj_ref[LOW] = (part_ref[...] + d_gate).astype(BF)
     ext[LOW] = dconv_ref[...]
-    ext[HIGH] = head_ref[...].astype(F32)
+    from_chip, from_next = chip_ref[...].astype(F32), next_ref[...].astype(F32)
+    ext[HIGH] = jnp.where(ids[2] == 0, from_chip, from_next)
     mix(ext, ahead_ref.at[HIGH], taps_ref, even, odd, acc, True)
     dproj_ref[HIGH] = (acc[...] + dgate_ref[...]).astype(BF)
     cross_ref[NZ] = dproj_ref[:, 0:256]
@@ -363,15 +374,15 @@
     )(*operands)
 
 
-def conv(ids, p, tail, head, d_gated, taps, back, ahead, w, cross):
+def conv(ids, p, for_chip, for_next, d_gated, taps, back, ahead, w, cross):
     half, whole = (128, 512), (256, 512)
-    tail, head = next_row(tail, 1), next_row(head, -1)
+    halos = to_other_core(for_chip), to_next_chip(for_next)
     inside = mix_call(
         inside_kernel, "inside", [(half, BF), (half, F32), (half, F32), (half, F32)], p, d_gated, taps, back, ahead
     )
     return mix_call(
         edges_kernel, "edges", [(whole, BF), (whole, BF), (whole, BF), (w.shape, BF), (cross.shape, BF)],
-        p, d_gated, taps, back, ahead, tail, head, *inside, ids, w, cross,
+        p, d_gated, taps, back, ahead, *halos, *inside, ids, w, cross,
         specs=[VMEM] * 11 + [SMEM, HBM, VMEM], scratch=[pltpu.SemaphoreType.DMA], aliases={13: 4},
     )
 
@@ -488,9 +499,9 @@
     p4 = around_z(after(p3, own), 1)
     other = [to_other_core(block) for block in after(own, back, ahead, taps, mine)]
     acc, weight, mine, cross = project_own(ids, [q3, p3, p4], own, mine, cross)
-    projected, tail, head, weight = project_other(ids, other, cross, acc, weight, d_gated)
+    projected, for_chip, for_next, weight = project_other(ids, other, cross, acc, weight, d_gated)
     gated, d_proj, far, weight, cross = conv(
-        ids, projected, tail, head, d_gated, taps, back, ahead, weight, cross
+        ids, projected, for_chip, for_next, d_gated, taps, back, ahead, weight, cross
     )
     d_tokens, grad = sum_up(ids, d_proj, far, weight, mine, cross)
     return gated, d_tokens, grad * (1.0 / math.sqrt(seq_total))

time: 108 us -> 107 us (level)
  starting transfers between devices: 44.4 us -> 42.4 us
    ppermute x2 -> x1, starting transfers between devices: 5.14 us -> 1.24 us  [to_next_chip(): return lax.ppermute(value, 'row', pairs)]
    ppermute x14, starting transfers between devices: 22.6 us -> 24.3 us  [around_z(): return lax.ppermute(value, ('row', 'col'), pairs)]
where the time goes in v5:
time: 107 us; the launch traced here: 106 us
  starting transfers between devices  42.4 us (40%)
  waiting for transfers between devices  32.8 us (31%)
  Pallas kernels  25.4 us (24%)
  other arithmetic  2.8 us (3%)
  local copies, waits for them, and re-layouts  2.08 us (2%)
    ppermute x14, starting transfers between devices, around_z(): return lax.ppermute(value, ('row', 'col'), pairs)  24.3 us
    pallas_call x2, Pallas kernels, mix_call(): pl.pallas_call(kernel, in_specs=specs or [VMEM] * len(operands), out_spec...  16.4 us
    ppermute x14, waiting for transfers between devices, around_z(): return lax.ppermute(value, ('row', 'col'), pairs)  15.4 us
    ppermute x6, waiting for transfers between devices, narrow(): return lax.ppermute(value, 'row', pairs)  10.5 us
    ppermute x6, starting transfers between devices, wide(): return lax.ppermute(value, 'row', pairs)  7.85 us
    ppermute x6, starting transfers between devices, narrow(): return lax.ppermute(value, 'row', pairs)  7.75 us
    ppermute x6, waiting for transfers between devices, wide(): return lax.ppermute(value, 'row', pairs)  6.89 us
  transfers between devices with their start and end apart: 33, of which 15 were waited for; matrix products, arithmetic and copies ran while one was open for 3% of the time, Pallas kernels for 14%

profile of v5, /device:TPU:96, one launch (start us, length us, event | category | flops | bytes accessed | tf_op | source)
XLA Modules:
  0.0 106.4 jit_solution(16617005540882419634)
XLA Ops:
  0.6 3.2 %collective-permute-start.7 = (bf16[256,512]{1,0:T(8,128)(2,1)}, bf16[256,512]{1,0:T(8,128)(2,1)S(1)}, u32[]{:S(2)}, u32[]{:S(2)}) collective-permute-start(bf16[256,512]{1,0:T(8,128)(2,1)} %refs_0_.3), channel_id=1, source_target_pairs={{0,1},{1,2},{2,3},{3,4},{4,5},{5,6},{6,7},{7,0},{8,15},{9,8},{10,9... | collective-permute-start | bytes 786440 | tf_op jit(solution)/shard_map/ppermute | solution.py:30
  3.8 2.8 %collective-permute-start = (bf16[128,512]{1,0:T(8,128)(2,1)}, bf16[128,512]{1,0:T(8,128)(2,1)S(1)}, u32[]{:S(2)}, u32[]{:S(2)}) collective-permute-start(bf16[128,512]{1,0:T(8,128)(2,1)} %refs_0_.2), channel_id=1, source_target_pairs={{0,48},{8,200},{16,0},{24,216},{32,16},{40,232},{48,32},{56,248},{... | collective-permute-start | bytes 393224 | tf_op jit(solution)/shard_map/ppermute | solution.py:38
  8.3 2.5 %collective-permute-done.refs_1_ = bf16[128,512]{1,0:T(8,128)(2,1)S(1)} collective-permute-done((bf16[128,512]{1,0:T(8,128)(2,1)}, bf16[128,512]{1,0:T(8,128)(2,1)S(1)}, u32[]{:S(2)}, u32[]{:S(2)}) %collective-permute-start) | collective-permute-done | bytes 131104 | tf_op jit(solution)/shard_map/ppermute | solution.py:38
  10.8 2.5 %collective-permute-done.1.refs_2_ = bf16[128,512]{1,0:T(8,128)(2,1)S(1)} collective-permute-done((bf16[128,512]{1,0:T(8,128)(2,1)}, bf16[128,512]{1,0:T(8,128)(2,1)S(1)}, u32[]{:S(2)}, u32[]{:S(2)}) %collective-permute-start.1) | collective-permute-done | bytes 131104 | tf_op jit(solution)/shard_map/ppermute | solution.py:38
  13.4 1.3 %collective-permute-done.2.refs_3_ = bf16[128,512]{1,0:T(8,128)(2,1)S(1)} collective-permute-done((bf16[128,512]{1,0:T(8,128)(2,1)}, bf16[128,512]{1,0:T(8,128)(2,1)S(1)}, u32[]{:S(2)}, u32[]{:S(2)}) %collective-permute-start.2) | collective-permute-done | bytes 131104 | tf_op jit(solution)/shard_map/ppermute | solution.py:38
  15.6 1.1 %collective-permute-start.9 = (bf16[256,512]{1,0:T(8,128)(2,1)S(1)}, bf16[256,512]{1,0:T(8,128)(2,1)S(1)}, u32[]{:S(2)}, u32[]{:S(2)}) collective-permute-start(bf16[256,512]{1,0:T(8,128)(2,1)S(1)} %collective-permute-done.7.refs_2_), channel_id=1, source_target_pairs={{0,1},{1,2},{2,3},{3,4},{4,5},{5,6},{6,7},{7,0},{8,15},{9,8},{10,9... | collective-permute-start | bytes 786440 | tf_op jit(solution)/shard_map/ppermute | solution.py:30
  16.7 3.0 %collective-permute-start.3 = (bf16[4,128,512]{2,1,0:T(8,128)(2,1)S(1)}, bf16[4,128,512]{2,1,0:T(8,128)(2,1)S(1)}, u32[]{:S(2)}, u32[]{:S(2)}) collective-permute-start(bf16[4,128,512]{2,1,0:T(8,128)(2,1)S(1)} %stack.21.refs_3_), channel_id=1, source_target_pairs={{0,192},{8,56},{16,208},{24,8},{32,224},{40,24},{48,240},{56,40},{... | collective-permute-start | bytes 1572872 | tf_op jit(solution)/shard_map/ppermute | solution.py:46
  24.1 2.7 %collective-permute-start.15 = (bf16[256,512]{1,0:T(8,128)(2,1)S(1)}, bf16[256,512]{1,0:T(8,128)(2,1)S(1)}, u32[]{:S(2)}, u32[]{:S(2)}) collective-permute-start(bf16[256,512]{1,0:T(8,128)(2,1)S(1)} %collective-permute-done.9.refs_4_), channel_id=1, source_target_pairs={{0,1},{1,2},{2,3},{3,4},{4,5},{5,6},{6,7},{7,0},{8,15},{9,8},{10,9... | collective-permute-start | bytes 786440 | tf_op jit(solution)/shard_map/ppermute | solution.py:30
  27.7 1.3 %collective-permute-done.8.refs_3_ = bf16[256,512]{1,0:T(8,128)(2,1)S(1)} collective-permute-done((bf16[256,512]{1,0:T(8,128)(2,1)S(1)}, bf16[256,512]{1,0:T(8,128)(2,1)S(1)}, u32[]{:S(2)}, u32[]{:S(2)}) %collective-permute-start.8) | collective-permute-done | bytes 262176 | tf_op jit(solution)/shard_map/ppermute | solution.py:30
  29.2 2.9 %collective-permute-done.3.refs_4_ = bf16[4,128,512]{2,1,0:T(8,128)(2,1)S(1)} collective-permute-done((bf16[4,128,512]{2,1,0:T(8,128)(2,1)S(1)}, bf16[4,128,512]{2,1,0:T(8,128)(2,1)S(1)}, u32[]{:S(2)}, u32[]{:S(2)}) %collective-permute-start.3) | collective-permute-done | bytes 524320 | tf_op jit(solution)/shard_map/ppermute | solution.py:46
  32.1 4.0 %collective-permute-done.5.refs_6_ = bf16[4,128,512]{2,1,0:T(8,128)(2,1)S(1)} collective-permute-done((bf16[4,128,512]{2,1,0:T(8,128)(2,1)S(1)}, bf16[4,128,512]{2,1,0:T(8,128)(2,1)S(1)}, u32[]{:S(2)}, u32[]{:S(2)}) %collective-permute-start.5) | collective-permute-done | bytes 524320 | tf_op jit(solution)/shard_map/ppermute | solution.py:46
  36.1 1.0 collective-permute-start.16
  39.4 3.0 %collective-permute-done.16.refs_2_ = bf16[256,512]{1,0:T(8,128)(2,1)S(1)} collective-permute-done((bf16[256,512]{1,0:T(8,128)(2,1)S(1)}, bf16[256,512]{1,0:T(8,128)(2,1)S(1)}, u32[]{:S(2)}, u32[]{:S(2)}) %collective-permute-start.16) | collective-permute-done | bytes 262176 | tf_op jit(solution)/shard_map/ppermute | solution.py:30
  42.4 1.6 %project_own.1 = (f32[256,512]{1,0:T(8,128)S(1)}, bf16[4,4,2,128,512]{4,3,2,1,0:T(8,128)(2,1)S(1)}, bf16[8,256,256]{2,1,0:T(8,128)(2,1)S(1)}, bf16[10,256,256]{2,1,0:T(8,128)(2,1)S(1)}) custom-call(s32[4]{0:T(128)S(1)} %pad_add_fusion.ids, bf16[256,512]{1,0:T(8,128)(2,1)S(1)} %collective-permute-done.14.refs_0_, ...), custom_call_target="tpu_custom_call", output_to_operand_aliasing={{2}: (8, {}), {3}: (9, {})} | custom-call | flops 4294967296 | bytes 4194304 | tf_op jit(solution)/shard_map/project_own/pallas_call | solution.py:225
  44.1 1.5 %project_other.1 = (bf16[256,512]{1,0:T(8,128)(2,1)S(1)}, bf16[128,512]{1,0:T(8,128)(2,1)S(1)}, bf16[128,512]{1,0:T(8,128)(2,1)S(1)}, bf16[4,4,2,128,512]{4,3,2,1,0:T(8,128)(2,1)S(1)}) custom-call(s32[4]{0:T(128)S(1)} %pad_add_fusion.ids, bf16[4,128,512]{2,1,0:T(8,128)(2,1)S(1)} %collective-permute-done.10.refs_0_, ...), custom_call_target="tpu_custom_call", output_to_operand_aliasing={{3}: (7, {})} | custom-call | flops 1073741824 | bytes 4194304 | tf_op jit(solution)/shard_map/project_other/pallas_call | solution.py:264
  45.8 1.2 %collective-permute-start.18 = (bf16[128,512]{1,0:T(8,128)(2,1)S(1)}, bf16[128,512]{1,0:T(8,128)(2,1)S(1)}, u32[]{:S(2)}, u32[]{:S(2)}) collective-permute-start(bf16[128,512]{1,0:T(8,128)(2,1)S(1)} %get-tuple-element.69), channel_id=1, source_target_pairs={{8,16},{24,32},{40,48},{56,64},{72,80},{88,96},{104,112},{120,128}... | collective-permute-start | bytes 393224 | tf_op jit(solution)/shard_map/ppermute | solution.py:56
  47.0 7.5 %inside.1 = (bf16[128,512]{1,0:T(8,128)(2,1)S(1)}, f32[128,512]{1,0:T(8,128)S(1)}, f32[128,512]{1,0:T(8,128)S(1)}, f32[128,512]{1,0:T(8,128)S(1)}) custom-call(bf16[256,512]{1,0:T(8,128)(2,1)S(1)} %get-tuple-element.67.p_ref, bf16[256,512]{1,0:T(8,128)(2,1)S(1)} %copy-done.1, bf16[8,16,16,512]{3,2,1,0:T(8,128)(2,1)S(1)} %broadcast_in_dim.46.taps_ref, ...), custom_call_target="tpu_custom_call" | custom-call | flops 4294967296 | bytes 4194304 | tf_op jit(solution)/shard_map/inside/pallas_call | solution.py:358
  54.5 8.9 %edges.1 = (bf16[256,512]{1,0:T(8,128)(2,1)}, bf16[256,512]{1,0:T(8,128)(2,1)S(1)}, bf16[256,512]{1,0:T(8,128)(2,1)S(1)}, bf16[4,4,2,128,512]{4,3,2,1,0:T(8,128)(2,1)S(1)}, bf16[10,256,256]{2,1,0:T(8,128)(2,1)S(1)}) custom-call(bf16[256,512]{1,0:T(8,128)(2,1)S(1)} %get-tuple-element.67.p_ref, ...), custom_call_target="tpu_custom_call", output_to_operand_aliasing={{4}: (13, {})} | custom-call | flops 4294967296 | bytes 4194304 | tf_op jit(solution)/shard_map/edges/pallas_call | solution.py:358
  63.6 3.8 %collective-permute-start.20 = (bf16[256,512]{1,0:T(8,128)(2,1)S(1)}, bf16[256,512]{1,0:T(8,128)(2,1)S(1)}, u32[]{:S(2)}, u32[]{:S(2)}) collective-permute-start(bf16[256,512]{1,0:T(8,128)(2,1)S(1)} %get-tuple-element.87), channel_id=1, source_target_pairs={{0,1},{1,2},{2,3},{3,4},{4,5},{5,6},{6,7},{7,0},{8,15},{9,8},{10,9... | collective-permute-start | bytes 786440 | tf_op jit(solution)/shard_map/ppermute | solution.py:30
  67.3 1.7 %near_terms.1 = (bf16[256,512]{1,0:T(8,128)(2,1)S(1)}, bf16[256,512]{1,0:T(8,128)(2,1)S(1)}, bf16[256,512]{1,0:T(8,128)(2,1)S(1)}, bf16[256,512]{1,0:T(8,128)(2,...) custom-call(s32[4]{0:T(128)S(1)} %pad_add_fusion.ids, ...), custom_call_target="tpu_custom_call" | custom-call | flops 939524096 | bytes 6291456 | tf_op jit(solution)/shard_map/near_terms/pallas_call | solution.py:400
  69.1 2.0 %weight_terms.1 = (bf16[4,128,512]{2,1,0:T(8,128)(2,1)S(1)}, bf16[4,128,512]{2,1,0:T(8,128)(2,1)S(1)}, bf16[4,128,512]{2,1,0:T(8,128)(2,1)S(1)}, bf16[4,128,512]{2,1,0:T(8,128)(2,1)S(1)}) custom-call(s32[4]{0:T(128)S(1)} %pad_add_fusion.ids, bf16[8,256,256]{2,1,0:T(8,128)(2,1)S(1)} %get-tuple-element.82.mine, ...), custom_call_target="tpu_custom_call" | custom-call | flops 1073741824 | bytes 5242880 | tf_op jit(solution)/shard_map/weight_terms/pallas_call | solution.py:447
  71.1 1.6 %collective-permute-done.20.b = bf16[256,512]{1,0:T(8,128)(2,1)S(1)} collective-permute-done((bf16[256,512]{1,0:T(8,128)(2,1)S(1)}, bf16[256,512]{1,0:T(8,128)(2,1)S(1)}, u32[]{:S(2)}, u32[]{:S(2)}) %collective-permute-start.20) | collective-permute-done | bytes 262176 | tf_op jit(solution)/shard_map/ppermute | solution.py:30
  72.8 3.8 %collective-permute-start.21 = (bf16[256,512]{1,0:T(8,128)(2,1)S(1)}, bf16[256,512]{1,0:T(8,128)(2,1)S(1)}, u32[]{:S(2)}, u32[]{:S(2)}) collective-permute-start(bf16[256,512]{1,0:T(8,128)(2,1)S(1)} %add.69), channel_id=1, source_target_pairs={{0,1},{1,2},{2,3},{3,4},{4,5},{5,6},{6,7},{7,0},{8,15},{9,8},{10,9... | collective-permute-start | bytes 786440 | tf_op jit(solution)/shard_map/ppermute | solution.py:30
  76.6 2.2 %collective-permute-start.28 = (bf16[4,128,512]{2,1,0:T(8,128)(2,1)S(1)}, bf16[4,128,512]{2,1,0:T(8,128)(2,1)S(1)}, u32[]{:S(2)}, u32[]{:S(2)}) collective-permute-start(bf16[4,128,512]{2,1,0:T(8,128)(2,1)S(1)} %get-tuple-element.93), channel_id=1, source_target_pairs={{0,128},{8,40},{16,144},{24,56},{32,160},{40,8},{48,176},{56,24},{... | collective-permute-start | bytes 1572872 | tf_op jit(solution)/shard_map/ppermute | solution.py:46
  78.8 1.1 %collective-permute-start.29 = (bf16[4,128,512]{2,1,0:T(8,128)(2,1)S(1)}, bf16[4,128,512]{2,1,0:T(8,128)(2,1)S(1)}, u32[]{:S(2)}, u32[]{:S(2)}) collective-permute-start(bf16[4,128,512]{2,1,0:T(8,128)(2,1)S(1)} %get-tuple-element.94), channel_id=1, source_target_pairs={{0,192},{8,56},{16,208},{24,8},{32,224},{40,24},{48,240},{56,40},{... | collective-permute-start | bytes 1572872 | tf_op jit(solution)/shard_map/ppermute | solution.py:46
  80.0 3.2 %collective-permute-done.21.b = bf16[256,512]{1,0:T(8,128)(2,1)S(1)} collective-permute-done((bf16[256,512]{1,0:T(8,128)(2,1)S(1)}, bf16[256,512]{1,0:T(8,128)(2,1)S(1)}, u32[]{:S(2)}, u32[]{:S(2)}) %collective-permute-start.21) | collective-permute-done | bytes 262176 | tf_op jit(solution)/shard_map/ppermute | solution.py:30
  83.2 3.8 %collective-permute-start.22 = (bf16[256,512]{1,0:T(8,128)(2,1)S(1)}, bf16[256,512]{1,0:T(8,128)(2,1)S(1)}, u32[]{:S(2)}, u32[]{:S(2)}) collective-permute-start(bf16[256,512]{1,0:T(8,128)(2,1)S(1)} %add.70), channel_id=1, source_target_pairs={{0,1},{1,2},{2,3},{3,4},{4,5},{5,6},{6,7},{7,0},{8,15},{9,8},{10,9... | collective-permute-start | bytes 786440 | tf_op jit(solution)/shard_map/ppermute | solution.py:30
  87.0 1.9 %collective-permute-done.25.b = bf16[256,512]{1,0:T(8,128)(2,1)S(1)} collective-permute-done((bf16[256,512]{1,0:T(8,128)(2,1)S(1)}, bf16[256,512]{1,0:T(8,128)(2,1)S(1)}, u32[]{:S(2)}, u32[]{:S(2)}) %collective-permute-start.25) | collective-permute-done | bytes 262176 | tf_op jit(solution)/shard_map/ppermute | solution.py:30
  89.1 3.9 %collective-permute-done.22.b = bf16[256,512]{1,0:T(8,128)(2,1)S(1)} collective-permute-done((bf16[256,512]{1,0:T(8,128)(2,1)S(1)}, bf16[256,512]{1,0:T(8,128)(2,1)S(1)}, u32[]{:S(2)}, u32[]{:S(2)}) %collective-permute-start.22) | collective-permute-done | bytes 262176 | tf_op jit(solution)/shard_map/ppermute | solution.py:30
  93.0 3.8 %collective-permute-start.23 = (bf16[256,512]{1,0:T(8,128)(2,1)S(1)}, bf16[256,512]{1,0:T(8,128)(2,1)S(1)}, u32[]{:S(2)}, u32[]{:S(2)}) collective-permute-start(bf16[256,512]{1,0:T(8,128)(2,1)S(1)} %add.71), channel_id=1, source_target_pairs={{0,1},{1,2},{2,3},{3,4},{4,5},{5,6},{6,7},{7,0},{8,15},{9,8},{10,9... | collective-permute-start | bytes 786440 | tf_op jit(solution)/shard_map/ppermute | solution.py:30
  97.3 3.1 %collective-permute-start.32 = (bf16[128,512]{1,0:T(8,128)(2,1)S(1)}, bf16[128,512]{1,0:T(8,128)(2,1)S(1)}, u32[]{:S(2)}, u32[]{:S(2)}) collective-permute-start(bf16[128,512]{1,0:T(8,128)(2,1)S(1)} %get-tuple-element.98), channel_id=1, source_target_pairs={{0,48},{8,200},{16,0},{24,216},{32,16},{40,232},{48,32},{56,248},{... | collective-permute-start | bytes 393224 | tf_op jit(solution)/shard_map/ppermute | solution.py:38
  101.5 3.2 %collective-permute-done.30 = bf16[128,512]{1,0:T(8,128)(2,1)S(1)} collective-permute-done((bf16[128,512]{1,0:T(8,128)(2,1)S(1)}, bf16[128,512]{1,0:T(8,128)(2,1)S(1)}, u32[]{:S(2)}, u32[]{:S(2)}) %collective-permute-start.30) | collective-permute-done | bytes 131104 | tf_op jit(solution)/shard_map/ppermute | solution.py:38
  (69 shorter events, 14.3 us)
Async XLA Ops:
  0.6 15.0 %collective-permute-start.7 = (bf16[256,512]{1,0:T(8,128)(2,1)}, bf16[256,512]{1,0:T(8,128)(2,1)S(1)}, u32[]{:S(2)}, u32[]{:S(2)}) collective-permute-start(bf16[256,512]{1,0:T(8,128)(2,1)} %refs_0_.3), channel_id=1, source_target_pairs={{0,1},{1,2},{2,3},{3,4},{4,5},{5,6},{6,7},{7,0},{8,15},{9,8},{10,9... | collective-permute-start | bytes 786440 | tf_op jit(solution)/shard_map/ppermute | solution.py:30
  3.8 7.0 %collective-permute-start = (bf16[128,512]{1,0:T(8,128)(2,1)}, bf16[128,512]{1,0:T(8,128)(2,1)S(1)}, u32[]{:S(2)}, u32[]{:S(2)}) collective-permute-start(bf16[128,512]{1,0:T(8,128)(2,1)} %refs_0_.2), channel_id=1, source_target_pairs={{0,48},{8,200},{16,0},{24,216},{32,16},{40,232},{48,32},{56,248},{... | collective-permute-start | bytes 393224 | tf_op jit(solution)/shard_map/ppermute | solution.py:38
  6.6 6.8 %collective-permute-start.1 = (bf16[128,512]{1,0:T(8,128)(2,1)}, bf16[128,512]{1,0:T(8,128)(2,1)S(1)}, u32[]{:S(2)}, u32[]{:S(2)}) collective-permute-start(bf16[128,512]{1,0:T(8,128)(2,1)} %refs_0_.2), channel_id=1, source_target_pairs={{0,32},{8,136},{16,48},{24,152},{32,0},{40,168},{48,16},{56,184},{... | collective-permute-start | bytes 393224 | tf_op jit(solution)/shard_map/ppermute | solution.py:38
  7.4 7.3 %collective-permute-start.2 = (bf16[128,512]{1,0:T(8,128)(2,1)}, bf16[128,512]{1,0:T(8,128)(2,1)S(1)}, u32[]{:S(2)}, u32[]{:S(2)}) collective-permute-start(bf16[128,512]{1,0:T(8,128)(2,1)} %refs_0_.2), channel_id=1, source_target_pairs={{0,16},{8,72},{16,32},{24,88},{32,48},{40,104},{48,0},{56,120},{64... | collective-permute-start | bytes 393224 | tf_op jit(solution)/shard_map/ppermute | solution.py:38
  8.3 13.1 %collective-permute-start.6 = (bf16[256,512]{1,0:T(8,128)(2,1)}, bf16[256,512]{1,0:T(8,128)(2,1)S(1)}, u32[]{:S(2)}, u32[]{:S(2)}) collective-permute-start(bf16[256,512]{1,0:T(8,128)(2,1)} %refs_0_.3), channel_id=1, source_target_pairs={{0,7},{1,0},{2,1},{3,2},{4,3},{5,4},{6,5},{7,6},{8,9},{9,10},{10,1... | collective-permute-start | bytes 786440 | tf_op jit(solution)/shard_map/ppermute | solution.py:30
  15.6 8.4 %collective-permute-start.9 = (bf16[256,512]{1,0:T(8,128)(2,1)S(1)}, bf16[256,512]{1,0:T(8,128)(2,1)S(1)}, u32[]{:S(2)}, u32[]{:S(2)}) collective-permute-start(bf16[256,512]{1,0:T(8,128)(2,1)S(1)} %collective-permute-done.7.refs_2_), channel_id=1, source_target_pairs={{0,1},{1,2},{2,3},{3,4},{4,5},{5,6},{6,7},{7,0},{8,15},{9,8},{10,9... | collective-permute-start | bytes 786440 | tf_op jit(solution)/shard_map/ppermute | solution.py:30
  16.7 15.3 %collective-permute-start.3 = (bf16[4,128,512]{2,1,0:T(8,128)(2,1)S(1)}, bf16[4,128,512]{2,1,0:T(8,128)(2,1)S(1)}, u32[]{:S(2)}, u32[]{:S(2)}) collective-permute-start(bf16[4,128,512]{2,1,0:T(8,128)(2,1)S(1)} %stack.21.refs_3_), channel_id=1, source_target_pairs={{0,192},{8,56},{16,208},{24,8},{32,224},{40,24},{48,240},{56,40},{... | collective-permute-start | bytes 1572872 | tf_op jit(solution)/shard_map/ppermute | solution.py:46
  19.8 12.3 %collective-permute-start.4 = (bf16[4,128,512]{2,1,0:T(8,128)(2,1)S(1)}, bf16[4,128,512]{2,1,0:T(8,128)(2,1)S(1)}, u32[]{:S(2)}, u32[]{:S(2)}) collective-permute-start(bf16[4,128,512]{2,1,0:T(8,128)(2,1)S(1)} %stack.21.refs_3_), channel_id=1, source_target_pairs={{0,128},{8,40},{16,144},{24,56},{32,160},{40,8},{48,176},{56,24},{... | collective-permute-start | bytes 1572872 | tf_op jit(solution)/shard_map/ppermute | solution.py:46
  20.4 15.7 %collective-permute-start.5 = (bf16[4,128,512]{2,1,0:T(8,128)(2,1)S(1)}, bf16[4,128,512]{2,1,0:T(8,128)(2,1)S(1)}, u32[]{:S(2)}, u32[]{:S(2)}) collective-permute-start(bf16[4,128,512]{2,1,0:T(8,128)(2,1)S(1)} %stack.21.refs_3_), channel_id=1, source_target_pairs={{0,64},{8,24},{16,80},{24,40},{32,96},{40,56},{48,112},{56,8},{64,... | collective-permute-start | bytes 1572872 | tf_op jit(solution)/shard_map/ppermute | solution.py:46
  21.4 7.7 %collective-permute-start.8 = (bf16[256,512]{1,0:T(8,128)(2,1)S(1)}, bf16[256,512]{1,0:T(8,128)(2,1)S(1)}, u32[]{:S(2)}, u32[]{:S(2)}) collective-permute-start(bf16[256,512]{1,0:T(8,128)(2,1)S(1)} %collective-permute-done.6.refs_1_), channel_id=1, source_target_pairs={{0,7},{1,0},{2,1},{3,2},{4,3},{5,4},{6,5},{7,6},{8,9},{9,10},{10,1... | collective-permute-start | bytes 786440 | tf_op jit(solution)/shard_map/ppermute | solution.py:30
  24.1 12.0 %collective-permute-start.15 = (bf16[256,512]{1,0:T(8,128)(2,1)S(1)}, bf16[256,512]{1,0:T(8,128)(2,1)S(1)}, u32[]{:S(2)}, u32[]{:S(2)}) collective-permute-start(bf16[256,512]{1,0:T(8,128)(2,1)S(1)} %collective-permute-done.9.refs_4_), channel_id=1, source_target_pairs={{0,1},{1,2},{2,3},{3,4},{4,5},{5,6},{6,7},{7,0},{8,15},{9,8},{10,9... | collective-permute-start | bytes 786440 | tf_op jit(solution)/shard_map/ppermute | solution.py:30
  29.0 10.1 %collective-permute-start.14 = (bf16[256,512]{1,0:T(8,128)(2,1)S(1)}, bf16[256,512]{1,0:T(8,128)(2,1)S(1)}, u32[]{:S(2)}, u32[]{:S(2)}) collective-permute-start(bf16[256,512]{1,0:T(8,128)(2,1)S(1)} %collective-permute-done.8.refs_3_), channel_id=1, source_target_pairs={{0,7},{1,0},{2,1},{3,2},{4,3},{5,4},{6,5},{7,6},{8,9},{9,10},{10,1... | collective-permute-start | bytes 786440 | tf_op jit(solution)/shard_map/ppermute | solution.py:30
  36.1 6.4 %collective-permute-start.16 = (bf16[256,512]{1,0:T(8,128)(2,1)S(1)}, bf16[256,512]{1,0:T(8,128)(2,1)S(1)}, u32[]{:S(2)}, u32[]{:S(2)}) collective-permute-start(bf16[256,512]{1,0:T(8,128)(2,1)S(1)} %collective-permute-done.15.refs_1_), channel_id=1, source_target_pairs={{0,1},{1,2},{2,3},{3,4},{4,5},{5,6},{6,7},{7,0},{8,15},{9,8},{10,9... | collective-permute-start | bytes 786440 | tf_op jit(solution)/shard_map/ppermute | solution.py:30
  38.3 5.8 %collective-permute-start.10 = (bf16[4,128,512]{2,1,0:T(8,128)(2,1)S(1)}, bf16[4,128,512]{2,1,0:T(8,128)(2,1)S(1)}, u32[]{:S(2)}, u32[]{:S(2)}) collective-permute-start(bf16[4,128,512]{2,1,0:T(8,128)(2,1)S(1)} %stack.21.refs_3_), channel_id=1, source_target_pairs={{0,8},{8,0},{16,24},{24,16},{32,40},{40,32},{48,56},{56,48},{64,72... | collective-permute-start | bytes 1572872 | tf_op jit(solution)/shard_map/ppermute | solution.py:50
  38.4 5.7 %collective-permute-start.11 = (bf16[4,128,512]{2,1,0:T(8,128)(2,1)S(1)}, bf16[4,128,512]{2,1,0:T(8,128)(2,1)S(1)}, u32[]{:S(2)}, u32[]{:S(2)}) collective-permute-start(bf16[4,128,512]{2,1,0:T(8,128)(2,1)S(1)} %collective-permute-done.3.refs_4_), channel_id=1, source_target_pairs={{0,8},{8,0},{16,24},{24,16},{32,40},{40,32},{48,56},{56,48},{64,72... | collective-permute-start | bytes 1572872 | tf_op jit(solution)/shard_map/ppermute | solution.py:50
  38.9 5.2 %collective-permute-start.12 = (bf16[4,128,512]{2,1,0:T(8,128)(2,1)S(1)}, bf16[4,128,512]{2,1,0:T(8,128)(2,1)S(1)}, u32[]{:S(2)}, u32[]{:S(2)}) collective-permute-start(bf16[4,128,512]{2,1,0:T(8,128)(2,1)S(1)} %collective-permute-done.4.refs_5_), channel_id=1, source_target_pairs={{0,8},{8,0},{16,24},{24,16},{32,40},{40,32},{48,56},{56,48},{64,72... | collective-permute-start | bytes 1572872 | tf_op jit(solution)/shard_map/ppermute | solution.py:50
  45.7 8.8 %collective-permute-start.17 = (bf16[128,512]{1,0:T(8,128)(2,1)S(1)}, bf16[128,512]{1,0:T(8,128)(2,1)S(1)}, u32[]{:S(2)}, u32[]{:S(2)}) collective-permute-start(bf16[128,512]{1,0:T(8,128)(2,1)S(1)} %get-tuple-element.68), channel_id=1, source_target_pairs={{0,8},{8,0},{16,24},{24,16},{32,40},{40,32},{48,56},{56,48},{64,72... | collective-permute-start | bytes 393224 | tf_op jit(solution)/shard_map/ppermute | solution.py:50
  45.8 8.7 %collective-permute-start.18 = (bf16[128,512]{1,0:T(8,128)(2,1)S(1)}, bf16[128,512]{1,0:T(8,128)(2,1)S(1)}, u32[]{:S(2)}, u32[]{:S(2)}) collective-permute-start(bf16[128,512]{1,0:T(8,128)(2,1)S(1)} %get-tuple-element.69), channel_id=1, source_target_pairs={{8,16},{24,32},{40,48},{56,64},{72,80},{88,96},{104,112},{120,128}... | collective-permute-start | bytes 393224 | tf_op jit(solution)/shard_map/ppermute | solution.py:56
  63.5 5.7 %collective-permute-start.19 = (bf16[10,256,256]{2,1,0:T(8,128)(2,1)S(1)}, bf16[10,256,256]{2,1,0:T(8,128)(2,1)S(1)}, u32[]{:S(2)}, u32[]{:S(2)}) collective-permute-start(bf16[10,256,256]{2,1,0:T(8,128)(2,1)S(1)} %get-tuple-element.83), channel_id=1, source_target_pairs={{0,8},{8,0},{16,24},{24,16},{32,40},{40,32},{48,56},{56,48},{64,72... | collective-permute-start | bytes 3932168 | tf_op jit(solution)/shard_map/ppermute | solution.py:50
  63.6 9.2 %collective-permute-start.20 = (bf16[256,512]{1,0:T(8,128)(2,1)S(1)}, bf16[256,512]{1,0:T(8,128)(2,1)S(1)}, u32[]{:S(2)}, u32[]{:S(2)}) collective-permute-start(bf16[256,512]{1,0:T(8,128)(2,1)S(1)} %get-tuple-element.87), channel_id=1, source_target_pairs={{0,1},{1,2},{2,3},{3,4},{4,5},{5,6},{6,7},{7,0},{8,15},{9,8},{10,9... | collective-permute-start | bytes 786440 | tf_op jit(solution)/shard_map/ppermute | solution.py:30
  69.0 10.8 %collective-permute-start.24 = (bf16[256,512]{1,0:T(8,128)(2,1)S(1)}, bf16[256,512]{1,0:T(8,128)(2,1)S(1)}, u32[]{:S(2)}, u32[]{:S(2)}) collective-permute-start(bf16[256,512]{1,0:T(8,128)(2,1)S(1)} %get-tuple-element.90), channel_id=1, source_target_pairs={{0,7},{1,0},{2,1},{3,2},{4,3},{5,4},{6,5},{7,6},{8,9},{9,10},{10,1... | collective-permute-start | bytes 786440 | tf_op jit(solution)/shard_map/ppermute | solution.py:30
  72.8 10.3 %collective-permute-start.21 = (bf16[256,512]{1,0:T(8,128)(2,1)S(1)}, bf16[256,512]{1,0:T(8,128)(2,1)S(1)}, u32[]{:S(2)}, u32[]{:S(2)}) collective-permute-start(bf16[256,512]{1,0:T(8,128)(2,1)S(1)} %add.69), channel_id=1, source_target_pairs={{0,1},{1,2},{2,3},{3,4},{4,5},{5,6},{6,7},{7,0},{8,15},{9,8},{10,9... | collective-permute-start | bytes 786440 | tf_op jit(solution)/shard_map/ppermute | solution.py:30
  76.6 20.2 %collective-permute-start.27 = (bf16[4,128,512]{2,1,0:T(8,128)(2,1)S(1)}, bf16[4,128,512]{2,1,0:T(8,128)(2,1)S(1)}, u32[]{:S(2)}, u32[]{:S(2)}) collective-permute-start(bf16[4,128,512]{2,1,0:T(8,128)(2,1)S(1)} %get-tuple-element.92), channel_id=1, source_target_pairs={{0,64},{8,24},{16,80},{24,40},{32,96},{40,56},{48,112},{56,8},{64,... | collective-permute-start | bytes 1572872 | tf_op jit(solution)/shard_map/ppermute | solution.py:46
  76.6 20.2 %collective-permute-start.28 = (bf16[4,128,512]{2,1,0:T(8,128)(2,1)S(1)}, bf16[4,128,512]{2,1,0:T(8,128)(2,1)S(1)}, u32[]{:S(2)}, u32[]{:S(2)}) collective-permute-start(bf16[4,128,512]{2,1,0:T(8,128)(2,1)S(1)} %get-tuple-element.93), channel_id=1, source_target_pairs={{0,128},{8,40},{16,144},{24,56},{32,160},{40,8},{48,176},{56,24},{... | collective-permute-start | bytes 1572872 | tf_op jit(solution)/shard_map/ppermute | solution.py:46
  78.8 18.0 %collective-permute-start.29 = (bf16[4,128,512]{2,1,0:T(8,128)(2,1)S(1)}, bf16[4,128,512]{2,1,0:T(8,128)(2,1)S(1)}, u32[]{:S(2)}, u32[]{:S(2)}) collective-permute-start(bf16[4,128,512]{2,1,0:T(8,128)(2,1)S(1)} %get-tuple-element.94), channel_id=1, source_target_pairs={{0,192},{8,56},{16,208},{24,8},{32,224},{40,24},{48,240},{56,40},{... | collective-permute-start | bytes 1572872 | tf_op jit(solution)/shard_map/ppermute | solution.py:46
  79.9 9.0 %collective-permute-start.25 = (bf16[256,512]{1,0:T(8,128)(2,1)S(1)}, bf16[256,512]{1,0:T(8,128)(2,1)S(1)}, u32[]{:S(2)}, u32[]{:S(2)}) collective-permute-start(bf16[256,512]{1,0:T(8,128)(2,1)S(1)} %add.72), channel_id=1, source_target_pairs={{0,7},{1,0},{2,1},{3,2},{4,3},{5,4},{6,5},{7,6},{8,9},{9,10},{10,1... | collective-permute-start | bytes 786440 | tf_op jit(solution)/shard_map/ppermute | solution.py:30
  83.2 9.7 %collective-permute-start.22 = (bf16[256,512]{1,0:T(8,128)(2,1)S(1)}, bf16[256,512]{1,0:T(8,128)(2,1)S(1)}, u32[]{:S(2)}, u32[]{:S(2)}) collective-permute-start(bf16[256,512]{1,0:T(8,128)(2,1)S(1)} %add.70), channel_id=1, source_target_pairs={{0,1},{1,2},{2,3},{3,4},{4,5},{5,6},{6,7},{7,0},{8,15},{9,8},{10,9... | collective-permute-start | bytes 786440 | tf_op jit(solution)/shard_map/ppermute | solution.py:30
  89.0 11.4 %collective-permute-start.26 = (bf16[256,512]{1,0:T(8,128)(2,1)S(1)}, bf16[256,512]{1,0:T(8,128)(2,1)S(1)}, u32[]{:S(2)}, u32[]{:S(2)}) collective-permute-start(bf16[256,512]{1,0:T(8,128)(2,1)S(1)} %add.73), channel_id=1, source_target_pairs={{0,7},{1,0},{2,1},{3,2},{4,3},{5,4},{6,5},{7,6},{8,9},{9,10},{10,1... | collective-permute-start | bytes 786440 | tf_op jit(solution)/shard_map/ppermute | solution.py:30
  93.0 7.7 %collective-permute-start.23 = (bf16[256,512]{1,0:T(8,128)(2,1)S(1)}, bf16[256,512]{1,0:T(8,128)(2,1)S(1)}, u32[]{:S(2)}, u32[]{:S(2)}) collective-permute-start(bf16[256,512]{1,0:T(8,128)(2,1)S(1)} %add.71), channel_id=1, source_target_pairs={{0,1},{1,2},{2,3},{3,4},{4,5},{5,6},{6,7},{7,0},{8,15},{9,8},{10,9... | collective-permute-start | bytes 786440 | tf_op jit(solution)/shard_map/ppermute | solution.py:30
  97.1 7.7 %collective-permute-start.30 = (bf16[128,512]{1,0:T(8,128)(2,1)S(1)}, bf16[128,512]{1,0:T(8,128)(2,1)S(1)}, u32[]{:S(2)}, u32[]{:S(2)}) collective-permute-start(bf16[128,512]{1,0:T(8,128)(2,1)S(1)} %get-tuple-element.96), channel_id=1, source_target_pairs={{0,16},{8,72},{16,32},{24,88},{32,48},{40,104},{48,0},{56,120},{64... | collective-permute-start | bytes 393224 | tf_op jit(solution)/shard_map/ppermute | solution.py:38
  97.2 7.6 %collective-permute-start.31 = (bf16[128,512]{1,0:T(8,128)(2,1)S(1)}, bf16[128,512]{1,0:T(8,128)(2,1)S(1)}, u32[]{:S(2)}, u32[]{:S(2)}) collective-permute-start(bf16[128,512]{1,0:T(8,128)(2,1)S(1)} %get-tuple-element.97), channel_id=1, source_target_pairs={{0,32},{8,136},{16,48},{24,152},{32,0},{40,168},{48,16},{56,184},{... | collective-permute-start | bytes 393224 | tf_op jit(solution)/shard_map/ppermute | solution.py:38
  97.3 8.4 %collective-permute-start.32 = (bf16[128,512]{1,0:T(8,128)(2,1)S(1)}, bf16[128,512]{1,0:T(8,128)(2,1)S(1)}, u32[]{:S(2)}, u32[]{:S(2)}) collective-permute-start(bf16[128,512]{1,0:T(8,128)(2,1)S(1)} %get-tuple-element.98), channel_id=1, source_target_pairs={{0,48},{8,200},{16,0},{24,216},{32,16},{40,232},{48,32},{56,248},{... | collective-permute-start | bytes 393224 | tf_op jit(solution)/shard_map/ppermute | solution.py:38
  (4 other events, 44.1 us)

commit v6 on v5

--- a/solution.py
+++ b/solution.py
@@ -387,23 +387,20 @@
     )
 
 
-NEAR = (3, 5, 2, 6, 1, 7, 0)
-
-
-def near_kernel(ids, d_ref, w, *outs):
+def near_kernel(order, ids, d_ref, w, *outs):
     d = d_ref[...]
-    for steps, out in zip(NEAR, outs):
+    for steps, out in zip(order, outs):
         out[...] = back_term(d, weight_rows(ids, steps, w)[...].reshape(512, 512))
 
 
-def near_terms(ids, d_proj, weight):
-    return pl.pallas_call(
-        near_kernel,
+def near_terms(ids, d_proj, weight, order, flops):
+    return pl.pallas_call(
+        functools.partial(near_kernel, order),
         in_specs=[SMEM, VMEM, VMEM],
-        out_specs=[VMEM] * 7,
-        out_shape=[jax.ShapeDtypeStruct((256, 512), BF)] * 7,
+        out_specs=[VMEM] * len(order),
+        out_shape=[jax.ShapeDtypeStruct((256, 512), BF)] * len(order),
         compiler_params=pltpu.CompilerParams(vmem_limit_bytes=4 << 20),
-        cost_estimate=pl.CostEstimate(flops=2 * 256 * 512 * 512 * 7, bytes_accessed=6 << 20, transcendentals=0),
+        cost_estimate=pl.CostEstimate(flops=flops, bytes_accessed=len(order) << 20, transcendentals=0),
         name="near_terms",
     )(ids, d_proj, weight)
 
@@ -459,10 +456,11 @@
 def sum_up(ids, d_proj, far, weight, mine, cross):
     p = around_z(far, 1)
     theirs = to_other_core(cross)
-    p3, q3, p2, q2, p1, q1, own = near_terms(ids, d_proj, weight)
+    p3, q3 = near_terms(ids, d_proj, weight, (3, 5), 1 << 28)
     q = around_z(q3, -1)
-    g = weight_terms(ids, mine, after(theirs, own), d_proj)
-    p = around_z(add(after(p3, g[0]), p), 1)
+    g = weight_terms(ids, mine, after(theirs, q3), d_proj)
+    p2, q2, p1, q1, own = near_terms(ids, after(d_proj, g[0]), weight, (2, 6, 1, 7, 0), 1 << 33)
+    p = around_z(add(after(p3, own), p), 1)
     s = [g[0]] + [wide(g[k], k) for k in (1, 2, 3)]
     q = around_z(add(q2, q), -1)
     p = around_z(add(p2, p), 1)

time: 107 us -> 106 us (level)
    pallas_call x1 -> x2, Pallas kernels: 1.7 us -> 2.46 us  [near_terms(): pl.pallas_call(functools.partial(near_kernel, order), in_specs=[SMEM, VME...]
  transfers between devices with their start and end apart: 33 -> 33, of which waited for: 15 -> 15; matrix products, arithmetic and copies ran while one was open for 3% -> 3% of each run, Pallas kernels for 14% -> 15%
where the time goes in v6:
time: 106 us
  starting transfers between devices  42.4 us (40%)
  waiting for transfers between devices  31.8 us (30%)
  Pallas kernels  26.2 us (25%)
  other arithmetic  2.8 us (3%)
  local copies, waits for them, and re-layouts  2.08 us (2%)
    ppermute x14, starting transfers between devices, around_z(): return lax.ppermute(value, ('row', 'col'), pairs)  24.3 us
    pallas_call x2, Pallas kernels, mix_call(): pl.pallas_call(kernel, in_specs=specs or [VMEM] * len(operands), out_spec...  16.4 us
    ppermute x14, waiting for transfers between devices, around_z(): return lax.ppermute(value, ('row', 'col'), pairs)  14.4 us
    ppermute x6, waiting for transfers between devices, narrow(): return lax.ppermute(value, 'row', pairs)  10.5 us
    ppermute x6, starting transfers between devices, wide(): return lax.ppermute(value, 'row', pairs)  7.85 us
    ppermute x6, starting transfers between devices, narrow(): return lax.ppermute(value, 'row', pairs)  7.75 us
    ppermute x6, waiting for transfers between devices, wide(): return lax.ppermute(value, 'row', pairs)  6.89 us
    pallas_call x2, Pallas kernels, near_terms(): pl.pallas_call(functools.partial(near_kernel, order), in_specs=[SMEM, VME...  2.46 us
  transfers between devices with their start and end apart: 33, of which 15 were waited for; matrix products, arithmetic and copies ran while one was open for 3% of the time, Pallas kernels for 15%

profile of v6, /device:TPU:96, one launch (start us, length us, event | category | flops | bytes accessed | tf_op | source)
XLA Modules:
  0.0 106.1 jit_solution(14385993734689669902)
XLA Ops:
  0.6 3.2 %collective-permute-start.7 = (bf16[256,512]{1,0:T(8,128)(2,1)}, bf16[256,512]{1,0:T(8,128)(2,1)S(1)}, u32[]{:S(2)}, u32[]{:S(2)}) collective-permute-start(bf16[256,512]{1,0:T(8,128)(2,1)} %refs_0_.3), channel_id=1, source_target_pairs={{0,1},{1,2},{2,3},{3,4},{4,5},{5,6},{6,7},{7,0},{8,15},{9,8},{10,9... | collective-permute-start | bytes 786440 | tf_op jit(solution)/shard_map/ppermute | solution.py:30
  3.8 2.8 %collective-permute-start = (bf16[128,512]{1,0:T(8,128)(2,1)}, bf16[128,512]{1,0:T(8,128)(2,1)S(1)}, u32[]{:S(2)}, u32[]{:S(2)}) collective-permute-start(bf16[128,512]{1,0:T(8,128)(2,1)} %refs_0_.2), channel_id=1, source_target_pairs={{0,48},{8,200},{16,0},{24,216},{32,16},{40,232},{48,32},{56,248},{... | collective-permute-start | bytes 393224 | tf_op jit(solution)/shard_map/ppermute | solution.py:38
  8.3 2.5 %collective-permute-done.refs_1_ = bf16[128,512]{1,0:T(8,128)(2,1)S(1)} collective-permute-done((bf16[128,512]{1,0:T(8,128)(2,1)}, bf16[128,512]{1,0:T(8,128)(2,1)S(1)}, u32[]{:S(2)}, u32[]{:S(2)}) %collective-permute-start) | collective-permute-done | bytes 131104 | tf_op jit(solution)/shard_map/ppermute | solution.py:38
  10.8 2.5 %collective-permute-done.1.refs_2_ = bf16[128,512]{1,0:T(8,128)(2,1)S(1)} collective-permute-done((bf16[128,512]{1,0:T(8,128)(2,1)}, bf16[128,512]{1,0:T(8,128)(2,1)S(1)}, u32[]{:S(2)}, u32[]{:S(2)}) %collective-permute-start.1) | collective-permute-done | bytes 131104 | tf_op jit(solution)/shard_map/ppermute | solution.py:38
  13.4 1.3 %collective-permute-done.2.refs_3_ = bf16[128,512]{1,0:T(8,128)(2,1)S(1)} collective-permute-done((bf16[128,512]{1,0:T(8,128)(2,1)}, bf16[128,512]{1,0:T(8,128)(2,1)S(1)}, u32[]{:S(2)}, u32[]{:S(2)}) %collective-permute-start.2) | collective-permute-done | bytes 131104 | tf_op jit(solution)/shard_map/ppermute | solution.py:38
  15.6 1.1 %collective-permute-start.9 = (bf16[256,512]{1,0:T(8,128)(2,1)S(1)}, bf16[256,512]{1,0:T(8,128)(2,1)S(1)}, u32[]{:S(2)}, u32[]{:S(2)}) collective-permute-start(bf16[256,512]{1,0:T(8,128)(2,1)S(1)} %collective-permute-done.7.refs_2_), channel_id=1, source_target_pairs={{0,1},{1,2},{2,3},{3,4},{4,5},{5,6},{6,7},{7,0},{8,15},{9,8},{10,9... | collective-permute-start | bytes 786440 | tf_op jit(solution)/shard_map/ppermute | solution.py:30
  16.7 3.0 %collective-permute-start.3 = (bf16[4,128,512]{2,1,0:T(8,128)(2,1)S(1)}, bf16[4,128,512]{2,1,0:T(8,128)(2,1)S(1)}, u32[]{:S(2)}, u32[]{:S(2)}) collective-permute-start(bf16[4,128,512]{2,1,0:T(8,128)(2,1)S(1)} %stack.21.refs_3_), channel_id=1, source_target_pairs={{0,192},{8,56},{16,208},{24,8},{32,224},{40,24},{48,240},{56,40},{... | collective-permute-start | bytes 1572872 | tf_op jit(solution)/shard_map/ppermute | solution.py:46
  24.1 2.7 %collective-permute-start.15 = (bf16[256,512]{1,0:T(8,128)(2,1)S(1)}, bf16[256,512]{1,0:T(8,128)(2,1)S(1)}, u32[]{:S(2)}, u32[]{:S(2)}) collective-permute-start(bf16[256,512]{1,0:T(8,128)(2,1)S(1)} %collective-permute-done.9.refs_4_), channel_id=1, source_target_pairs={{0,1},{1,2},{2,3},{3,4},{4,5},{5,6},{6,7},{7,0},{8,15},{9,8},{10,9... | collective-permute-start | bytes 786440 | tf_op jit(solution)/shard_map/ppermute | solution.py:30
  27.7 1.3 %collective-permute-done.8.refs_3_ = bf16[256,512]{1,0:T(8,128)(2,1)S(1)} collective-permute-done((bf16[256,512]{1,0:T(8,128)(2,1)S(1)}, bf16[256,512]{1,0:T(8,128)(2,1)S(1)}, u32[]{:S(2)}, u32[]{:S(2)}) %collective-permute-start.8) | collective-permute-done | bytes 262176 | tf_op jit(solution)/shard_map/ppermute | solution.py:30
  29.2 2.9 %collective-permute-done.3.refs_4_ = bf16[4,128,512]{2,1,0:T(8,128)(2,1)S(1)} collective-permute-done((bf16[4,128,512]{2,1,0:T(8,128)(2,1)S(1)}, bf16[4,128,512]{2,1,0:T(8,128)(2,1)S(1)}, u32[]{:S(2)}, u32[]{:S(2)}) %collective-permute-start.3) | collective-permute-done | bytes 524320 | tf_op jit(solution)/shard_map/ppermute | solution.py:46
  32.1 4.0 %collective-permute-done.5.refs_6_ = bf16[4,128,512]{2,1,0:T(8,128)(2,1)S(1)} collective-permute-done((bf16[4,128,512]{2,1,0:T(8,128)(2,1)S(1)}, bf16[4,128,512]{2,1,0:T(8,128)(2,1)S(1)}, u32[]{:S(2)}, u32[]{:S(2)}) %collective-permute-start.5) | collective-permute-done | bytes 524320 | tf_op jit(solution)/shard_map/ppermute | solution.py:46
  39.4 3.0 %collective-permute-done.16.refs_2_ = bf16[256,512]{1,0:T(8,128)(2,1)S(1)} collective-permute-done((bf16[256,512]{1,0:T(8,128)(2,1)S(1)}, bf16[256,512]{1,0:T(8,128)(2,1)S(1)}, u32[]{:S(2)}, u32[]{:S(2)}) %collective-permute-start.16) | collective-permute-done | bytes 262176 | tf_op jit(solution)/shard_map/ppermute | solution.py:30
  42.4 1.6 %project_own.1 = (f32[256,512]{1,0:T(8,128)S(1)}, bf16[4,4,2,128,512]{4,3,2,1,0:T(8,128)(2,1)S(1)}, bf16[8,256,256]{2,1,0:T(8,128)(2,1)S(1)}, bf16[10,256,256]{2,1,0:T(8,128)(2,1)S(1)}) custom-call(s32[4]{0:T(128)S(1)} %pad_add_fusion.ids, bf16[256,512]{1,0:T(8,128)(2,1)S(1)} %collective-permute-done.14.refs_0_, ...), custom_call_target="tpu_custom_call", output_to_operand_aliasing={{2}: (8, {}), {3}: (9, {})} | custom-call | flops 4294967296 | bytes 4194304 | tf_op jit(solution)/shard_map/project_own/pallas_call | solution.py:225
  44.1 1.5 %project_other.1 = (bf16[256,512]{1,0:T(8,128)(2,1)S(1)}, bf16[128,512]{1,0:T(8,128)(2,1)S(1)}, bf16[128,512]{1,0:T(8,128)(2,1)S(1)}, bf16[4,4,2,128,512]{4,3,2,1,0:T(8,128)(2,1)S(1)}) custom-call(s32[4]{0:T(128)S(1)} %pad_add_fusion.ids, bf16[4,128,512]{2,1,0:T(8,128)(2,1)S(1)} %collective-permute-done.10.refs_0_, ...), custom_call_target="tpu_custom_call", output_to_operand_aliasing={{3}: (7, {})} | custom-call | flops 1073741824 | bytes 4194304 | tf_op jit(solution)/shard_map/project_other/pallas_call | solution.py:264
  45.8 1.2 %collective-permute-start.18 = (bf16[128,512]{1,0:T(8,128)(2,1)S(1)}, bf16[128,512]{1,0:T(8,128)(2,1)S(1)}, u32[]{:S(2)}, u32[]{:S(2)}) collective-permute-start(bf16[128,512]{1,0:T(8,128)(2,1)S(1)} %get-tuple-element.70), channel_id=1, source_target_pairs={{8,16},{24,32},{40,48},{56,64},{72,80},{88,96},{104,112},{120,128}... | collective-permute-start | bytes 393224 | tf_op jit(solution)/shard_map/ppermute | solution.py:56
  47.0 7.5 %inside.1 = (bf16[128,512]{1,0:T(8,128)(2,1)S(1)}, f32[128,512]{1,0:T(8,128)S(1)}, f32[128,512]{1,0:T(8,128)S(1)}, f32[128,512]{1,0:T(8,128)S(1)}) custom-call(bf16[256,512]{1,0:T(8,128)(2,1)S(1)} %get-tuple-element.68.p_ref, bf16[256,512]{1,0:T(8,128)(2,1)S(1)} %copy-done.1, bf16[8,16,16,512]{3,2,1,0:T(8,128)(2,1)S(1)} %broadcast_in_dim.46.taps_ref, ...), custom_call_target="tpu_custom_call" | custom-call | flops 4294967296 | bytes 4194304 | tf_op jit(solution)/shard_map/inside/pallas_call | solution.py:358
  54.5 8.9 %edges.1 = (bf16[256,512]{1,0:T(8,128)(2,1)}, bf16[256,512]{1,0:T(8,128)(2,1)S(1)}, bf16[256,512]{1,0:T(8,128)(2,1)S(1)}, bf16[4,4,2,128,512]{4,3,2,1,0:T(8,128)(2,1)S(1)}, bf16[10,256,256]{2,1,0:T(8,128)(2,1)S(1)}) custom-call(bf16[256,512]{1,0:T(8,128)(2,1)S(1)} %get-tuple-element.68.p_ref, ...), custom_call_target="tpu_custom_call", output_to_operand_aliasing={{4}: (13, {})} | custom-call | flops 4294967296 | bytes 4194304 | tf_op jit(solution)/shard_map/edges/pallas_call | solution.py:358
  63.6 1.0 near_terms.2
  65.1 3.3 %collective-permute-start.20 = (bf16[256,512]{1,0:T(8,128)(2,1)S(1)}, bf16[256,512]{1,0:T(8,128)(2,1)S(1)}, u32[]{:S(2)}, u32[]{:S(2)}) collective-permute-start(bf16[256,512]{1,0:T(8,128)(2,1)S(1)} %get-tuple-element.90), channel_id=1, source_target_pairs={{0,1},{1,2},{2,3},{3,4},{4,5},{5,6},{6,7},{7,0},{8,15},{9,8},{10,9... | collective-permute-start | bytes 786440 | tf_op jit(solution)/shard_map/ppermute | solution.py:30
  68.5 2.0 %weight_terms.1 = (bf16[4,128,512]{2,1,0:T(8,128)(2,1)S(1)}, bf16[4,128,512]{2,1,0:T(8,128)(2,1)S(1)}, bf16[4,128,512]{2,1,0:T(8,128)(2,1)S(1)}, bf16[4,128,512]{2,1,0:T(8,128)(2,1)S(1)}) custom-call(s32[4]{0:T(128)S(1)} %pad_add_fusion.ids, bf16[8,256,256]{2,1,0:T(8,128)(2,1)S(1)} %get-tuple-element.78.mine, ...), custom_call_target="tpu_custom_call" | custom-call | flops 1073741824 | bytes 5242880 | tf_op jit(solution)/shard_map/weight_terms/pallas_call | solution.py:444
  70.4 1.4 %near_terms.3 = (bf16[256,512]{1,0:T(8,128)(2,1)S(1)}, bf16[256,512]{1,0:T(8,128)(2,1)S(1)}, bf16[256,512]{1,0:T(8,128)(2,1)S(1)}, bf16[256,512]{1,0:T(8,128)(2,1)S(1)}, bf16[256,512]{1,0:T(8,128)(2,1)S(1)}) custom-call(s32[4]{0:T(128)S(1)} %pad_add_fusion.ids, bf16[256,512]{1,0:T(8,128)(2,1)S(1)} %get-tuple-element.84.d_ref.d_mine, ...), custom_call_target="tpu_custom_call" | custom-call | flops 8589934592 | bytes 5242880 | tf_op jit(solution)/shard_map/near_terms/pallas_call | solution.py:397
  71.9 2.7 %collective-permute-done.20.b = bf16[256,512]{1,0:T(8,128)(2,1)S(1)} collective-permute-done((bf16[256,512]{1,0:T(8,128)(2,1)S(1)}, bf16[256,512]{1,0:T(8,128)(2,1)S(1)}, u32[]{:S(2)}, u32[]{:S(2)}) %collective-permute-start.20) | collective-permute-done | bytes 262176 | tf_op jit(solution)/shard_map/ppermute | solution.py:30
  74.7 3.8 %collective-permute-start.21 = (bf16[256,512]{1,0:T(8,128)(2,1)S(1)}, bf16[256,512]{1,0:T(8,128)(2,1)S(1)}, u32[]{:S(2)}, u32[]{:S(2)}) collective-permute-start(bf16[256,512]{1,0:T(8,128)(2,1)S(1)} %add.69), channel_id=1, source_target_pairs={{0,1},{1,2},{2,3},{3,4},{4,5},{5,6},{6,7},{7,0},{8,15},{9,8},{10,9... | collective-permute-start | bytes 786440 | tf_op jit(solution)/shard_map/ppermute | solution.py:30
  78.5 2.2 %collective-permute-start.28 = (bf16[4,128,512]{2,1,0:T(8,128)(2,1)S(1)}, bf16[4,128,512]{2,1,0:T(8,128)(2,1)S(1)}, u32[]{:S(2)}, u32[]{:S(2)}) collective-permute-start(bf16[4,128,512]{2,1,0:T(8,128)(2,1)S(1)} %get-tuple-element.95), channel_id=1, source_target_pairs={{0,128},{8,40},{16,144},{24,56},{32,160},{40,8},{48,176},{56,24},{... | collective-permute-start | bytes 1572872 | tf_op jit(solution)/shard_map/ppermute | solution.py:46
  80.6 1.1 %collective-permute-start.29 = (bf16[4,128,512]{2,1,0:T(8,128)(2,1)S(1)}, bf16[4,128,512]{2,1,0:T(8,128)(2,1)S(1)}, u32[]{:S(2)}, u32[]{:S(2)}) collective-permute-start(bf16[4,128,512]{2,1,0:T(8,128)(2,1)S(1)} %get-tuple-element.96), channel_id=1, source_target_pairs={{0,192},{8,56},{16,208},{24,8},{32,224},{40,24},{48,240},{56,40},{... | collective-permute-start | bytes 1572872 | tf_op jit(solution)/shard_map/ppermute | solution.py:46
  81.9 1.4 %collective-permute-done.21.b = bf16[256,512]{1,0:T(8,128)(2,1)S(1)} collective-permute-done((bf16[256,512]{1,0:T(8,128)(2,1)S(1)}, bf16[256,512]{1,0:T(8,128)(2,1)S(1)}, u32[]{:S(2)}, u32[]{:S(2)}) %collective-permute-start.21) | collective-permute-done | bytes 262176 | tf_op jit(solution)/shard_map/ppermute | solution.py:30
  83.3 3.8 %collective-permute-start.22 = (bf16[256,512]{1,0:T(8,128)(2,1)S(1)}, bf16[256,512]{1,0:T(8,128)(2,1)S(1)}, u32[]{:S(2)}, u32[]{:S(2)}) collective-permute-start(bf16[256,512]{1,0:T(8,128)(2,1)S(1)} %add.70), channel_id=1, source_target_pairs={{0,1},{1,2},{2,3},{3,4},{4,5},{5,6},{6,7},{7,0},{8,15},{9,8},{10,9... | collective-permute-start | bytes 786440 | tf_op jit(solution)/shard_map/ppermute | solution.py:30
  87.1 4.4 %collective-permute-done.25.b = bf16[256,512]{1,0:T(8,128)(2,1)S(1)} collective-permute-done((bf16[256,512]{1,0:T(8,128)(2,1)S(1)}, bf16[256,512]{1,0:T(8,128)(2,1)S(1)}, u32[]{:S(2)}, u32[]{:S(2)}) %collective-permute-start.25) | collective-permute-done | bytes 262176 | tf_op jit(solution)/shard_map/ppermute | solution.py:30
  91.6 1.0 collective-permute-done.22.b
  92.8 3.8 %collective-permute-start.23 = (bf16[256,512]{1,0:T(8,128)(2,1)S(1)}, bf16[256,512]{1,0:T(8,128)(2,1)S(1)}, u32[]{:S(2)}, u32[]{:S(2)}) collective-permute-start(bf16[256,512]{1,0:T(8,128)(2,1)S(1)} %add.71), channel_id=1, source_target_pairs={{0,1},{1,2},{2,3},{3,4},{4,5},{5,6},{6,7},{7,0},{8,15},{9,8},{10,9... | collective-permute-start | bytes 786440 | tf_op jit(solution)/shard_map/ppermute | solution.py:30
  97.4 2.7 %collective-permute-start.32 = (bf16[128,512]{1,0:T(8,128)(2,1)S(1)}, bf16[128,512]{1,0:T(8,128)(2,1)S(1)}, u32[]{:S(2)}, u32[]{:S(2)}) collective-permute-start(bf16[128,512]{1,0:T(8,128)(2,1)S(1)} %get-tuple-element.100), channel_id=1, source_target_pairs={{0,48},{8,200},{16,0},{24,216},{32,16},{40,232},{48,32},{56,248},{... | collective-permute-start | bytes 393224 | tf_op jit(solution)/shard_map/ppermute | solution.py:38
  101.3 3.2 %collective-permute-done.30 = bf16[128,512]{1,0:T(8,128)(2,1)S(1)} collective-permute-done((bf16[128,512]{1,0:T(8,128)(2,1)S(1)}, bf16[128,512]{1,0:T(8,128)(2,1)S(1)}, u32[]{:S(2)}, u32[]{:S(2)}) %collective-permute-start.30) | collective-permute-done | bytes 131104 | tf_op jit(solution)/shard_map/ppermute | solution.py:38
  (70 shorter events, 16.2 us)
Async XLA Ops:
  0.6 15.0 %collective-permute-start.7 = (bf16[256,512]{1,0:T(8,128)(2,1)}, bf16[256,512]{1,0:T(8,128)(2,1)S(1)}, u32[]{:S(2)}, u32[]{:S(2)}) collective-permute-start(bf16[256,512]{1,0:T(8,128)(2,1)} %refs_0_.3), channel_id=1, source_target_pairs={{0,1},{1,2},{2,3},{3,4},{4,5},{5,6},{6,7},{7,0},{8,15},{9,8},{10,9... | collective-permute-start | bytes 786440 | tf_op jit(solution)/shard_map/ppermute | solution.py:30
  3.8 7.0 %collective-permute-start = (bf16[128,512]{1,0:T(8,128)(2,1)}, bf16[128,512]{1,0:T(8,128)(2,1)S(1)}, u32[]{:S(2)}, u32[]{:S(2)}) collective-permute-start(bf16[128,512]{1,0:T(8,128)(2,1)} %refs_0_.2), channel_id=1, source_target_pairs={{0,48},{8,200},{16,0},{24,216},{32,16},{40,232},{48,32},{56,248},{... | collective-permute-start | bytes 393224 | tf_op jit(solution)/shard_map/ppermute | solution.py:38
  6.6 6.8 %collective-permute-start.1 = (bf16[128,512]{1,0:T(8,128)(2,1)}, bf16[128,512]{1,0:T(8,128)(2,1)S(1)}, u32[]{:S(2)}, u32[]{:S(2)}) collective-permute-start(bf16[128,512]{1,0:T(8,128)(2,1)} %refs_0_.2), channel_id=1, source_target_pairs={{0,32},{8,136},{16,48},{24,152},{32,0},{40,168},{48,16},{56,184},{... | collective-permute-start | bytes 393224 | tf_op jit(solution)/shard_map/ppermute | solution.py:38
  7.4 7.3 %collective-permute-start.2 = (bf16[128,512]{1,0:T(8,128)(2,1)}, bf16[128,512]{1,0:T(8,128)(2,1)S(1)}, u32[]{:S(2)}, u32[]{:S(2)}) collective-permute-start(bf16[128,512]{1,0:T(8,128)(2,1)} %refs_0_.2), channel_id=1, source_target_pairs={{0,16},{8,72},{16,32},{24,88},{32,48},{40,104},{48,0},{56,120},{64... | collective-permute-start | bytes 393224 | tf_op jit(solution)/shard_map/ppermute | solution.py:38
  8.3 13.1 %collective-permute-start.6 = (bf16[256,512]{1,0:T(8,128)(2,1)}, bf16[256,512]{1,0:T(8,128)(2,1)S(1)}, u32[]{:S(2)}, u32[]{:S(2)}) collective-permute-start(bf16[256,512]{1,0:T(8,128)(2,1)} %refs_0_.3), channel_id=1, source_target_pairs={{0,7},{1,0},{2,1},{3,2},{4,3},{5,4},{6,5},{7,6},{8,9},{9,10},{10,1... | collective-permute-start | bytes 786440 | tf_op jit(solution)/shard_map/ppermute | solution.py:30
  15.6 8.4 %collective-permute-start.9 = (bf16[256,512]{1,0:T(8,128)(2,1)S(1)}, bf16[256,512]{1,0:T(8,128)(2,1)S(1)}, u32[]{:S(2)}, u32[]{:S(2)}) collective-permute-start(bf16[256,512]{1,0:T(8,128)(2,1)S(1)} %collective-permute-done.7.refs_2_), channel_id=1, source_target_pairs={{0,1},{1,2},{2,3},{3,4},{4,5},{5,6},{6,7},{7,0},{8,15},{9,8},{10,9... | collective-permute-start | bytes 786440 | tf_op jit(solution)/shard_map/ppermute | solution.py:30
  16.7 15.3 %collective-permute-start.3 = (bf16[4,128,512]{2,1,0:T(8,128)(2,1)S(1)}, bf16[4,128,512]{2,1,0:T(8,128)(2,1)S(1)}, u32[]{:S(2)}, u32[]{:S(2)}) collective-permute-start(bf16[4,128,512]{2,1,0:T(8,128)(2,1)S(1)} %stack.21.refs_3_), channel_id=1, source_target_pairs={{0,192},{8,56},{16,208},{24,8},{32,224},{40,24},{48,240},{56,40},{... | collective-permute-start | bytes 1572872 | tf_op jit(solution)/shard_map/ppermute | solution.py:46
  19.8 12.3 %collective-permute-start.4 = (bf16[4,128,512]{2,1,0:T(8,128)(2,1)S(1)}, bf16[4,128,512]{2,1,0:T(8,128)(2,1)S(1)}, u32[]{:S(2)}, u32[]{:S(2)}) collective-permute-start(bf16[4,128,512]{2,1,0:T(8,128)(2,1)S(1)} %stack.21.refs_3_), channel_id=1, source_target_pairs={{0,128},{8,40},{16,144},{24,56},{32,160},{40,8},{48,176},{56,24},{... | collective-permute-start | bytes 1572872 | tf_op jit(solution)/shard_map/ppermute | solution.py:46
  20.4 15.7 %collective-permute-start.5 = (bf16[4,128,512]{2,1,0:T(8,128)(2,1)S(1)}, bf16[4,128,512]{2,1,0:T(8,128)(2,1)S(1)}, u32[]{:S(2)}, u32[]{:S(2)}) collective-permute-start(bf16[4,128,512]{2,1,0:T(8,128)(2,1)S(1)} %stack.21.refs_3_), channel_id=1, source_target_pairs={{0,64},{8,24},{16,80},{24,40},{32,96},{40,56},{48,112},{56,8},{64,... | collective-permute-start | bytes 1572872 | tf_op jit(solution)/shard_map/ppermute | solution.py:46
  21.4 7.7 %collective-permute-start.8 = (bf16[256,512]{1,0:T(8,128)(2,1)S(1)}, bf16[256,512]{1,0:T(8,128)(2,1)S(1)}, u32[]{:S(2)}, u32[]{:S(2)}) collective-permute-start(bf16[256,512]{1,0:T(8,128)(2,1)S(1)} %collective-permute-done.6.refs_1_), channel_id=1, source_target_pairs={{0,7},{1,0},{2,1},{3,2},{4,3},{5,4},{6,5},{7,6},{8,9},{9,10},{10,1... | collective-permute-start | bytes 786440 | tf_op jit(solution)/shard_map/ppermute | solution.py:30
  24.1 12.0 %collective-permute-start.15 = (bf16[256,512]{1,0:T(8,128)(2,1)S(1)}, bf16[256,512]{1,0:T(8,128)(2,1)S(1)}, u32[]{:S(2)}, u32[]{:S(2)}) collective-permute-start(bf16[256,512]{1,0:T(8,128)(2,1)S(1)} %collective-permute-done.9.refs_4_), channel_id=1, source_target_pairs={{0,1},{1,2},{2,3},{3,4},{4,5},{5,6},{6,7},{7,0},{8,15},{9,8},{10,9... | collective-permute-start | bytes 786440 | tf_op jit(solution)/shard_map/ppermute | solution.py:30
  29.0 10.1 %collective-permute-start.14 = (bf16[256,512]{1,0:T(8,128)(2,1)S(1)}, bf16[256,512]{1,0:T(8,128)(2,1)S(1)}, u32[]{:S(2)}, u32[]{:S(2)}) collective-permute-start(bf16[256,512]{1,0:T(8,128)(2,1)S(1)} %collective-permute-done.8.refs_3_), channel_id=1, source_target_pairs={{0,7},{1,0},{2,1},{3,2},{4,3},{5,4},{6,5},{7,6},{8,9},{9,10},{10,1... | collective-permute-start | bytes 786440 | tf_op jit(solution)/shard_map/ppermute | solution.py:30
  36.1 6.4 %collective-permute-start.16 = (bf16[256,512]{1,0:T(8,128)(2,1)S(1)}, bf16[256,512]{1,0:T(8,128)(2,1)S(1)}, u32[]{:S(2)}, u32[]{:S(2)}) collective-permute-start(bf16[256,512]{1,0:T(8,128)(2,1)S(1)} %collective-permute-done.15.refs_1_), channel_id=1, source_target_pairs={{0,1},{1,2},{2,3},{3,4},{4,5},{5,6},{6,7},{7,0},{8,15},{9,8},{10,9... | collective-permute-start | bytes 786440 | tf_op jit(solution)/shard_map/ppermute | solution.py:30
  38.3 5.8 %collective-permute-start.10 = (bf16[4,128,512]{2,1,0:T(8,128)(2,1)S(1)}, bf16[4,128,512]{2,1,0:T(8,128)(2,1)S(1)}, u32[]{:S(2)}, u32[]{:S(2)}) collective-permute-start(bf16[4,128,512]{2,1,0:T(8,128)(2,1)S(1)} %stack.21.refs_3_), channel_id=1, source_target_pairs={{0,8},{8,0},{16,24},{24,16},{32,40},{40,32},{48,56},{56,48},{64,72... | collective-permute-start | bytes 1572872 | tf_op jit(solution)/shard_map/ppermute | solution.py:50
  38.4 5.7 %collective-permute-start.11 = (bf16[4,128,512]{2,1,0:T(8,128)(2,1)S(1)}, bf16[4,128,512]{2,1,0:T(8,128)(2,1)S(1)}, u32[]{:S(2)}, u32[]{:S(2)}) collective-permute-start(bf16[4,128,512]{2,1,0:T(8,128)(2,1)S(1)} %collective-permute-done.3.refs_4_), channel_id=1, source_target_pairs={{0,8},{8,0},{16,24},{24,16},{32,40},{40,32},{48,56},{56,48},{64,72... | collective-permute-start | bytes 1572872 | tf_op jit(solution)/shard_map/ppermute | solution.py:50
  38.9 5.2 %collective-permute-start.12 = (bf16[4,128,512]{2,1,0:T(8,128)(2,1)S(1)}, bf16[4,128,512]{2,1,0:T(8,128)(2,1)S(1)}, u32[]{:S(2)}, u32[]{:S(2)}) collective-permute-start(bf16[4,128,512]{2,1,0:T(8,128)(2,1)S(1)} %collective-permute-done.4.refs_5_), channel_id=1, source_target_pairs={{0,8},{8,0},{16,24},{24,16},{32,40},{40,32},{48,56},{56,48},{64,72... | collective-permute-start | bytes 1572872 | tf_op jit(solution)/shard_map/ppermute | solution.py:50
  39.1 5.0 %collective-permute-start.13 = (bf16[4,128,512]{2,1,0:T(8,128)(2,1)S(1)}, bf16[4,128,512]{2,1,0:T(8,128)(2,1)S(1)}, u32[]{:S(2)}, u32[]{:S(2)}) collective-permute-start(bf16[4,128,512]{2,1,0:T(8,128)(2,1)S(1)} %collective-permute-done.5.refs_6_), channel_id=1, source_target_pairs={{0,8},{8,0},{16,24},{24,16},{32,40},{40,32},{48,56},{56,48},{64,72... | collective-permute-start | bytes 1572872 | tf_op jit(solution)/shard_map/ppermute | solution.py:50
  45.7 8.8 %collective-permute-start.17 = (bf16[128,512]{1,0:T(8,128)(2,1)S(1)}, bf16[128,512]{1,0:T(8,128)(2,1)S(1)}, u32[]{:S(2)}, u32[]{:S(2)}) collective-permute-start(bf16[128,512]{1,0:T(8,128)(2,1)S(1)} %get-tuple-element.69), channel_id=1, source_target_pairs={{0,8},{8,0},{16,24},{24,16},{32,40},{40,32},{48,56},{56,48},{64,72... | collective-permute-start | bytes 393224 | tf_op jit(solution)/shard_map/ppermute | solution.py:50
  45.8 8.7 %collective-permute-start.18 = (bf16[128,512]{1,0:T(8,128)(2,1)S(1)}, bf16[128,512]{1,0:T(8,128)(2,1)S(1)}, u32[]{:S(2)}, u32[]{:S(2)}) collective-permute-start(bf16[128,512]{1,0:T(8,128)(2,1)S(1)} %get-tuple-element.70), channel_id=1, source_target_pairs={{8,16},{24,32},{40,48},{56,64},{72,80},{88,96},{104,112},{120,128}... | collective-permute-start | bytes 393224 | tf_op jit(solution)/shard_map/ppermute | solution.py:56
  64.6 17.1 %collective-permute-start.24 = (bf16[256,512]{1,0:T(8,128)(2,1)S(1)}, bf16[256,512]{1,0:T(8,128)(2,1)S(1)}, u32[]{:S(2)}, u32[]{:S(2)}) collective-permute-start(bf16[256,512]{1,0:T(8,128)(2,1)S(1)} %get-tuple-element.81), channel_id=1, source_target_pairs={{0,7},{1,0},{2,1},{3,2},{4,3},{5,4},{6,5},{7,6},{8,9},{9,10},{10,1... | collective-permute-start | bytes 786440 | tf_op jit(solution)/shard_map/ppermute | solution.py:30
  65.1 9.5 %collective-permute-start.20 = (bf16[256,512]{1,0:T(8,128)(2,1)S(1)}, bf16[256,512]{1,0:T(8,128)(2,1)S(1)}, u32[]{:S(2)}, u32[]{:S(2)}) collective-permute-start(bf16[256,512]{1,0:T(8,128)(2,1)S(1)} %get-tuple-element.90), channel_id=1, source_target_pairs={{0,1},{1,2},{2,3},{3,4},{4,5},{5,6},{6,7},{7,0},{8,15},{9,8},{10,9... | collective-permute-start | bytes 786440 | tf_op jit(solution)/shard_map/ppermute | solution.py:30
  74.7 8.6 %collective-permute-start.21 = (bf16[256,512]{1,0:T(8,128)(2,1)S(1)}, bf16[256,512]{1,0:T(8,128)(2,1)S(1)}, u32[]{:S(2)}, u32[]{:S(2)}) collective-permute-start(bf16[256,512]{1,0:T(8,128)(2,1)S(1)} %add.69), channel_id=1, source_target_pairs={{0,1},{1,2},{2,3},{3,4},{4,5},{5,6},{6,7},{7,0},{8,15},{9,8},{10,9... | collective-permute-start | bytes 786440 | tf_op jit(solution)/shard_map/ppermute | solution.py:30
  78.5 18.1 %collective-permute-start.27 = (bf16[4,128,512]{2,1,0:T(8,128)(2,1)S(1)}, bf16[4,128,512]{2,1,0:T(8,128)(2,1)S(1)}, u32[]{:S(2)}, u32[]{:S(2)}) collective-permute-start(bf16[4,128,512]{2,1,0:T(8,128)(2,1)S(1)} %get-tuple-element.94), channel_id=1, source_target_pairs={{0,64},{8,24},{16,80},{24,40},{32,96},{40,56},{48,112},{56,8},{64,... | collective-permute-start | bytes 1572872 | tf_op jit(solution)/shard_map/ppermute | solution.py:46
  78.5 18.1 %collective-permute-start.28 = (bf16[4,128,512]{2,1,0:T(8,128)(2,1)S(1)}, bf16[4,128,512]{2,1,0:T(8,128)(2,1)S(1)}, u32[]{:S(2)}, u32[]{:S(2)}) collective-permute-start(bf16[4,128,512]{2,1,0:T(8,128)(2,1)S(1)} %get-tuple-element.95), channel_id=1, source_target_pairs={{0,128},{8,40},{16,144},{24,56},{32,160},{40,8},{48,176},{56,24},{... | collective-permute-start | bytes 1572872 | tf_op jit(solution)/shard_map/ppermute | solution.py:46
  80.6 15.9 %collective-permute-start.29 = (bf16[4,128,512]{2,1,0:T(8,128)(2,1)S(1)}, bf16[4,128,512]{2,1,0:T(8,128)(2,1)S(1)}, u32[]{:S(2)}, u32[]{:S(2)}) collective-permute-start(bf16[4,128,512]{2,1,0:T(8,128)(2,1)S(1)} %get-tuple-element.96), channel_id=1, source_target_pairs={{0,192},{8,56},{16,208},{24,8},{32,224},{40,24},{48,240},{56,40},{... | collective-permute-start | bytes 1572872 | tf_op jit(solution)/shard_map/ppermute | solution.py:46
  81.8 9.7 %collective-permute-start.25 = (bf16[256,512]{1,0:T(8,128)(2,1)S(1)}, bf16[256,512]{1,0:T(8,128)(2,1)S(1)}, u32[]{:S(2)}, u32[]{:S(2)}) collective-permute-start(bf16[256,512]{1,0:T(8,128)(2,1)S(1)} %add.72), channel_id=1, source_target_pairs={{0,7},{1,0},{2,1},{3,2},{4,3},{5,4},{6,5},{7,6},{8,9},{9,10},{10,1... | collective-permute-start | bytes 786440 | tf_op jit(solution)/shard_map/ppermute | solution.py:30
  83.3 9.4 %collective-permute-start.22 = (bf16[256,512]{1,0:T(8,128)(2,1)S(1)}, bf16[256,512]{1,0:T(8,128)(2,1)S(1)}, u32[]{:S(2)}, u32[]{:S(2)}) collective-permute-start(bf16[256,512]{1,0:T(8,128)(2,1)S(1)} %add.70), channel_id=1, source_target_pairs={{0,1},{1,2},{2,3},{3,4},{4,5},{5,6},{6,7},{7,0},{8,15},{9,8},{10,9... | collective-permute-start | bytes 786440 | tf_op jit(solution)/shard_map/ppermute | solution.py:30
  91.6 8.9 %collective-permute-start.26 = (bf16[256,512]{1,0:T(8,128)(2,1)S(1)}, bf16[256,512]{1,0:T(8,128)(2,1)S(1)}, u32[]{:S(2)}, u32[]{:S(2)}) collective-permute-start(bf16[256,512]{1,0:T(8,128)(2,1)S(1)} %add.73), channel_id=1, source_target_pairs={{0,7},{1,0},{2,1},{3,2},{4,3},{5,4},{6,5},{7,6},{8,9},{9,10},{10,1... | collective-permute-start | bytes 786440 | tf_op jit(solution)/shard_map/ppermute | solution.py:30
  92.8 7.7 %collective-permute-start.23 = (bf16[256,512]{1,0:T(8,128)(2,1)S(1)}, bf16[256,512]{1,0:T(8,128)(2,1)S(1)}, u32[]{:S(2)}, u32[]{:S(2)}) collective-permute-start(bf16[256,512]{1,0:T(8,128)(2,1)S(1)} %add.71), channel_id=1, source_target_pairs={{0,1},{1,2},{2,3},{3,4},{4,5},{5,6},{6,7},{7,0},{8,15},{9,8},{10,9... | collective-permute-start | bytes 786440 | tf_op jit(solution)/shard_map/ppermute | solution.py:30
  96.8 7.7 %collective-permute-start.30 = (bf16[128,512]{1,0:T(8,128)(2,1)S(1)}, bf16[128,512]{1,0:T(8,128)(2,1)S(1)}, u32[]{:S(2)}, u32[]{:S(2)}) collective-permute-start(bf16[128,512]{1,0:T(8,128)(2,1)S(1)} %get-tuple-element.98), channel_id=1, source_target_pairs={{0,16},{8,72},{16,32},{24,88},{32,48},{40,104},{48,0},{56,120},{64... | collective-permute-start | bytes 393224 | tf_op jit(solution)/shard_map/ppermute | solution.py:38
  96.9 7.6 %collective-permute-start.31 = (bf16[128,512]{1,0:T(8,128)(2,1)S(1)}, bf16[128,512]{1,0:T(8,128)(2,1)S(1)}, u32[]{:S(2)}, u32[]{:S(2)}) collective-permute-start(bf16[128,512]{1,0:T(8,128)(2,1)S(1)} %get-tuple-element.99), channel_id=1, source_target_pairs={{0,32},{8,136},{16,48},{24,152},{32,0},{40,168},{48,16},{56,184},{... | collective-permute-start | bytes 393224 | tf_op jit(solution)/shard_map/ppermute | solution.py:38
  97.4 8.0 %collective-permute-start.32 = (bf16[128,512]{1,0:T(8,128)(2,1)S(1)}, bf16[128,512]{1,0:T(8,128)(2,1)S(1)}, u32[]{:S(2)}, u32[]{:S(2)}) collective-permute-start(bf16[128,512]{1,0:T(8,128)(2,1)S(1)} %get-tuple-element.100), channel_id=1, source_target_pairs={{0,48},{8,200},{16,0},{24,216},{32,16},{40,232},{48,32},{56,248},{... | collective-permute-start | bytes 393224 | tf_op jit(solution)/shard_map/ppermute | solution.py:38
  (4 other events, 44.1 us)
